TPU v7x, 32 devices: a whole 2x2x4 slice. The times are simulated.
32 devices in a mesh: replica: 2 (over x), fsdp: 16 (over z, y, core).
Axes of the slice: x: 2, y: 2, z: 4, core: 2. Of those that a mesh axis runs over, the one named last changes fastest.
Arguments:
- activations: bfloat16 [8192, 4096], P(('replica', 'fsdp')), may hold values from -6 to 6
- inner_weight: bfloat16 [2, 4096, 512], P('replica', 'fsdp'), may hold values from -0.09375 to 0.09375
- local_params: float32 [2, 2, 2, 4096, 512], P('replica', None, None, 'fsdp'), may hold values from -6 to 6
- base_params: float32 [2, 2, 4096, 512], P(None, None, 'fsdp'), may hold values from -6 to 6
- momentum: float32 [2, 2, 4096, 512], P(None, None, 'fsdp'), may hold values from -3 to 3
- inner_steps: int32 [2], P('replica'), may hold values from 16 to 72, as said below
Outputs:
- keys: bfloat16 [8192, 512], P(('replica', 'fsdp'))
- new_base: float32 [2, 2, 4096, 512], P(None, None, 'fsdp')
- new_momentum: float32 [2, 2, 4096, 512], P(None, None, 'fsdp')
Inputs may be any that keep to these rules, and one draw needn't show every extreme that they name: `inner_steps`: some replica has done exactly 72 steps.
All inputs are finite; a program needn't handle non-finite values.
Results may differ from a plain program's by a relative error of at most 0.007.
Values may be sent and summed in bfloat16 or wider, within the bound.
No kernel may reach another device: no remote copies, remote signals or barrier semaphores. Data moves between devices by JAX's collectives and lax.ppermute only.
A program may use at most 64 MiB of HBM per device.

v0:
```python
import jax
import jax.numpy as jnp
from jax import lax
from jax.sharding import PartitionSpec as P


def nesterov(average, momentum, base_params):
    new_momentum = 0.9 * momentum + average
    new_base = base_params - 0.7 * (average + 0.9 * new_momentum)
    return (new_base, new_momentum)


def body(activations, inner_weight, local_params, base_params, momentum, inner_steps):
    counts = lax.all_gather(inner_steps, "replica", axis=0, tiled=True)
    total = jnp.sum(counts.astype(jnp.float32))
    own = inner_steps[0].astype(jnp.float32)
    difference = (base_params - local_params[0]).astype(jnp.bfloat16)
    weighted = own * difference.astype(jnp.float32)
    average = lax.psum(weighted, "replica") / total
    new_base, new_momentum = nesterov(average, momentum, base_params)
    folded = jnp.dot(
        activations,
        lax.all_gather(inner_weight[0], "fsdp", axis=0, tiled=True),
        preferred_element_type=jnp.float32,
    )
    keys = folded.astype(jnp.bfloat16)
    return (keys, new_base, new_momentum)


def solution(mesh):
    return jax.shard_map(
        body,
        mesh=mesh,
        in_specs=(
            P(("replica", "fsdp"), None),
            P("replica", "fsdp", None),
            P("replica", None, None, "fsdp", None),
            P(None, None, "fsdp", None),
            P(None, None, "fsdp", None),
            P("replica"),
        ),
        out_specs=(
            P(("replica", "fsdp"), None),
            P(None, None, "fsdp", None),
            P(None, None, "fsdp", None),
        ),
        check_vma=False,
    )
```

profile of v0, /device:TPU:0, one launch (start us, length us, event | category | flops | bytes accessed | tf_op | source)
XLA Modules:
  0.0 96.7 jit_solution(7231155000233127482)
XLA Ops:
  8.0 0.0 copy-start
  8.0 0.0 all-reduce.3.cloned.1.call-start
  8.8 4.0 %convert_multiply_fusion = f32[2,2,256,512]{3,2,1,0:T(8,128)} fusion(f32[2,2,256,512]{3,2,1,0:T(8,128)} %param.9, f32[1,2,2,256,512]{4,3,2,1,0:T(8,128)} %param.8, f32[]{:T(128)} %bitcast.1), kind=kLoop, calls=%fused_computation.6 | loop fusion | flops 2097152 | bytes 6291460 | tf_op jit(solution)/shard_map/mul | solution.py:18
  12.9 0.0 copy-start.1
  12.9 0.0 all-reduce.3.cloned.1.call-update
  12.9 0.0 all-gather.3.cloned.1.call-start
  13.0 0.5 all-gather.3.cloned.1.call-update
  13.5 0.0 copy-done.1
  13.5 0.6 dynamic-slice
  14.1 0.8 dynamic-update-slice
  14.9 5.2 %all-reduce = s32[2]{0:T(128)S(1)} all-reduce(s32[2]{0:T(128)S(1)} %dynamic-update-slice), channel_id=1, replica_groups=mesh['replica'=2,'fsdp'=16] {'replica'}, use_global_device_ids=true, to_apply=%add | all-reduce | flops 2 | bytes 16
  20.1 0.6 convert_reduce_fusion
  20.7 58.1 %all-reduce.3.cloned.1.call-done = f32[2,2,256,512]{3,2,1,0:T(8,128)} async-done(((f32[2,2,256,512]{3,2,1,0:T(8,128)}), f32[2,2,256,512]{3,2,1,0:T(8,128)}) %all-reduce.3.cloned.1.call-update) | async-done | bytes 2097168 | tf_op jit(solution)/shard_map/psum | solution.py:19
  78.8 6.4 %multiply_subtract_fusion = (f32[2,2,256,512]{3,2,1,0:T(8,128)}, f32[2,2,256,512]{3,2,1,0:T(8,128)}) fusion(f32[2,2,256,512]{3,2,1,0:T(8,128)} %param.9, f32[2,2,256,512]{3,2,1,0:T(8,128)} %all-reduce.3.cloned.1.call-done, f32[]{:T(128)} %convert_reduce_fusion, f32[2,2,256,512]{3,2,1,0:T(8,128)} %param.10), kind=kLoop, calls=%fused_computation.4 | loop fusion | flops 3670016 | bytes 10485764 | tf_op jit(solution)/shard_map/sub | solution.py:9
  85.2 0.0 all-gather.3.cloned.1.call-done
  85.2 0.0 copy-done
  85.2 4.1 %fusion.3 = bf16[256,512]{1,0:T(8,128)(2,1)} fusion(bf16[256,4096]{1,0:T(8,128)(2,1)S(1)} %copy-done, bf16[1,4096,512]{2,1,0:T(8,128)(2,1)} %all-gather.3.cloned.1.call-done), kind=kOutput, calls=%fused_computation.7 | convolution fusion | flops 1073872896 | bytes 6553600 | tf_op jit(solution)/shard_map/dot_general | solution.py:21
  (1 shorter events, 0.0 us)
Async XLA Ops:
  8.0 77.2 %copy-start = (bf16[256,4096]{1,0:T(8,128)(2,1)S(1)}, bf16[256,4096]{1,0:T(8,128)(2,1)}, u32[]{:S(2)}) copy-start(bf16[256,4096]{1,0:T(8,128)(2,1)} %param.6) | copy-start | bytes 6291460
  8.0 70.8 %all-reduce.3.cloned.1.call-start = ((), (), s32[]{:S(2)}) async-start(), calls=%async_computation | async-start | bytes 4194304 | tf_op jit(solution)/shard_map/psum | solution.py:19
  12.9 0.7 copy-start.1
  12.9 72.2 %all-gather.3.cloned.1.call-start = ((), (), s32[]{:S(2)}) async-start(), calls=%async_computation.1 | async-start | bytes 4456448 | tf_op jit(solution)/shard_map/all_gather | solution.py:23
Sparse Core Ops, SparseCore 0:
  13.0 65.7 all-reduce.2
Sparse Core Ops, SparseCore 1:
  15.5 53.2 all-gather.2
where the time goes:
time: 97 us; the launch traced here: 96.7 us
  waiting for transfers between devices  58.7 us (61%)
  between operations  16.3 us (17%)
  other arithmetic  11 us (11%)
  blocking collectives  5.19 us (5%)
  matrix products  4.14 us (4%)
  local copies, waits for them, and re-layouts  1.39 us (1%)
    psum x1, waiting for transfers between devices, body(): average = lax.psum(weighted, 'replica') / total  58.1 us
    sub x1, other arithmetic, nesterov(): new_base = base_params - 0.7 * (average + 0.9 * new_momentum)  6.37 us
    unnamed x1, blocking collectives  5.19 us
    dot_general x1, matrix products, body(): jnp.dot(activations, lax.all_gather(inner_weight[0], 'fsdp', axis=0, tile...  4.14 us
    mul x1, other arithmetic, body(): weighted = own * difference.astype(jnp.float32)  4.04 us
  transfers between devices with their start and end apart: 2, of which 1 were waited for; matrix products, arithmetic and copies ran while one was open for 9% of the time, Pallas kernels for 0%

commit v1 on v0

v1 whole, which is shorter than its diff:
```python
import functools

import jax
import jax.numpy as jnp
from jax import lax
from jax.experimental import pallas as pl
from jax.experimental.pallas import tpu as pltpu
from jax.sharding import PartitionSpec as P

F32, BF16 = jnp.float32, jnp.bfloat16
MIB = 1024 * 1024
HBM = pl.BlockSpec(memory_space=pltpu.HBM)
VMEM = pl.BlockSpec(memory_space=pltpu.VMEM)


def nesterov(average, momentum, base_params):
    new_momentum = 0.9 * momentum + average
    new_base = base_params - 0.7 * (average + 0.9 * new_momentum)
    return (new_base, new_momentum)


def general(activations, inner_weight, local_params, base_params, momentum, inner_steps):
    counts = lax.all_gather(inner_steps, "replica", axis=0, tiled=True)
    total = jnp.sum(counts.astype(F32))
    own = inner_steps[0].astype(F32)
    difference = (base_params - local_params[0]).astype(BF16)
    average = lax.psum(own * difference.astype(F32), "replica") / total
    new_base, new_momentum = nesterov(average, momentum, base_params)
    weight = lax.all_gather(inner_weight[0], "fsdp", axis=0, tiled=True)
    keys = jnp.dot(activations, weight, preferred_element_type=F32).astype(BF16)
    return (keys, new_base, new_momentum)


def index(z, y, c):
    return (z * 2 + y) * 2 + c


def place(p):
    p = p % 8
    return (p, 0) if p < 4 else (7 - p, 1)


def cycle(x, by):
    pairs = [
        (index(*place(p), c), index(*place(p + by), c)) for p in range(8) for c in range(2)
    ]
    return lax.ppermute(x, "fsdp", pairs)


def up(x):
    return cycle(x, 1)


def down(x):
    return cycle(x, -1)


def send_core(x):
    pairs = [(i, i ^ 1) for i in range(16)]
    return lax.ppermute(x, "fsdp", pairs)


def send_x(x):
    return lax.ppermute(x, "replica", [(0, 1), (1, 0)])


def tie(*xs):
    return lax.optimization_barrier(xs)


def cost(flops, bytes_accessed):
    return pl.CostEstimate(flops=int(flops), bytes_accessed=int(bytes_accessed), transcendentals=0)


def params(limit=16):
    return pltpu.CompilerParams(vmem_limit_bytes=limit * MIB)


def difference_kernel(pieces, base, local, steps, out, count, held, sems):
    rows = base.shape[0]
    piece = rows // pieces
    copies = []
    for j in range(pieces):
        for i, ref in enumerate((base, local)):
            at = pl.ds(j * piece, piece)
            copies.append(pltpu.make_async_copy(ref.at[at, :], held.at[i, at, :], sems.at[i, j]))
    load = pltpu.make_async_copy(steps, count, sems.at[0, pieces])
    for copy in copies:
        copy.start()
    load.start()
    for j in range(pieces):
        copies[2 * j].wait()
        copies[2 * j + 1].wait()
        at = pl.ds(j * piece, piece)
        out[at, :] = (held[0, at, :] - held[1, at, :]).astype(BF16)
    load.wait()
    extra = out.shape[0] - rows
    out[pl.ds(rows, extra), :] = jnp.full((extra, out.shape[1]), count[0].astype(F32), F32).astype(BF16)


def difference(base, local, steps):
    rows, width = base.shape
    pieces = 4
    return pl.pallas_call(
        functools.partial(difference_kernel, pieces),
        out_shape=jax.ShapeDtypeStruct((rows + 16, width), BF16),
        in_specs=[HBM, HBM, HBM],
        out_specs=pl.BlockSpec(memory_space=pltpu.VMEM),
        scratch_shapes=[
            pltpu.SMEM((1,), jnp.int32),
            pltpu.VMEM((2, rows, width), F32),
            pltpu.SemaphoreType.DMA((2, pieces + 1)),
        ],
        compiler_params=params(52),
        cost_estimate=cost(2 * rows * width, 10 * rows * width),
        name="difference",
    )(base, local, steps)


def outer_kernel(pieces, base, mom, own, got, new_base, new_mom, held, sems):
    rows = base.shape[0]
    piece = rows // pieces
    mine = own[pl.ds(rows, 16), :][0:1, :].astype(F32)
    theirs = got[pl.ds(rows, 16), :][0:1, :].astype(F32)
    scale = 1.0 / (mine + theirs)
    mine, theirs = mine * scale, theirs * scale
    copies = []
    for j in range(pieces):
        at = pl.ds(j * piece, piece)
        average = mine * own[at, :].astype(F32) + theirs * got[at, :].astype(F32)
        momentum = 0.9 * mom[at, :] + average
        held[1, at, :] = momentum
        held[0, at, :] = base[at, :] - 0.7 * (average + 0.9 * momentum)
        for i, ref in enumerate((new_base, new_mom)):
            copies.append(pltpu.make_async_copy(held.at[i, at, :], ref.at[at, :], sems.at[i, j]))
            copies[-1].start()
    for copy in copies:
        copy.wait()


def outer(base, mom, own, got):
    rows, width = base.shape
    pieces = 8
    shape = jax.ShapeDtypeStruct(base.shape, F32)
    return pl.pallas_call(
        functools.partial(outer_kernel, pieces),
        out_shape=(shape, shape),
        in_specs=[VMEM] * 4,
        out_specs=(HBM, HBM),
        scratch_shapes=[pltpu.VMEM((2, rows, width), F32), pltpu.SemaphoreType.DMA((2, pieces))],
        compiler_params=params(),
        cost_estimate=cost(10 * rows * width, 20 * rows * width),
        name="outer_step",
    )(base, mom, own, got)


def dot(a, b):
    return jnp.dot(a, b, preferred_element_type=F32)


def column(by, mine, depth):
    f = lax.axis_index("fsdp")
    z, y, c = f // 4, (f // 2) % 2, f % 2
    p = (z + y * (7 - 2 * z) + by + 8) % 8
    far = p // 4
    z, y = p + far * (7 - 2 * p), far
    c = c if mine else 1 - c
    return pl.multiple_of(index(z, y, c) * depth, depth)


def partial_kernel(places, whole, first, act, sib, *refs):
    n = len(places)
    refs, (own_out, sib_out) = refs[:-2], refs[-2:]
    parts = 1 if whole else 2
    weights, state = refs[:-2] if not first else refs, refs[-2:]
    depth = act.shape[1] // 16
    own = None if first else state[0][...]
    theirs = None if first else state[1][...]
    at = 0
    for by in places:
        if by == 0:
            w = weights[at][...]
            at += 1
        else:
            w = jnp.concatenate([weights[at][...], weights[at + 1][...]], axis=0)
            at += 2
        columns = pl.ds(column(by, True, depth), depth)
        a, b = dot(act[:, columns], w), dot(sib[:, columns], w)
        own = a if own is None else own + a
        theirs = b if theirs is None else theirs + b
    own_out[...] = own
    sib_out[...] = theirs


def partial_sums(places, act, sib, weights, state):
    tokens = act.shape[0]
    width = weights[0].shape[1]
    out = jax.ShapeDtypeStruct((tokens, width), F32)
    return pl.pallas_call(
        functools.partial(partial_kernel, places, False, not state),
        out_shape=(out, out),
        in_specs=[VMEM] * (2 + len(weights) + len(state)),
        out_specs=(VMEM, VMEM),
        compiler_params=params(),
        cost_estimate=cost(0, 0),
        name="partial_keys",
    )(act, sib, *weights, *state)


def finish_kernel(act, wa, wb, va, vb, own, got, keys):
    half = wa.shape[0]
    depth = 2 * half
    total = own[...] + got[...]
    for mine, a, b in ((True, wa, wb), (False, va, vb)):
        w = jnp.concatenate([a[...], b[...]], axis=0)
        total += dot(act[:, pl.ds(column(4, mine, depth), depth)], w)
    keys[...] = total.astype(BF16)


def finish(act, wa, wb, va, vb, own, got):
    tokens, width = own.shape
    return pl.pallas_call(
        finish_kernel,
        out_shape=jax.ShapeDtypeStruct((tokens, width), BF16),
        in_specs=[VMEM] * 7,
        out_specs=VMEM,
        compiler_params=params(),
        cost_estimate=cost(0, 0),
        name="finish_keys",
    )(act, wa, wb, va, vb, own, got)


def special(activations, inner_weight, local_params, base_params, momentum, inner_steps):
    shape = base_params.shape
    flat = lambda a: a.reshape(-1, shape[-1])
    base, mom, local = flat(base_params), flat(momentum), flat(local_params)
    w = inner_weight[0]
    half = w.shape[0] // 2

    own = difference(base, local, inner_steps)
    got = send_x(own)
    sib = send_core(activations)

    w = tie(w, own)[0]
    wa, wb = w[:half], w[half:]
    ua, da = [up(wa)], [down(wa)]
    wb = tie(wb, sib)[0]
    ub, db = [up(wb)], [down(wb)]
    for _ in range(2):
        ua.append(up(ua[-1]))
        da.append(down(da[-1]))
        ub.append(up(ub[-1]))
        db.append(down(db[-1]))
    state = partial_sums(
        (0, -1, 1, -2, 2), activations, sib,
        (w, ua[0], ub[0], da[0], db[0], ua[1], ub[1], da[1], db[1]), (),
    )
    ua4, db4 = up(ua[2]), down(db[2])
    state = partial_sums((-3, 3), activations, sib, (ua[2], ub[2], da[2], db[2]), state)
    swapped = send_core(state[1])

    ua4, db4, swapped, got = tie(ua4, db4, swapped, got)
    va, vb = send_core(ua4), send_core(db4)
    keys = finish(activations, ua4, db4, va, vb, state[0], swapped)
    new = outer(base, mom, own, got)
    return (keys, new[0].reshape(shape), new[1].reshape(shape))


def solution(mesh):
    fast = mesh.shape["replica"] == 2 and mesh.shape["fsdp"] == 16
    return jax.shard_map(
        special if fast else general,
        mesh=mesh,
        in_specs=(
            P(("replica", "fsdp"), None),
            P("replica", "fsdp", None),
            P("replica", None, None, "fsdp", None),
            P(None, None, "fsdp", None),
            P(None, None, "fsdp", None),
            P("replica"),
        ),
        out_specs=(
            P(("replica", "fsdp"), None),
            P(None, None, "fsdp", None),
            P(None, None, "fsdp", None),
        ),
        check_vma=False,
    )
```

time: 97 us -> 41 us (0.42)
  waiting for transfers between devices: 58.7 us -> 13.8 us
  starting transfers between devices: 0.08 us -> 18.6 us
  between operations: 16.3 us -> 1.39 us
  other arithmetic: 11 us -> 0 us
  Pallas kernels: 0 us -> 6.98 us
  blocking collectives: 5.19 us -> 0 us
  matrix products: 4.14 us -> 0 us
  local copies, waits for them, and re-layouts: 1.39 us -> 0.03 us
    psum x1 -> x0, waiting for transfers between devices: 58.1 us -> none  [body(): average = lax.psum(weighted, 'replica') / total]
    ppermute x0 -> x19, starting transfers between devices: none -> 18.6 us  [the longest x14 15 us: cycle(): return lax.ppermute(x, 'fsdp', pairs)]
    ppermute x0 -> x19, waiting for transfers between devices: none -> 13.8 us  [the longest x14 13.8 us: cycle(): return lax.ppermute(x, 'fsdp', pairs)]
    pallas_call x0 -> x5, Pallas kernels: none -> 6.98 us  [the longest x1 2.45 us: difference(): pl.pallas_call(functools.partial(difference_kernel, pieces), out_shape=ja...]
    sub x1 -> x0, other arithmetic: 6.37 us -> none  [nesterov(): new_base = base_params - 0.7 * (average + 0.9 * new_momentum)]
    unnamed x1 -> x0, blocking collectives: 5.19 us -> none
    dot_general x1 -> x0, matrix products: 4.14 us -> none  [body(): jnp.dot(activations, lax.all_gather(inner_weight[0], 'fsdp', axis=0, tile...]
    mul x1 -> x0, other arithmetic: 4.04 us -> none  [body(): weighted = own * difference.astype(jnp.float32)]
  transfers between devices with their start and end apart: 2 -> 19, of which waited for: 1 -> 8; matrix products, arithmetic and copies ran while one was open for 9% -> 0% of each run, Pallas kernels for 0% -> 15%
where the time goes in v1:
time: 41 us; the launch traced here: 40.9 us
  starting transfers between devices  18.6 us (45%)
  waiting for transfers between devices  13.8 us (34%)
  Pallas kernels  6.98 us (17%)
  between operations  1.39 us (3%)
    ppermute x14, starting transfers between devices, cycle(): return lax.ppermute(x, 'fsdp', pairs)  15 us
    ppermute x14, waiting for transfers between devices, cycle(): return lax.ppermute(x, 'fsdp', pairs)  13.8 us
    ppermute x1, starting transfers between devices, send_x(): return lax.ppermute(x, 'replica', [(0, 1), (1, 0)])  2.56 us
    pallas_call x1, Pallas kernels, difference(): pl.pallas_call(functools.partial(difference_kernel, pieces), out_shape=ja...  2.45 us
    pallas_call x1, Pallas kernels, outer(): pl.pallas_call(functools.partial(outer_kernel, pieces), out_shape=(shape,...  2.25 us
    pallas_call x2, Pallas kernels, partial_sums(): pl.pallas_call(functools.partial(partial_kernel, places, False, not state...  1.27 us
    ppermute x4, starting transfers between devices, send_core(): return lax.ppermute(x, 'fsdp', pairs)  1.1 us
    pallas_call x1, Pallas kernels, finish(): pl.pallas_call(finish_kernel, out_shape=jax.ShapeDtypeStruct((tokens, wid...  1.01 us
  transfers between devices with their start and end apart: 19, of which 8 were waited for; matrix products, arithmetic and copies ran while one was open for 0% of the time, Pallas kernels for 15%

profile of v1, /device:TPU:0, one launch (start us, length us, event | category | flops | bytes accessed | tf_op | source)
XLA Modules:
  0.0 40.9 jit_solution(2095759963330956593)
XLA Ops:
  0.6 0.5 %collective-permute-start.4 = (bf16[256,4096]{1,0:T(8,128)(2,1)}, bf16[256,4096]{1,0:T(8,128)(2,1)S(1)}, u32[]{:S(2)}, u32[]{:S(2)}) collective-permute-start(bf16[256,4096]{1,0:T(8,128)(2,1)} %act.5), channel_id=1, source_target_pairs={{0,1},{1,0},{2,3},{3,2},{4,5},{5,4},{6,7},{7,6},{8,9},{9,8},{10,11... | collective-permute-start | bytes 6291464 | tf_op jit(solution)/shard_map/ppermute | solution.py:60
  1.8 0.0 copy-start.3
  1.8 0.0 copy-start
  1.8 2.4 %difference.1.own = bf16[1040,512]{1,0:T(8,128)(2,1)S(1)} custom-call(f32[1024,512]{1,0:T(8,128)} %bitcast.6, f32[1024,512]{1,0:T(8,128)} %bitcast.11, s32[1]{0:T(128)S(6)} %copy.9.steps), custom_call_target="tpu_custom_call" | custom-call | flops 1048576 | bytes 5242880 | tf_op jit(solution)/shard_map/difference/pallas_call | solution.py:104
  4.3 2.6 %collective-permute-start.16 = (bf16[1040,512]{1,0:T(8,128)(2,1)S(1)}, bf16[1040,512]{1,0:T(8,128)(2,1)S(1)}, u32[]{:S(2)}, u32[]{:S(2)}) collective-permute-start(bf16[1040,512]{1,0:T(8,128)(2,1)S(1)} %difference.1.own), channel_id=1, source_target_pairs={{0,16},{16,0},{1,17},{17,1},{2,18},{18,2},{3,19},{19,3},{4,20},{20... | collective-permute-start | bytes 3194888 | tf_op jit(solution)/shard_map/ppermute | solution.py:64
  6.8 0.0 copy-done.3
  6.9 1.6 %collective-permute-start = (bf16[128,512]{1,0:T(8,128)(2,1)S(1)}, bf16[128,512]{1,0:T(8,128)(2,1)S(1)}, u32[]{:S(2)}, u32[]{:S(2)}) collective-permute-start(bf16[128,512]{1,0:T(8,128)(2,1)S(1)} %get-tuple-element.28), channel_id=1, source_target_pairs={{0,4},{1,5},{4,8},{5,9},{8,12},{9,13},{12,14},{13,15},{14,10},{15,... | collective-permute-start | bytes 393224 | tf_op jit(solution)/shard_map/ppermute | solution.py:47
  8.5 0.4 %collective-permute-start.12 = (bf16[128,512]{1,0:T(8,128)(2,1)S(1)}, bf16[128,512]{1,0:T(8,128)(2,1)S(1)}, u32[]{:S(2)}, u32[]{:S(2)}) collective-permute-start(bf16[128,512]{1,0:T(8,128)(2,1)S(1)} %get-tuple-element.28), channel_id=1, source_target_pairs={{0,2},{1,3},{4,0},{5,1},{8,4},{9,5},{12,8},{13,9},{14,12},{15,13},... | collective-permute-start | bytes 393224 | tf_op jit(solution)/shard_map/ppermute | solution.py:47
  8.9 0.0 collective-permute-done.4.sib
  8.9 1.5 %collective-permute-start.5 = (bf16[128,512]{1,0:T(8,128)(2,1)S(1)}, bf16[128,512]{1,0:T(8,128)(2,1)S(1)}, u32[]{:S(2)}, u32[]{:S(2)}) collective-permute-start(bf16[128,512]{1,0:T(8,128)(2,1)S(1)} %get-tuple-element.16), channel_id=1, source_target_pairs={{0,2},{1,3},{4,0},{5,1},{8,4},{9,5},{12,8},{13,9},{14,12},{15,13},... | collective-permute-start | bytes 393224 | tf_op jit(solution)/shard_map/ppermute | solution.py:47
  10.5 0.5 %collective-permute-start.9 = (bf16[128,512]{1,0:T(8,128)(2,1)S(1)}, bf16[128,512]{1,0:T(8,128)(2,1)S(1)}, u32[]{:S(2)}, u32[]{:S(2)}) collective-permute-start(bf16[128,512]{1,0:T(8,128)(2,1)S(1)} %get-tuple-element.16), channel_id=1, source_target_pairs={{0,4},{1,5},{4,8},{5,9},{8,12},{9,13},{12,14},{13,15},{14,10},{15,... | collective-permute-start | bytes 393224 | tf_op jit(solution)/shard_map/ppermute | solution.py:47
  11.0 1.6 %collective-permute-done.refs_1_ = bf16[128,512]{1,0:T(8,128)(2,1)S(1)} collective-permute-done((bf16[128,512]{1,0:T(8,128)(2,1)S(1)}, bf16[128,512]{1,0:T(8,128)(2,1)S(1)}, u32[]{:S(2)}, u32[]{:S(2)}) %collective-permute-start) | collective-permute-done | bytes 131104 | tf_op jit(solution)/shard_map/ppermute | solution.py:47
  12.6 2.3 %collective-permute-start.1 = (bf16[128,512]{1,0:T(8,128)(2,1)S(1)}, bf16[128,512]{1,0:T(8,128)(2,1)S(1)}, u32[]{:S(2)}, u32[]{:S(2)}) collective-permute-start(bf16[128,512]{1,0:T(8,128)(2,1)S(1)} %collective-permute-done.refs_1_), channel_id=1, source_target_pairs={{0,4},{1,5},{4,8},{5,9},{8,12},{9,13},{12,14},{13,15},{14,10},{15,... | collective-permute-start | bytes 393224 | tf_op jit(solution)/shard_map/ppermute | solution.py:47
  14.8 0.0 collective-permute-done.12.refs_3_
  14.9 0.4 %collective-permute-start.13 = (bf16[128,512]{1,0:T(8,128)(2,1)S(1)}, bf16[128,512]{1,0:T(8,128)(2,1)S(1)}, u32[]{:S(2)}, u32[]{:S(2)}) collective-permute-start(bf16[128,512]{1,0:T(8,128)(2,1)S(1)} %collective-permute-done.12.refs_3_), channel_id=1, source_target_pairs={{0,2},{1,3},{4,0},{5,1},{8,4},{9,5},{12,8},{13,9},{14,12},{15,13},... | collective-permute-start | bytes 393224 | tf_op jit(solution)/shard_map/ppermute | solution.py:47
  15.3 2.1 %collective-permute-done.5.refs_4_ = bf16[128,512]{1,0:T(8,128)(2,1)S(1)} collective-permute-done((bf16[128,512]{1,0:T(8,128)(2,1)S(1)}, bf16[128,512]{1,0:T(8,128)(2,1)S(1)}, u32[]{:S(2)}, u32[]{:S(2)}) %collective-permute-start.5) | collective-permute-done | bytes 131104 | tf_op jit(solution)/shard_map/ppermute | solution.py:47
  17.4 0.4 %collective-permute-start.6 = (bf16[128,512]{1,0:T(8,128)(2,1)S(1)}, bf16[128,512]{1,0:T(8,128)(2,1)S(1)}, u32[]{:S(2)}, u32[]{:S(2)}) collective-permute-start(bf16[128,512]{1,0:T(8,128)(2,1)S(1)} %collective-permute-done.5.refs_4_), channel_id=1, source_target_pairs={{0,2},{1,3},{4,0},{5,1},{8,4},{9,5},{12,8},{13,9},{14,12},{15,13},... | collective-permute-start | bytes 393224 | tf_op jit(solution)/shard_map/ppermute | solution.py:47
  17.8 0.0 collective-permute-done.9.refs_2_
  17.8 1.6 %collective-permute-start.10 = (bf16[128,512]{1,0:T(8,128)(2,1)S(1)}, bf16[128,512]{1,0:T(8,128)(2,1)S(1)}, u32[]{:S(2)}, u32[]{:S(2)}) collective-permute-start(bf16[128,512]{1,0:T(8,128)(2,1)S(1)} %collective-permute-done.9.refs_2_), channel_id=1, source_target_pairs={{0,4},{1,5},{4,8},{5,9},{8,12},{9,13},{12,14},{13,15},{14,10},{15,... | collective-permute-start | bytes 393224 | tf_op jit(solution)/shard_map/ppermute | solution.py:47
  19.4 0.0 collective-permute-done.1.refs_5_
  19.4 1.6 %collective-permute-start.2 = (bf16[128,512]{1,0:T(8,128)(2,1)S(1)}, bf16[128,512]{1,0:T(8,128)(2,1)S(1)}, u32[]{:S(2)}, u32[]{:S(2)}) collective-permute-start(bf16[128,512]{1,0:T(8,128)(2,1)S(1)} %collective-permute-done.1.refs_5_), channel_id=1, source_target_pairs={{0,4},{1,5},{4,8},{5,9},{8,12},{9,13},{12,14},{13,15},{14,10},{15,... | collective-permute-start | bytes 393224 | tf_op jit(solution)/shard_map/ppermute | solution.py:47
  21.0 0.1 collective-permute-done.13.refs_7_
  21.1 0.4 %collective-permute-start.14 = (bf16[128,512]{1,0:T(8,128)(2,1)S(1)}, bf16[128,512]{1,0:T(8,128)(2,1)S(1)}, u32[]{:S(2)}, u32[]{:S(2)}) collective-permute-start(bf16[128,512]{1,0:T(8,128)(2,1)S(1)} %collective-permute-done.13.refs_7_), channel_id=1, source_target_pairs={{0,2},{1,3},{4,0},{5,1},{8,4},{9,5},{12,8},{13,9},{14,12},{15,13},... | collective-permute-start | bytes 393224 | tf_op jit(solution)/shard_map/ppermute | solution.py:47
  21.6 2.3 %collective-permute-done.6.refs_8_ = bf16[128,512]{1,0:T(8,128)(2,1)S(1)} collective-permute-done((bf16[128,512]{1,0:T(8,128)(2,1)S(1)}, bf16[128,512]{1,0:T(8,128)(2,1)S(1)}, u32[]{:S(2)}, u32[]{:S(2)}) %collective-permute-start.6) | collective-permute-done | bytes 131104 | tf_op jit(solution)/shard_map/ppermute | solution.py:47
  23.9 0.3 collective-permute-start.7
  24.2 0.0 collective-permute-done.10.refs_6_
  24.2 1.8 %collective-permute-start.11 = (bf16[128,512]{1,0:T(8,128)(2,1)S(1)}, bf16[128,512]{1,0:T(8,128)(2,1)S(1)}, u32[]{:S(2)}, u32[]{:S(2)}) collective-permute-start(bf16[128,512]{1,0:T(8,128)(2,1)S(1)} %collective-permute-done.10.refs_6_), channel_id=1, source_target_pairs={{0,4},{1,5},{4,8},{5,9},{8,12},{9,13},{12,14},{13,15},{14,10},{15,... | collective-permute-start | bytes 393224 | tf_op jit(solution)/shard_map/ppermute | solution.py:47
  25.9 0.0 copy-done
  25.9 0.8 %partial_keys.2 = (f32[256,512]{1,0:T(8,128)S(1)}, f32[256,512]{1,0:T(8,128)S(1)}) custom-call(bf16[256,4096]{1,0:T(8,128)(2,1)S(1)} %copy-done, bf16[256,4096]{1,0:T(8,128)(2,1)S(1)} %collective-permute-done.4.sib, bf16[256,512]{1,0:T(8,128)(2,1)S(1)} %bitcast.10, bf16[128,512]{1,0:T(8,128)(2,1)S(1)} %collective-permute-done.refs_1_, ...), custom_call_target="tpu_custom_call" | custom-call | tf_op jit(solution)/shard_map/partial_keys/pallas_call | solution.py:199
  26.8 0.0 collective-permute-done.2.refs_0_
  26.8 0.0 collective-permute-done.14.refs_2_
  26.8 2.1 %collective-permute-done.7.refs_3_ = bf16[128,512]{1,0:T(8,128)(2,1)S(1)} collective-permute-done((bf16[128,512]{1,0:T(8,128)(2,1)S(1)}, bf16[128,512]{1,0:T(8,128)(2,1)S(1)}, u32[]{:S(2)}, u32[]{:S(2)}) %collective-permute-start.7) | collective-permute-done | bytes 131104 | tf_op jit(solution)/shard_map/ppermute | solution.py:47
  28.9 0.3 collective-permute-done.11.refs_1_
  29.1 0.0 copy-start.1
  29.1 0.0 copy-start.2
  29.1 0.4 %partial_keys.3 = (f32[256,512]{1,0:T(8,128)S(1)}, f32[256,512]{1,0:T(8,128)S(1)}) custom-call(bf16[256,4096]{1,0:T(8,128)(2,1)S(1)} %copy-done, bf16[256,4096]{1,0:T(8,128)(2,1)S(1)} %collective-permute-done.4.sib, bf16[128,512]{1,0:T(8,128)(2,1)S(1)} %collective-permute-done.2.refs_0_, bf16[128,512]{1,0:T(8,128)(2,1)S(1)} %collective-permute-done.11.refs_1_, ...), custom_call_target="tpu_custom_call" | custom-call | tf_op jit(solution)/shard_map/partial_keys/pallas_call | solution.py:199
  29.6 0.1 collective-permute-start.15
  29.7 1.8 %collective-permute-start.3 = (bf16[128,512]{1,0:T(8,128)(2,1)S(1)}, bf16[128,512]{1,0:T(8,128)(2,1)S(1)}, u32[]{:S(2)}, u32[]{:S(2)}) collective-permute-start(bf16[128,512]{1,0:T(8,128)(2,1)S(1)} %collective-permute-done.2.refs_0_), channel_id=1, source_target_pairs={{0,4},{1,5},{4,8},{5,9},{8,12},{9,13},{12,14},{13,15},{14,10},{15,... | collective-permute-start | bytes 393224 | tf_op jit(solution)/shard_map/ppermute | solution.py:47
  31.5 0.3 collective-permute-start.8
  31.8 3.8 %collective-permute-done.3.wa = bf16[128,512]{1,0:T(8,128)(2,1)S(1)} collective-permute-done((bf16[128,512]{1,0:T(8,128)(2,1)S(1)}, bf16[128,512]{1,0:T(8,128)(2,1)S(1)}, u32[]{:S(2)}, u32[]{:S(2)}) %collective-permute-start.3) | collective-permute-done | bytes 131104 | tf_op jit(solution)/shard_map/ppermute | solution.py:47
  35.6 0.0 collective-permute-done.16.got
  35.6 1.5 %collective-permute-done.8.wb = bf16[128,512]{1,0:T(8,128)(2,1)S(1)} collective-permute-done((bf16[128,512]{1,0:T(8,128)(2,1)S(1)}, bf16[128,512]{1,0:T(8,128)(2,1)S(1)}, u32[]{:S(2)}, u32[]{:S(2)}) %collective-permute-start.8) | collective-permute-done | bytes 131104 | tf_op jit(solution)/shard_map/ppermute | solution.py:47
  37.0 0.0 collective-permute-done.15.got
  37.1 0.0 collective-permute-start.17
  37.1 0.5 %collective-permute-start.18 = (bf16[128,512]{1,0:T(8,128)(2,1)S(1)}, bf16[128,512]{1,0:T(8,128)(2,1)S(1)}, u32[]{:S(2)}, u32[]{:S(2)}) collective-permute-start(bf16[128,512]{1,0:T(8,128)(2,1)S(1)} %collective-permute-done.8.wb), channel_id=1, source_target_pairs={{0,1},{1,0},{2,3},{3,2},{4,5},{5,4},{6,7},{7,6},{8,9},{9,8},{10,11... | collective-permute-start | bytes 393224 | tf_op jit(solution)/shard_map/ppermute | solution.py:60
  37.6 0.0 copy-done.1
  37.6 0.0 copy-done.2
  37.6 2.2 %outer_step.1 = (f32[1024,512]{1,0:T(8,128)}, f32[1024,512]{1,0:T(8,128)}) custom-call(f32[1024,512]{1,0:T(8,128)S(1)} %bitcast.7, f32[1024,512]{1,0:T(8,128)S(1)} %bitcast.8, bf16[1040,512]{1,0:T(8,128)(2,1)S(1)} %difference.1.own, bf16[1040,512]{1,0:T(8,128)(2,1)S(1)} %collective-permute-done.16.got), custom_call_target="tpu_custom_call" | custom-call | flops 5242880 | bytes 10485760 | tf_op jit(solution)/shard_map/outer_step/pallas_call | solution.py:145
  39.8 0.0 collective-permute-done.17.va
  39.8 0.0 collective-permute-done.18.vb
  39.8 1.0 %finish_keys.1 = bf16[256,512]{1,0:T(8,128)(2,1)} custom-call(bf16[256,4096]{1,0:T(8,128)(2,1)S(1)} %copy-done, bf16[128,512]{1,0:T(8,128)(2,1)S(1)} %collective-permute-done.3.wa, bf16[128,512]{1,0:T(8,128)(2,1)S(1)} %collective-permute-done.8.wb, bf16[128,512]{1,0:T(8,128)(2,1)S(1)} %collective-permute-done.17.va, ...), custom_call_target="tpu_custom_call" | custom-call | tf_op jit(solution)/shard_map/finish_keys/pallas_call | solution.py:222
  (1 shorter events, 0.0 us)
Async XLA Ops:
  0.6 8.3 %collective-permute-start.4 = (bf16[256,4096]{1,0:T(8,128)(2,1)}, bf16[256,4096]{1,0:T(8,128)(2,1)S(1)}, u32[]{:S(2)}, u32[]{:S(2)}) collective-permute-start(bf16[256,4096]{1,0:T(8,128)(2,1)} %act.5), channel_id=1, source_target_pairs={{0,1},{1,0},{2,3},{3,2},{4,5},{5,4},{6,7},{7,6},{8,9},{9,8},{10,11... | collective-permute-start | bytes 6291464 | tf_op jit(solution)/shard_map/ppermute | solution.py:60
  1.8 5.0 %copy-start.3 = (bf16[1,256,512]{2,1,0:T(8,128)(2,1)S(1)}, bf16[1,256,512]{2,1,0:T(8,128)(2,1)}, u32[]{:S(2)}) copy-start(bf16[1,256,512]{2,1,0:T(8,128)(2,1)} %param.7) | copy-start | bytes 786436
  1.8 24.1 %copy-start = (bf16[256,4096]{1,0:T(8,128)(2,1)S(1)}, bf16[256,4096]{1,0:T(8,128)(2,1)}, u32[]{:S(2)}) copy-start(bf16[256,4096]{1,0:T(8,128)(2,1)} %act.5) | copy-start | bytes 6291460
  4.3 31.3 %collective-permute-start.16 = (bf16[1040,512]{1,0:T(8,128)(2,1)S(1)}, bf16[1040,512]{1,0:T(8,128)(2,1)S(1)}, u32[]{:S(2)}, u32[]{:S(2)}) collective-permute-start(bf16[1040,512]{1,0:T(8,128)(2,1)S(1)} %difference.1.own), channel_id=1, source_target_pairs={{0,16},{16,0},{1,17},{17,1},{2,18},{18,2},{3,19},{19,3},{4,20},{20... | collective-permute-start | bytes 3194888 | tf_op jit(solution)/shard_map/ppermute | solution.py:64
  6.9 5.7 %collective-permute-start = (bf16[128,512]{1,0:T(8,128)(2,1)S(1)}, bf16[128,512]{1,0:T(8,128)(2,1)S(1)}, u32[]{:S(2)}, u32[]{:S(2)}) collective-permute-start(bf16[128,512]{1,0:T(8,128)(2,1)S(1)} %get-tuple-element.28), channel_id=1, source_target_pairs={{0,4},{1,5},{4,8},{5,9},{8,12},{9,13},{12,14},{13,15},{14,10},{15,... | collective-permute-start | bytes 393224 | tf_op jit(solution)/shard_map/ppermute | solution.py:47
  8.5 6.4 %collective-permute-start.12 = (bf16[128,512]{1,0:T(8,128)(2,1)S(1)}, bf16[128,512]{1,0:T(8,128)(2,1)S(1)}, u32[]{:S(2)}, u32[]{:S(2)}) collective-permute-start(bf16[128,512]{1,0:T(8,128)(2,1)S(1)} %get-tuple-element.28), channel_id=1, source_target_pairs={{0,2},{1,3},{4,0},{5,1},{8,4},{9,5},{12,8},{13,9},{14,12},{15,13},... | collective-permute-start | bytes 393224 | tf_op jit(solution)/shard_map/ppermute | solution.py:47
  8.9 8.4 %collective-permute-start.5 = (bf16[128,512]{1,0:T(8,128)(2,1)S(1)}, bf16[128,512]{1,0:T(8,128)(2,1)S(1)}, u32[]{:S(2)}, u32[]{:S(2)}) collective-permute-start(bf16[128,512]{1,0:T(8,128)(2,1)S(1)} %get-tuple-element.16), channel_id=1, source_target_pairs={{0,2},{1,3},{4,0},{5,1},{8,4},{9,5},{12,8},{13,9},{14,12},{15,13},... | collective-permute-start | bytes 393224 | tf_op jit(solution)/shard_map/ppermute | solution.py:47
  10.5 7.4 %collective-permute-start.9 = (bf16[128,512]{1,0:T(8,128)(2,1)S(1)}, bf16[128,512]{1,0:T(8,128)(2,1)S(1)}, u32[]{:S(2)}, u32[]{:S(2)}) collective-permute-start(bf16[128,512]{1,0:T(8,128)(2,1)S(1)} %get-tuple-element.16), channel_id=1, source_target_pairs={{0,4},{1,5},{4,8},{5,9},{8,12},{9,13},{12,14},{13,15},{14,10},{15,... | collective-permute-start | bytes 393224 | tf_op jit(solution)/shard_map/ppermute | solution.py:47
  12.6 6.9 %collective-permute-start.1 = (bf16[128,512]{1,0:T(8,128)(2,1)S(1)}, bf16[128,512]{1,0:T(8,128)(2,1)S(1)}, u32[]{:S(2)}, u32[]{:S(2)}) collective-permute-start(bf16[128,512]{1,0:T(8,128)(2,1)S(1)} %collective-permute-done.refs_1_), channel_id=1, source_target_pairs={{0,4},{1,5},{4,8},{5,9},{8,12},{9,13},{12,14},{13,15},{14,10},{15,... | collective-permute-start | bytes 393224 | tf_op jit(solution)/shard_map/ppermute | solution.py:47
  14.9 6.3 %collective-permute-start.13 = (bf16[128,512]{1,0:T(8,128)(2,1)S(1)}, bf16[128,512]{1,0:T(8,128)(2,1)S(1)}, u32[]{:S(2)}, u32[]{:S(2)}) collective-permute-start(bf16[128,512]{1,0:T(8,128)(2,1)S(1)} %collective-permute-done.12.refs_3_), channel_id=1, source_target_pairs={{0,2},{1,3},{4,0},{5,1},{8,4},{9,5},{12,8},{13,9},{14,12},{15,13},... | collective-permute-start | bytes 393224 | tf_op jit(solution)/shard_map/ppermute | solution.py:47
  17.4 6.5 %collective-permute-start.6 = (bf16[128,512]{1,0:T(8,128)(2,1)S(1)}, bf16[128,512]{1,0:T(8,128)(2,1)S(1)}, u32[]{:S(2)}, u32[]{:S(2)}) collective-permute-start(bf16[128,512]{1,0:T(8,128)(2,1)S(1)} %collective-permute-done.5.refs_4_), channel_id=1, source_target_pairs={{0,2},{1,3},{4,0},{5,1},{8,4},{9,5},{12,8},{13,9},{14,12},{15,13},... | collective-permute-start | bytes 393224 | tf_op jit(solution)/shard_map/ppermute | solution.py:47
  17.8 6.3 %collective-permute-start.10 = (bf16[128,512]{1,0:T(8,128)(2,1)S(1)}, bf16[128,512]{1,0:T(8,128)(2,1)S(1)}, u32[]{:S(2)}, u32[]{:S(2)}) collective-permute-start(bf16[128,512]{1,0:T(8,128)(2,1)S(1)} %collective-permute-done.9.refs_2_), channel_id=1, source_target_pairs={{0,4},{1,5},{4,8},{5,9},{8,12},{9,13},{12,14},{13,15},{14,10},{15,... | collective-permute-start | bytes 393224 | tf_op jit(solution)/shard_map/ppermute | solution.py:47
  19.4 7.4 %collective-permute-start.2 = (bf16[128,512]{1,0:T(8,128)(2,1)S(1)}, bf16[128,512]{1,0:T(8,128)(2,1)S(1)}, u32[]{:S(2)}, u32[]{:S(2)}) collective-permute-start(bf16[128,512]{1,0:T(8,128)(2,1)S(1)} %collective-permute-done.1.refs_5_), channel_id=1, source_target_pairs={{0,4},{1,5},{4,8},{5,9},{8,12},{9,13},{12,14},{13,15},{14,10},{15,... | collective-permute-start | bytes 393224 | tf_op jit(solution)/shard_map/ppermute | solution.py:47
  21.1 5.7 %collective-permute-start.14 = (bf16[128,512]{1,0:T(8,128)(2,1)S(1)}, bf16[128,512]{1,0:T(8,128)(2,1)S(1)}, u32[]{:S(2)}, u32[]{:S(2)}) collective-permute-start(bf16[128,512]{1,0:T(8,128)(2,1)S(1)} %collective-permute-done.13.refs_7_), channel_id=1, source_target_pairs={{0,2},{1,3},{4,0},{5,1},{8,4},{9,5},{12,8},{13,9},{14,12},{15,13},... | collective-permute-start | bytes 393224 | tf_op jit(solution)/shard_map/ppermute | solution.py:47
  23.9 5.0 %collective-permute-start.7 = (bf16[128,512]{1,0:T(8,128)(2,1)S(1)}, bf16[128,512]{1,0:T(8,128)(2,1)S(1)}, u32[]{:S(2)}, u32[]{:S(2)}) collective-permute-start(bf16[128,512]{1,0:T(8,128)(2,1)S(1)} %collective-permute-done.6.refs_8_), channel_id=1, source_target_pairs={{0,2},{1,3},{4,0},{5,1},{8,4},{9,5},{12,8},{13,9},{14,12},{15,13},... | collective-permute-start | bytes 393224 | tf_op jit(solution)/shard_map/ppermute | solution.py:47
  24.2 5.0 %collective-permute-start.11 = (bf16[128,512]{1,0:T(8,128)(2,1)S(1)}, bf16[128,512]{1,0:T(8,128)(2,1)S(1)}, u32[]{:S(2)}, u32[]{:S(2)}) collective-permute-start(bf16[128,512]{1,0:T(8,128)(2,1)S(1)} %collective-permute-done.10.refs_6_), channel_id=1, source_target_pairs={{0,4},{1,5},{4,8},{5,9},{8,12},{9,13},{12,14},{13,15},{14,10},{15,... | collective-permute-start | bytes 393224 | tf_op jit(solution)/shard_map/ppermute | solution.py:47
  29.1 8.4 %copy-start.1 = (f32[2,2,256,512]{3,2,1,0:T(8,128)S(1)}, f32[2,2,256,512]{3,2,1,0:T(8,128)}, u32[]{:S(2)}) copy-start(f32[2,2,256,512]{3,2,1,0:T(8,128)} %param.9) | copy-start | bytes 6291460
  29.1 8.4 %copy-start.2 = (f32[2,2,256,512]{3,2,1,0:T(8,128)S(1)}, f32[2,2,256,512]{3,2,1,0:T(8,128)}, u32[]{:S(2)}) copy-start(f32[2,2,256,512]{3,2,1,0:T(8,128)} %param.10) | copy-start | bytes 6291460
  29.6 7.5 %collective-permute-start.15 = (f32[256,512]{1,0:T(8,128)S(1)}, f32[256,512]{1,0:T(8,128)S(1)}, u32[]{:S(2)}, u32[]{:S(2)}) collective-permute-start(f32[256,512]{1,0:T(8,128)S(1)} %get-tuple-element.19), channel_id=1, source_target_pairs={{0,1},{1,0},{2,3},{3,2},{4,5},{5,4},{6,7},{7,6},{8,9},{9,8},{10,11... | collective-permute-start | bytes 1572872 | tf_op jit(solution)/shard_map/ppermute | solution.py:60
  29.7 5.9 %collective-permute-start.3 = (bf16[128,512]{1,0:T(8,128)(2,1)S(1)}, bf16[128,512]{1,0:T(8,128)(2,1)S(1)}, u32[]{:S(2)}, u32[]{:S(2)}) collective-permute-start(bf16[128,512]{1,0:T(8,128)(2,1)S(1)} %collective-permute-done.2.refs_0_), channel_id=1, source_target_pairs={{0,4},{1,5},{4,8},{5,9},{8,12},{9,13},{12,14},{13,15},{14,10},{15,... | collective-permute-start | bytes 393224 | tf_op jit(solution)/shard_map/ppermute | solution.py:47
  31.5 5.6 %collective-permute-start.8 = (bf16[128,512]{1,0:T(8,128)(2,1)S(1)}, bf16[128,512]{1,0:T(8,128)(2,1)S(1)}, u32[]{:S(2)}, u32[]{:S(2)}) collective-permute-start(bf16[128,512]{1,0:T(8,128)(2,1)S(1)} %collective-permute-done.7.refs_3_), channel_id=1, source_target_pairs={{0,2},{1,3},{4,0},{5,1},{8,4},{9,5},{12,8},{13,9},{14,12},{15,13},... | collective-permute-start | bytes 393224 | tf_op jit(solution)/shard_map/ppermute | solution.py:47
  37.1 2.8 %collective-permute-start.17 = (bf16[128,512]{1,0:T(8,128)(2,1)S(1)}, bf16[128,512]{1,0:T(8,128)(2,1)S(1)}, u32[]{:S(2)}, u32[]{:S(2)}) collective-permute-start(bf16[128,512]{1,0:T(8,128)(2,1)S(1)} %collective-permute-done.3.wa), channel_id=1, source_target_pairs={{0,1},{1,0},{2,3},{3,2},{4,5},{5,4},{6,7},{7,6},{8,9},{9,8},{10,11... | collective-permute-start | bytes 393224 | tf_op jit(solution)/shard_map/ppermute | solution.py:60
  37.1 2.8 %collective-permute-start.18 = (bf16[128,512]{1,0:T(8,128)(2,1)S(1)}, bf16[128,512]{1,0:T(8,128)(2,1)S(1)}, u32[]{:S(2)}, u32[]{:S(2)}) collective-permute-start(bf16[128,512]{1,0:T(8,128)(2,1)S(1)} %collective-permute-done.8.wb), channel_id=1, source_target_pairs={{0,1},{1,0},{2,3},{3,2},{4,5},{5,4},{6,7},{7,6},{8,9},{9,8},{10,11... | collective-permute-start | bytes 393224 | tf_op jit(solution)/shard_map/ppermute | solution.py:60

commit v2 on v1

--- a/solution.py
+++ b/solution.py
@@ -76,7 +76,7 @@
     return pltpu.CompilerParams(vmem_limit_bytes=limit * MIB)
 
 
-def difference_kernel(pieces, base, local, steps, out, count, held, sems):
+def difference_kernel(pieces, base, local, steps, out, held, sems):
     rows = base.shape[0]
     piece = rows // pieces
     copies = []
@@ -84,18 +84,16 @@
         for i, ref in enumerate((base, local)):
             at = pl.ds(j * piece, piece)
             copies.append(pltpu.make_async_copy(ref.at[at, :], held.at[i, at, :], sems.at[i, j]))
-    load = pltpu.make_async_copy(steps, count, sems.at[0, pieces])
+
     for copy in copies:
         copy.start()
-    load.start()
     for j in range(pieces):
         copies[2 * j].wait()
         copies[2 * j + 1].wait()
         at = pl.ds(j * piece, piece)
         out[at, :] = (held[0, at, :] - held[1, at, :]).astype(BF16)
-    load.wait()
     extra = out.shape[0] - rows
-    out[pl.ds(rows, extra), :] = jnp.full((extra, out.shape[1]), count[0].astype(F32), F32).astype(BF16)
+    out[pl.ds(rows, extra), :] = jnp.broadcast_to(steps[...].astype(F32), (extra, out.shape[1])).astype(BF16)
 
 
 def difference(base, local, steps):
@@ -104,17 +102,16 @@
     return pl.pallas_call(
         functools.partial(difference_kernel, pieces),
         out_shape=jax.ShapeDtypeStruct((rows + 16, width), BF16),
-        in_specs=[HBM, HBM, HBM],
+        in_specs=[HBM, HBM, VMEM],
         out_specs=pl.BlockSpec(memory_space=pltpu.VMEM),
         scratch_shapes=[
-            pltpu.SMEM((1,), jnp.int32),
             pltpu.VMEM((2, rows, width), F32),
-            pltpu.SemaphoreType.DMA((2, pieces + 1)),
+            pltpu.SemaphoreType.DMA((2, pieces)),
         ],
         compiler_params=params(52),
         cost_estimate=cost(2 * rows * width, 10 * rows * width),
         name="difference",
-    )(base, local, steps)
+    )(base, local, steps.reshape(1, 1))
 
 
 def outer_kernel(pieces, base, mom, own, got, new_base, new_mom, held, sems):
@@ -189,16 +186,16 @@
         own = a if own is None else own + a
         theirs = b if theirs is None else theirs + b
     own_out[...] = own
-    sib_out[...] = theirs
-
-
-def partial_sums(places, act, sib, weights, state):
+    sib_out[...] = theirs.astype(sib_out.dtype)
+
+
+def partial_sums(places, act, sib, weights, state, kind=F32):
     tokens = act.shape[0]
     width = weights[0].shape[1]
     out = jax.ShapeDtypeStruct((tokens, width), F32)
     return pl.pallas_call(
         functools.partial(partial_kernel, places, False, not state),
-        out_shape=(out, out),
+        out_shape=(out, jax.ShapeDtypeStruct((tokens, width), kind)),
         in_specs=[VMEM] * (2 + len(weights) + len(state)),
         out_specs=(VMEM, VMEM),
         compiler_params=params(),
@@ -210,7 +207,7 @@
 def finish_kernel(act, wa, wb, va, vb, own, got, keys):
     half = wa.shape[0]
     depth = 2 * half
-    total = own[...] + got[...]
+    total = own[...] + got[...].astype(F32)
     for mine, a, b in ((True, wa, wb), (False, va, vb)):
         w = jnp.concatenate([a[...], b[...]], axis=0)
         total += dot(act[:, pl.ds(column(4, mine, depth), depth)], w)
@@ -246,23 +243,26 @@
     ua, da = [up(wa)], [down(wa)]
     wb = tie(wb, sib)[0]
     ub, db = [up(wb)], [down(wb)]
-    for _ in range(2):
-        ua.append(up(ua[-1]))
-        da.append(down(da[-1]))
-        ub.append(up(ub[-1]))
-        db.append(down(db[-1]))
-    state = partial_sums(
-        (0, -1, 1, -2, 2), activations, sib,
-        (w, ua[0], ub[0], da[0], db[0], ua[1], ub[1], da[1], db[1]), (),
-    )
+    ua.append(up(ua[0]))
+    da.append(down(da[0]))
+    ub.append(up(ub[0]))
+    db.append(down(db[0]))
+    state = partial_sums((0, -1, 1), activations, sib, (w, ua[0], ub[0], da[0], db[0]), ())
+    ua[1], da[1], *state = tie(ua[1], da[1], *state)
+    ua.append(up(ua[1]))
+    da.append(down(da[1]))
+    ub.append(up(ub[1]))
+    db.append(down(db[1]))
+    state = partial_sums((-2, 2), activations, sib, (ua[1], ub[1], da[1], db[1]), state)
+    ua[2], db[2], *state = tie(ua[2], db[2], *state)
     ua4, db4 = up(ua[2]), down(db[2])
-    state = partial_sums((-3, 3), activations, sib, (ua[2], ub[2], da[2], db[2]), state)
-    swapped = send_core(state[1])
-
-    ua4, db4, swapped, got = tie(ua4, db4, swapped, got)
+    own_sum, sib_sum = partial_sums((-3, 3), activations, sib, (ua[2], ub[2], da[2], db[2]), state, BF16)
+    swapped = send_core(sib_sum)
+    got, own_sum = tie(got, own_sum)
+    new = outer(base, mom, own, got)
+    ua4, db4, *new = tie(ua4, db4, *new)
     va, vb = send_core(ua4), send_core(db4)
-    keys = finish(activations, ua4, db4, va, vb, state[0], swapped)
-    new = outer(base, mom, own, got)
+    keys = finish(activations, ua4, db4, va, vb, own_sum, swapped)
     return (keys, new[0].reshape(shape), new[1].reshape(shape))
 
 

time: 41 us -> 36.1 us (0.88)
  waiting for transfers between devices: 13.8 us -> 9.34 us
  starting transfers between devices: 18.6 us -> 18 us
    ppermute x14, waiting for transfers between devices: 13.8 us -> 7.96 us  [cycle(): return lax.ppermute(x, 'fsdp', pairs)]
    ppermute x4, waiting for transfers between devices: 0.01 us -> 1.03 us  [send_core(): return lax.ppermute(x, 'fsdp', pairs)]
    ppermute x14, starting transfers between devices: 15 us -> 14.3 us  [cycle(): return lax.ppermute(x, 'fsdp', pairs)]
    pallas_call x2 -> x3, Pallas kernels: 1.27 us -> 1.44 us  [partial_sums(): pl.pallas_call(functools.partial(partial_kernel, places, False, not state...]
  transfers between devices with their start and end apart: 19 -> 19, of which waited for: 8 -> 9; matrix products, arithmetic and copies ran while one was open for 0% -> 0% of each run, Pallas kernels for 15% -> 17%
where the time goes in v2:
time: 36.1 us; the launch traced here: 35.9 us
  starting transfers between devices  18 us (50%)
  waiting for transfers between devices  9.34 us (26%)
  Pallas kernels  7.14 us (20%)
  between operations  1.38 us (4%)
    ppermute x14, starting transfers between devices, cycle(): return lax.ppermute(x, 'fsdp', pairs)  14.3 us
    ppermute x14, waiting for transfers between devices, cycle(): return lax.ppermute(x, 'fsdp', pairs)  7.96 us
    ppermute x1, starting transfers between devices, send_x(): return lax.ppermute(x, 'replica', [(0, 1), (1, 0)])  2.56 us
    pallas_call x1, Pallas kernels, difference(): pl.pallas_call(functools.partial(difference_kernel, pieces), out_shape=ja...  2.44 us
    pallas_call x1, Pallas kernels, outer(): pl.pallas_call(functools.partial(outer_kernel, pieces), out_shape=(shape,...  2.25 us
    pallas_call x3, Pallas kernels, partial_sums(): pl.pallas_call(functools.partial(partial_kernel, places, False, not state...  1.44 us
    ppermute x4, starting transfers between devices, send_core(): return lax.ppermute(x, 'fsdp', pairs)  1.16 us
    ppermute x4, waiting for transfers between devices, send_core(): return lax.ppermute(x, 'fsdp', pairs)  1.03 us
  transfers between devices with their start and end apart: 19, of which 9 were waited for; matrix products, arithmetic and copies ran while one was open for 0% of the time, Pallas kernels for 17%

profile of v2, /device:TPU:0, one launch (start us, length us, event | category | flops | bytes accessed | tf_op | source)
XLA Modules:
  0.0 35.9 jit_solution(1935759458134296777)
XLA Ops:
  0.6 0.5 %collective-permute-start.4 = (bf16[256,4096]{1,0:T(8,128)(2,1)}, bf16[256,4096]{1,0:T(8,128)(2,1)S(1)}, u32[]{:S(2)}, u32[]{:S(2)}) collective-permute-start(bf16[256,4096]{1,0:T(8,128)(2,1)} %act.7), channel_id=1, source_target_pairs={{0,1},{1,0},{2,3},{3,2},{4,5},{5,4},{6,7},{7,6},{8,9},{9,8},{10,11... | collective-permute-start | bytes 6291464 | tf_op jit(solution)/shard_map/ppermute | solution.py:60
  1.8 0.0 copy-start.3
  1.8 0.0 copy-start
  1.8 2.4 %difference.1.own = bf16[1040,512]{1,0:T(8,128)(2,1)S(1)} custom-call(f32[1024,512]{1,0:T(8,128)} %bitcast.8, f32[1024,512]{1,0:T(8,128)} %bitcast.13, s32[1,1]{1,0:T(1,128)} %bitcast.7.steps), custom_call_target="tpu_custom_call" | custom-call | flops 1048576 | bytes 5242880 | tf_op jit(solution)/shard_map/difference/pallas_call | solution.py:102
  4.3 2.6 %collective-permute-start.13 = (bf16[1040,512]{1,0:T(8,128)(2,1)S(1)}, bf16[1040,512]{1,0:T(8,128)(2,1)S(1)}, u32[]{:S(2)}, u32[]{:S(2)}) collective-permute-start(bf16[1040,512]{1,0:T(8,128)(2,1)S(1)} %difference.1.own), channel_id=1, source_target_pairs={{0,16},{16,0},{1,17},{17,1},{2,18},{18,2},{3,19},{19,3},{4,20},{20... | collective-permute-start | bytes 3194888 | tf_op jit(solution)/shard_map/ppermute | solution.py:64
  6.8 0.0 copy-done.3
  6.8 1.6 %collective-permute-start.2 = (bf16[128,512]{1,0:T(8,128)(2,1)S(1)}, bf16[128,512]{1,0:T(8,128)(2,1)S(1)}, u32[]{:S(2)}, u32[]{:S(2)}) collective-permute-start(bf16[128,512]{1,0:T(8,128)(2,1)S(1)} %get-tuple-element.52), channel_id=1, source_target_pairs={{0,2},{1,3},{4,0},{5,1},{8,4},{9,5},{12,8},{13,9},{14,12},{15,13},... | collective-permute-start | bytes 393224 | tf_op jit(solution)/shard_map/ppermute | solution.py:47
  8.4 0.5 %collective-permute-start = (bf16[128,512]{1,0:T(8,128)(2,1)S(1)}, bf16[128,512]{1,0:T(8,128)(2,1)S(1)}, u32[]{:S(2)}, u32[]{:S(2)}) collective-permute-start(bf16[128,512]{1,0:T(8,128)(2,1)S(1)} %get-tuple-element.52), channel_id=1, source_target_pairs={{0,4},{1,5},{4,8},{5,9},{8,12},{9,13},{12,14},{13,15},{14,10},{15,... | collective-permute-start | bytes 393224 | tf_op jit(solution)/shard_map/ppermute | solution.py:47
  8.9 0.0 collective-permute-done.4.sib
  8.9 1.5 %collective-permute-start.6 = (bf16[128,512]{1,0:T(8,128)(2,1)S(1)}, bf16[128,512]{1,0:T(8,128)(2,1)S(1)}, u32[]{:S(2)}, u32[]{:S(2)}) collective-permute-start(bf16[128,512]{1,0:T(8,128)(2,1)S(1)} %get-tuple-element.28), channel_id=1, source_target_pairs={{0,2},{1,3},{4,0},{5,1},{8,4},{9,5},{12,8},{13,9},{14,12},{15,13},... | collective-permute-start | bytes 393224 | tf_op jit(solution)/shard_map/ppermute | solution.py:47
  10.5 0.5 %collective-permute-start.5 = (bf16[128,512]{1,0:T(8,128)(2,1)S(1)}, bf16[128,512]{1,0:T(8,128)(2,1)S(1)}, u32[]{:S(2)}, u32[]{:S(2)}) collective-permute-start(bf16[128,512]{1,0:T(8,128)(2,1)S(1)} %get-tuple-element.28), channel_id=1, source_target_pairs={{0,4},{1,5},{4,8},{5,9},{8,12},{9,13},{12,14},{13,15},{14,10},{15,... | collective-permute-start | bytes 393224 | tf_op jit(solution)/shard_map/ppermute | solution.py:47
  11.0 2.3 %collective-permute-done.2.refs_3_ = bf16[128,512]{1,0:T(8,128)(2,1)S(1)} collective-permute-done((bf16[128,512]{1,0:T(8,128)(2,1)S(1)}, bf16[128,512]{1,0:T(8,128)(2,1)S(1)}, u32[]{:S(2)}, u32[]{:S(2)}) %collective-permute-start.2) | collective-permute-done | bytes 131104 | tf_op jit(solution)/shard_map/ppermute | solution.py:47
  13.2 1.5 %collective-permute-start.3 = (bf16[128,512]{1,0:T(8,128)(2,1)S(1)}, bf16[128,512]{1,0:T(8,128)(2,1)S(1)}, u32[]{:S(2)}, u32[]{:S(2)}) collective-permute-start(bf16[128,512]{1,0:T(8,128)(2,1)S(1)} %collective-permute-done.2.refs_3_), channel_id=1, source_target_pairs={{0,2},{1,3},{4,0},{5,1},{8,4},{9,5},{12,8},{13,9},{14,12},{15,13},... | collective-permute-start | bytes 393224 | tf_op jit(solution)/shard_map/ppermute | solution.py:47
  14.8 0.0 collective-permute-done.refs_1_
  14.8 0.5 %collective-permute-start.1 = (bf16[128,512]{1,0:T(8,128)(2,1)S(1)}, bf16[128,512]{1,0:T(8,128)(2,1)S(1)}, u32[]{:S(2)}, u32[]{:S(2)}) collective-permute-start(bf16[128,512]{1,0:T(8,128)(2,1)S(1)} %collective-permute-done.refs_1_), channel_id=1, source_target_pairs={{0,4},{1,5},{4,8},{5,9},{8,12},{9,13},{12,14},{13,15},{14,10},{15,... | collective-permute-start | bytes 393224 | tf_op jit(solution)/shard_map/ppermute | solution.py:47
  15.3 0.7 %collective-permute-done.6.refs_4_ = bf16[128,512]{1,0:T(8,128)(2,1)S(1)} collective-permute-done((bf16[128,512]{1,0:T(8,128)(2,1)S(1)}, bf16[128,512]{1,0:T(8,128)(2,1)S(1)}, u32[]{:S(2)}, u32[]{:S(2)}) %collective-permute-start.6) | collective-permute-done | bytes 131104 | tf_op jit(solution)/shard_map/ppermute | solution.py:47
  16.0 1.5 %collective-permute-start.8 = (bf16[128,512]{1,0:T(8,128)(2,1)S(1)}, bf16[128,512]{1,0:T(8,128)(2,1)S(1)}, u32[]{:S(2)}, u32[]{:S(2)}) collective-permute-start(bf16[128,512]{1,0:T(8,128)(2,1)S(1)} %collective-permute-done.6.refs_4_), channel_id=1, source_target_pairs={{0,2},{1,3},{4,0},{5,1},{8,4},{9,5},{12,8},{13,9},{14,12},{15,13},... | collective-permute-start | bytes 393224 | tf_op jit(solution)/shard_map/ppermute | solution.py:47
  17.6 0.0 collective-permute-done.5.refs_2_
  17.6 0.5 %collective-permute-start.10 = (bf16[128,512]{1,0:T(8,128)(2,1)S(1)}, bf16[128,512]{1,0:T(8,128)(2,1)S(1)}, u32[]{:S(2)}, u32[]{:S(2)}) collective-permute-start(bf16[128,512]{1,0:T(8,128)(2,1)S(1)} %collective-permute-done.5.refs_2_), channel_id=1, source_target_pairs={{0,4},{1,5},{4,8},{5,9},{8,12},{9,13},{12,14},{13,15},{14,10},{15,... | collective-permute-start | bytes 393224 | tf_op jit(solution)/shard_map/ppermute | solution.py:47
  18.1 0.0 copy-done
  18.1 0.6 %partial_keys.3 = (f32[256,512]{1,0:T(8,128)S(1)}, f32[256,512]{1,0:T(8,128)S(1)}) custom-call(bf16[256,4096]{1,0:T(8,128)(2,1)S(1)} %copy-done, bf16[256,4096]{1,0:T(8,128)(2,1)S(1)} %collective-permute-done.4.sib, bf16[256,512]{1,0:T(8,128)(2,1)S(1)} %bitcast.12, bf16[128,512]{1,0:T(8,128)(2,1)S(1)} %collective-permute-done.refs_1_, ...), custom_call_target="tpu_custom_call" | custom-call | tf_op jit(solution)/shard_map/partial_keys/pallas_call | solution.py:196
  18.7 0.5 %collective-permute-done.3.refs_2_ = bf16[128,512]{1,0:T(8,128)(2,1)S(1)} collective-permute-done((bf16[128,512]{1,0:T(8,128)(2,1)S(1)}, bf16[128,512]{1,0:T(8,128)(2,1)S(1)}, u32[]{:S(2)}, u32[]{:S(2)}) %collective-permute-start.3) | collective-permute-done | bytes 131104 | tf_op jit(solution)/shard_map/ppermute | solution.py:47
  19.1 1.8 %collective-permute-done.1.refs_0_ = bf16[128,512]{1,0:T(8,128)(2,1)S(1)} collective-permute-done((bf16[128,512]{1,0:T(8,128)(2,1)S(1)}, bf16[128,512]{1,0:T(8,128)(2,1)S(1)}, u32[]{:S(2)}, u32[]{:S(2)}) %collective-permute-start.1) | collective-permute-done | bytes 131104 | tf_op jit(solution)/shard_map/ppermute | solution.py:47
  20.9 0.5 %collective-permute-start.7 = (bf16[128,512]{1,0:T(8,128)(2,1)S(1)}, bf16[128,512]{1,0:T(8,128)(2,1)S(1)}, u32[]{:S(2)}, u32[]{:S(2)}) collective-permute-start(bf16[128,512]{1,0:T(8,128)(2,1)S(1)} %collective-permute-done.1.refs_0_), channel_id=1, source_target_pairs={{0,4},{1,5},{4,8},{5,9},{8,12},{9,13},{12,14},{13,15},{14,10},{15,... | collective-permute-start | bytes 393224 | tf_op jit(solution)/shard_map/ppermute | solution.py:47
  21.5 0.0 collective-permute-done.8.refs_3_
  21.5 1.5 %collective-permute-start.9 = (bf16[128,512]{1,0:T(8,128)(2,1)S(1)}, bf16[128,512]{1,0:T(8,128)(2,1)S(1)}, u32[]{:S(2)}, u32[]{:S(2)}) collective-permute-start(bf16[128,512]{1,0:T(8,128)(2,1)S(1)} %collective-permute-done.8.refs_3_), channel_id=1, source_target_pairs={{0,2},{1,3},{4,0},{5,1},{8,4},{9,5},{12,8},{13,9},{14,12},{15,13},... | collective-permute-start | bytes 393224 | tf_op jit(solution)/shard_map/ppermute | solution.py:47
  23.0 1.6 %collective-permute-start.15 = (bf16[128,512]{1,0:T(8,128)(2,1)S(1)}, bf16[128,512]{1,0:T(8,128)(2,1)S(1)}, u32[]{:S(2)}, u32[]{:S(2)}) collective-permute-start(bf16[128,512]{1,0:T(8,128)(2,1)S(1)} %collective-permute-done.3.refs_2_), channel_id=1, source_target_pairs={{0,2},{1,3},{4,0},{5,1},{8,4},{9,5},{12,8},{13,9},{14,12},{15,13},... | collective-permute-start | bytes 393224 | tf_op jit(solution)/shard_map/ppermute | solution.py:47
  24.6 0.0 collective-permute-done.10.refs_1_
  24.6 0.5 %collective-permute-start.14 = (bf16[128,512]{1,0:T(8,128)(2,1)S(1)}, bf16[128,512]{1,0:T(8,128)(2,1)S(1)}, u32[]{:S(2)}, u32[]{:S(2)}) collective-permute-start(bf16[128,512]{1,0:T(8,128)(2,1)S(1)} %collective-permute-done.10.refs_1_), channel_id=1, source_target_pairs={{0,4},{1,5},{4,8},{5,9},{8,12},{9,13},{12,14},{13,15},{14,10},{15,... | collective-permute-start | bytes 393224 | tf_op jit(solution)/shard_map/ppermute | solution.py:47
  25.0 0.4 %partial_keys.4 = (f32[256,512]{1,0:T(8,128)S(1)}, f32[256,512]{1,0:T(8,128)S(1)}) custom-call(bf16[256,4096]{1,0:T(8,128)(2,1)S(1)} %copy-done, bf16[256,4096]{1,0:T(8,128)(2,1)S(1)} %collective-permute-done.4.sib, bf16[128,512]{1,0:T(8,128)(2,1)S(1)} %collective-permute-done.1.refs_0_, bf16[128,512]{1,0:T(8,128)(2,1)S(1)} %collective-permute-done.10.refs_1_, ...), custom_call_target="tpu_custom_call" | custom-call | tf_op jit(solution)/shard_map/partial_keys/pallas_call | solution.py:196
  25.4 1.6 %collective-permute-done.7.refs_0_ = bf16[128,512]{1,0:T(8,128)(2,1)S(1)} collective-permute-done((bf16[128,512]{1,0:T(8,128)(2,1)S(1)}, bf16[128,512]{1,0:T(8,128)(2,1)S(1)}, u32[]{:S(2)}, u32[]{:S(2)}) %collective-permute-start.7) | collective-permute-done | bytes 131104 | tf_op jit(solution)/shard_map/ppermute | solution.py:47
  27.1 0.0 collective-permute-done.9.refs_3_
  27.1 0.0 copy-start.1
  27.1 0.0 copy-start.2
  27.1 1.0 %collective-permute-start.11 = (bf16[128,512]{1,0:T(8,128)(2,1)S(1)}, bf16[128,512]{1,0:T(8,128)(2,1)S(1)}, u32[]{:S(2)}, u32[]{:S(2)}) collective-permute-start(bf16[128,512]{1,0:T(8,128)(2,1)S(1)} %collective-permute-done.7.refs_0_), channel_id=1, source_target_pairs={{0,4},{1,5},{4,8},{5,9},{8,12},{9,13},{12,14},{13,15},{14,10},{15,... | collective-permute-start | bytes 393224 | tf_op jit(solution)/shard_map/ppermute | solution.py:47
  28.1 1.0 %collective-permute-start.12 = (bf16[128,512]{1,0:T(8,128)(2,1)S(1)}, bf16[128,512]{1,0:T(8,128)(2,1)S(1)}, u32[]{:S(2)}, u32[]{:S(2)}) collective-permute-start(bf16[128,512]{1,0:T(8,128)(2,1)S(1)} %collective-permute-done.9.refs_3_), channel_id=1, source_target_pairs={{0,2},{1,3},{4,0},{5,1},{8,4},{9,5},{12,8},{13,9},{14,12},{15,13},... | collective-permute-start | bytes 393224 | tf_op jit(solution)/shard_map/ppermute | solution.py:47
  29.1 0.0 collective-permute-done.15.refs_2_
  29.1 1.0 %collective-permute-done.14.refs_1_ = bf16[128,512]{1,0:T(8,128)(2,1)S(1)} collective-permute-done((bf16[128,512]{1,0:T(8,128)(2,1)S(1)}, bf16[128,512]{1,0:T(8,128)(2,1)S(1)}, u32[]{:S(2)}, u32[]{:S(2)}) %collective-permute-start.14) | collective-permute-done | bytes 131104 | tf_op jit(solution)/shard_map/ppermute | solution.py:47
  30.1 0.4 %partial_keys.5 = (f32[256,512]{1,0:T(8,128)S(1)}, bf16[256,512]{1,0:T(8,128)(2,1)S(1)}) custom-call(bf16[256,4096]{1,0:T(8,128)(2,1)S(1)} %copy-done, bf16[256,4096]{1,0:T(8,128)(2,1)S(1)} %collective-permute-done.4.sib, bf16[128,512]{1,0:T(8,128)(2,1)S(1)} %collective-permute-done.7.refs_0_, bf16[128,512]{1,0:T(8,128)(2,1)S(1)} %collective-permute-done.14.refs_1_, ...), custom_call_target="tpu_custom_call" | custom-call | tf_op jit(solution)/shard_map/partial_keys/pallas_call | solution.py:196
  30.6 0.1 collective-permute-start.18
  30.6 0.4 collective-permute-done.13.got
  31.0 0.0 copy-done.1
  31.0 0.0 copy-done.2
  31.0 2.2 %outer_step.1 = (f32[1024,512]{1,0:T(8,128)}, f32[1024,512]{1,0:T(8,128)}) custom-call(f32[1024,512]{1,0:T(8,128)S(1)} %bitcast.9, f32[1024,512]{1,0:T(8,128)S(1)} %bitcast.10, bf16[1040,512]{1,0:T(8,128)(2,1)S(1)} %difference.1.own, bf16[1040,512]{1,0:T(8,128)(2,1)S(1)} %collective-permute-done.13.got), custom_call_target="tpu_custom_call" | custom-call | flops 5242880 | bytes 10485760 | tf_op jit(solution)/shard_map/outer_step/pallas_call | solution.py:142
  33.3 0.0 collective-permute-done.11.wa
  33.3 0.0 collective-permute-done.12.wb
  33.3 0.2 collective-permute-start.16
  33.5 0.4 collective-permute-start.17
  33.9 0.0 collective-permute-done.18.got
  33.9 0.8 %collective-permute-done.16.va = bf16[128,512]{1,0:T(8,128)(2,1)S(1)} collective-permute-done((bf16[128,512]{1,0:T(8,128)(2,1)S(1)}, bf16[128,512]{1,0:T(8,128)(2,1)S(1)}, u32[]{:S(2)}, u32[]{:S(2)}) %collective-permute-start.16) | collective-permute-done | bytes 131104 | tf_op jit(solution)/shard_map/ppermute | solution.py:60
  34.7 0.2 collective-permute-done.17.vb
  34.9 1.0 %finish_keys.1 = bf16[256,512]{1,0:T(8,128)(2,1)} custom-call(bf16[256,4096]{1,0:T(8,128)(2,1)S(1)} %copy-done, bf16[128,512]{1,0:T(8,128)(2,1)S(1)} %collective-permute-done.11.wa, bf16[128,512]{1,0:T(8,128)(2,1)S(1)} %collective-permute-done.12.wb, bf16[128,512]{1,0:T(8,128)(2,1)S(1)} %collective-permute-done.16.va, ...), custom_call_target="tpu_custom_call" | custom-call | tf_op jit(solution)/shard_map/finish_keys/pallas_call | solution.py:219
  (1 shorter events, 0.0 us)
Async XLA Ops:
  0.6 8.3 %collective-permute-start.4 = (bf16[256,4096]{1,0:T(8,128)(2,1)}, bf16[256,4096]{1,0:T(8,128)(2,1)S(1)}, u32[]{:S(2)}, u32[]{:S(2)}) collective-permute-start(bf16[256,4096]{1,0:T(8,128)(2,1)} %act.7), channel_id=1, source_target_pairs={{0,1},{1,0},{2,3},{3,2},{4,5},{5,4},{6,7},{7,6},{8,9},{9,8},{10,11... | collective-permute-start | bytes 6291464 | tf_op jit(solution)/shard_map/ppermute | solution.py:60
  1.8 5.0 %copy-start.3 = (bf16[1,256,512]{2,1,0:T(8,128)(2,1)S(1)}, bf16[1,256,512]{2,1,0:T(8,128)(2,1)}, u32[]{:S(2)}) copy-start(bf16[1,256,512]{2,1,0:T(8,128)(2,1)} %param.7) | copy-start | bytes 786436
  1.8 16.3 %copy-start = (bf16[256,4096]{1,0:T(8,128)(2,1)S(1)}, bf16[256,4096]{1,0:T(8,128)(2,1)}, u32[]{:S(2)}) copy-start(bf16[256,4096]{1,0:T(8,128)(2,1)} %act.7) | copy-start | bytes 6291460
  4.3 26.7 %collective-permute-start.13 = (bf16[1040,512]{1,0:T(8,128)(2,1)S(1)}, bf16[1040,512]{1,0:T(8,128)(2,1)S(1)}, u32[]{:S(2)}, u32[]{:S(2)}) collective-permute-start(bf16[1040,512]{1,0:T(8,128)(2,1)S(1)} %difference.1.own), channel_id=1, source_target_pairs={{0,16},{16,0},{1,17},{17,1},{2,18},{18,2},{3,19},{19,3},{4,20},{20... | collective-permute-start | bytes 3194888 | tf_op jit(solution)/shard_map/ppermute | solution.py:64
  6.8 6.4 %collective-permute-start.2 = (bf16[128,512]{1,0:T(8,128)(2,1)S(1)}, bf16[128,512]{1,0:T(8,128)(2,1)S(1)}, u32[]{:S(2)}, u32[]{:S(2)}) collective-permute-start(bf16[128,512]{1,0:T(8,128)(2,1)S(1)} %get-tuple-element.52), channel_id=1, source_target_pairs={{0,2},{1,3},{4,0},{5,1},{8,4},{9,5},{12,8},{13,9},{14,12},{15,13},... | collective-permute-start | bytes 393224 | tf_op jit(solution)/shard_map/ppermute | solution.py:47
  8.4 6.4 %collective-permute-start = (bf16[128,512]{1,0:T(8,128)(2,1)S(1)}, bf16[128,512]{1,0:T(8,128)(2,1)S(1)}, u32[]{:S(2)}, u32[]{:S(2)}) collective-permute-start(bf16[128,512]{1,0:T(8,128)(2,1)S(1)} %get-tuple-element.52), channel_id=1, source_target_pairs={{0,4},{1,5},{4,8},{5,9},{8,12},{9,13},{12,14},{13,15},{14,10},{15,... | collective-permute-start | bytes 393224 | tf_op jit(solution)/shard_map/ppermute | solution.py:47
  8.9 7.1 %collective-permute-start.6 = (bf16[128,512]{1,0:T(8,128)(2,1)S(1)}, bf16[128,512]{1,0:T(8,128)(2,1)S(1)}, u32[]{:S(2)}, u32[]{:S(2)}) collective-permute-start(bf16[128,512]{1,0:T(8,128)(2,1)S(1)} %get-tuple-element.28), channel_id=1, source_target_pairs={{0,2},{1,3},{4,0},{5,1},{8,4},{9,5},{12,8},{13,9},{14,12},{15,13},... | collective-permute-start | bytes 393224 | tf_op jit(solution)/shard_map/ppermute | solution.py:47
  10.5 7.1 %collective-permute-start.5 = (bf16[128,512]{1,0:T(8,128)(2,1)S(1)}, bf16[128,512]{1,0:T(8,128)(2,1)S(1)}, u32[]{:S(2)}, u32[]{:S(2)}) collective-permute-start(bf16[128,512]{1,0:T(8,128)(2,1)S(1)} %get-tuple-element.28), channel_id=1, source_target_pairs={{0,4},{1,5},{4,8},{5,9},{8,12},{9,13},{12,14},{13,15},{14,10},{15,... | collective-permute-start | bytes 393224 | tf_op jit(solution)/shard_map/ppermute | solution.py:47
  13.2 5.9 %collective-permute-start.3 = (bf16[128,512]{1,0:T(8,128)(2,1)S(1)}, bf16[128,512]{1,0:T(8,128)(2,1)S(1)}, u32[]{:S(2)}, u32[]{:S(2)}) collective-permute-start(bf16[128,512]{1,0:T(8,128)(2,1)S(1)} %collective-permute-done.2.refs_3_), channel_id=1, source_target_pairs={{0,2},{1,3},{4,0},{5,1},{8,4},{9,5},{12,8},{13,9},{14,12},{15,13},... | collective-permute-start | bytes 393224 | tf_op jit(solution)/shard_map/ppermute | solution.py:47
  14.8 6.2 %collective-permute-start.1 = (bf16[128,512]{1,0:T(8,128)(2,1)S(1)}, bf16[128,512]{1,0:T(8,128)(2,1)S(1)}, u32[]{:S(2)}, u32[]{:S(2)}) collective-permute-start(bf16[128,512]{1,0:T(8,128)(2,1)S(1)} %collective-permute-done.refs_1_), channel_id=1, source_target_pairs={{0,4},{1,5},{4,8},{5,9},{8,12},{9,13},{12,14},{13,15},{14,10},{15,... | collective-permute-start | bytes 393224 | tf_op jit(solution)/shard_map/ppermute | solution.py:47
  16.0 5.4 %collective-permute-start.8 = (bf16[128,512]{1,0:T(8,128)(2,1)S(1)}, bf16[128,512]{1,0:T(8,128)(2,1)S(1)}, u32[]{:S(2)}, u32[]{:S(2)}) collective-permute-start(bf16[128,512]{1,0:T(8,128)(2,1)S(1)} %collective-permute-done.6.refs_4_), channel_id=1, source_target_pairs={{0,2},{1,3},{4,0},{5,1},{8,4},{9,5},{12,8},{13,9},{14,12},{15,13},... | collective-permute-start | bytes 393224 | tf_op jit(solution)/shard_map/ppermute | solution.py:47
  17.6 7.0 %collective-permute-start.10 = (bf16[128,512]{1,0:T(8,128)(2,1)S(1)}, bf16[128,512]{1,0:T(8,128)(2,1)S(1)}, u32[]{:S(2)}, u32[]{:S(2)}) collective-permute-start(bf16[128,512]{1,0:T(8,128)(2,1)S(1)} %collective-permute-done.5.refs_2_), channel_id=1, source_target_pairs={{0,4},{1,5},{4,8},{5,9},{8,12},{9,13},{12,14},{13,15},{14,10},{15,... | collective-permute-start | bytes 393224 | tf_op jit(solution)/shard_map/ppermute | solution.py:47
  20.9 6.1 %collective-permute-start.7 = (bf16[128,512]{1,0:T(8,128)(2,1)S(1)}, bf16[128,512]{1,0:T(8,128)(2,1)S(1)}, u32[]{:S(2)}, u32[]{:S(2)}) collective-permute-start(bf16[128,512]{1,0:T(8,128)(2,1)S(1)} %collective-permute-done.1.refs_0_), channel_id=1, source_target_pairs={{0,4},{1,5},{4,8},{5,9},{8,12},{9,13},{12,14},{13,15},{14,10},{15,... | collective-permute-start | bytes 393224 | tf_op jit(solution)/shard_map/ppermute | solution.py:47
  21.5 5.6 %collective-permute-start.9 = (bf16[128,512]{1,0:T(8,128)(2,1)S(1)}, bf16[128,512]{1,0:T(8,128)(2,1)S(1)}, u32[]{:S(2)}, u32[]{:S(2)}) collective-permute-start(bf16[128,512]{1,0:T(8,128)(2,1)S(1)} %collective-permute-done.8.refs_3_), channel_id=1, source_target_pairs={{0,2},{1,3},{4,0},{5,1},{8,4},{9,5},{12,8},{13,9},{14,12},{15,13},... | collective-permute-start | bytes 393224 | tf_op jit(solution)/shard_map/ppermute | solution.py:47
  23.0 6.2 %collective-permute-start.15 = (bf16[128,512]{1,0:T(8,128)(2,1)S(1)}, bf16[128,512]{1,0:T(8,128)(2,1)S(1)}, u32[]{:S(2)}, u32[]{:S(2)}) collective-permute-start(bf16[128,512]{1,0:T(8,128)(2,1)S(1)} %collective-permute-done.3.refs_2_), channel_id=1, source_target_pairs={{0,2},{1,3},{4,0},{5,1},{8,4},{9,5},{12,8},{13,9},{14,12},{15,13},... | collective-permute-start | bytes 393224 | tf_op jit(solution)/shard_map/ppermute | solution.py:47
  24.6 5.6 %collective-permute-start.14 = (bf16[128,512]{1,0:T(8,128)(2,1)S(1)}, bf16[128,512]{1,0:T(8,128)(2,1)S(1)}, u32[]{:S(2)}, u32[]{:S(2)}) collective-permute-start(bf16[128,512]{1,0:T(8,128)(2,1)S(1)} %collective-permute-done.10.refs_1_), channel_id=1, source_target_pairs={{0,4},{1,5},{4,8},{5,9},{8,12},{9,13},{12,14},{13,15},{14,10},{15,... | collective-permute-start | bytes 393224 | tf_op jit(solution)/shard_map/ppermute | solution.py:47
  27.1 3.9 %copy-start.1 = (f32[2,2,256,512]{3,2,1,0:T(8,128)S(1)}, f32[2,2,256,512]{3,2,1,0:T(8,128)}, u32[]{:S(2)}) copy-start(f32[2,2,256,512]{3,2,1,0:T(8,128)} %param.9) | copy-start | bytes 6291460
  27.1 3.9 %copy-start.2 = (f32[2,2,256,512]{3,2,1,0:T(8,128)S(1)}, f32[2,2,256,512]{3,2,1,0:T(8,128)}, u32[]{:S(2)}) copy-start(f32[2,2,256,512]{3,2,1,0:T(8,128)} %param.10) | copy-start | bytes 6291460
  27.1 6.2 %collective-permute-start.11 = (bf16[128,512]{1,0:T(8,128)(2,1)S(1)}, bf16[128,512]{1,0:T(8,128)(2,1)S(1)}, u32[]{:S(2)}, u32[]{:S(2)}) collective-permute-start(bf16[128,512]{1,0:T(8,128)(2,1)S(1)} %collective-permute-done.7.refs_0_), channel_id=1, source_target_pairs={{0,4},{1,5},{4,8},{5,9},{8,12},{9,13},{12,14},{13,15},{14,10},{15,... | collective-permute-start | bytes 393224 | tf_op jit(solution)/shard_map/ppermute | solution.py:47
  28.1 5.2 %collective-permute-start.12 = (bf16[128,512]{1,0:T(8,128)(2,1)S(1)}, bf16[128,512]{1,0:T(8,128)(2,1)S(1)}, u32[]{:S(2)}, u32[]{:S(2)}) collective-permute-start(bf16[128,512]{1,0:T(8,128)(2,1)S(1)} %collective-permute-done.9.refs_3_), channel_id=1, source_target_pairs={{0,2},{1,3},{4,0},{5,1},{8,4},{9,5},{12,8},{13,9},{14,12},{15,13},... | collective-permute-start | bytes 393224 | tf_op jit(solution)/shard_map/ppermute | solution.py:47
  30.6 3.3 %collective-permute-start.18 = (bf16[256,512]{1,0:T(8,128)(2,1)S(1)}, bf16[256,512]{1,0:T(8,128)(2,1)S(1)}, u32[]{:S(2)}, u32[]{:S(2)}) collective-permute-start(bf16[256,512]{1,0:T(8,128)(2,1)S(1)} %get-tuple-element.48), channel_id=1, source_target_pairs={{0,1},{1,0},{2,3},{3,2},{4,5},{5,4},{6,7},{7,6},{8,9},{9,8},{10,11... | collective-permute-start | bytes 786440 | tf_op jit(solution)/shard_map/ppermute | solution.py:60
  33.3 1.4 %collective-permute-start.16 = (bf16[128,512]{1,0:T(8,128)(2,1)S(1)}, bf16[128,512]{1,0:T(8,128)(2,1)S(1)}, u32[]{:S(2)}, u32[]{:S(2)}) collective-permute-start(bf16[128,512]{1,0:T(8,128)(2,1)S(1)} %collective-permute-done.11.wa), channel_id=1, source_target_pairs={{0,1},{1,0},{2,3},{3,2},{4,5},{5,4},{6,7},{7,6},{8,9},{9,8},{10,11... | collective-permute-start | bytes 393224 | tf_op jit(solution)/shard_map/ppermute | solution.py:60
  33.5 1.4 %collective-permute-start.17 = (bf16[128,512]{1,0:T(8,128)(2,1)S(1)}, bf16[128,512]{1,0:T(8,128)(2,1)S(1)}, u32[]{:S(2)}, u32[]{:S(2)}) collective-permute-start(bf16[128,512]{1,0:T(8,128)(2,1)S(1)} %collective-permute-done.12.wb), channel_id=1, source_target_pairs={{0,1},{1,0},{2,3},{3,2},{4,5},{5,4},{6,7},{7,6},{8,9},{9,8},{10,11... | collective-permute-start | bytes 393224 | tf_op jit(solution)/shard_map/ppermute | solution.py:60

commit v3 on v0

v3 whole, which is shorter than its diff:
```python
import functools

import jax
import jax.numpy as jnp
from jax import lax
from jax.experimental import pallas as pl
from jax.experimental.pallas import tpu as pltpu
from jax.sharding import PartitionSpec as P

F32, BF16 = jnp.float32, jnp.bfloat16
MIB = 1024 * 1024
HBM = pl.BlockSpec(memory_space=pltpu.HBM)
ANY = pl.BlockSpec(memory_space=pl.ANY)
VMEM = pl.BlockSpec(memory_space=pltpu.VMEM)


def nesterov(average, momentum, base_params):
    new_momentum = 0.9 * momentum + average
    new_base = base_params - 0.7 * (average + 0.9 * new_momentum)
    return (new_base, new_momentum)


def general(activations, inner_weight, local_params, base_params, momentum, inner_steps):
    counts = lax.all_gather(inner_steps, "replica", axis=0, tiled=True)
    total = jnp.sum(counts.astype(F32))
    own = inner_steps[0].astype(F32)
    difference = (base_params - local_params[0]).astype(BF16)
    average = lax.psum(own * difference.astype(F32), "replica") / total
    new_base, new_momentum = nesterov(average, momentum, base_params)
    weight = lax.all_gather(inner_weight[0], "fsdp", axis=0, tiled=True)
    keys = jnp.dot(activations, weight, preferred_element_type=F32).astype(BF16)
    return (keys, new_base, new_momentum)


def index(z, y, c):
    return (z * 2 + y) * 2 + c


def place(p):
    p = p % 8
    return (p, 0) if p < 4 else (7 - p, 1)


def cycle(x):
    pairs = [
        (index(*place(p), c), index(*place(p + 1 - 2 * c), c)) for p in range(8) for c in range(2)
    ]
    return lax.ppermute(x, "fsdp", pairs)


def send_core(x):
    pairs = [(i, i ^ 1) for i in range(16)]
    return lax.ppermute(x, "fsdp", pairs)


def send_x(x):
    return lax.ppermute(x, "replica", [(0, 1), (1, 0)])


def tie(*xs):
    return lax.optimization_barrier(xs)


def cost(flops, bytes_accessed):
    return pl.CostEstimate(flops=int(flops), bytes_accessed=int(bytes_accessed), transcendentals=0)


def params(limit=16):
    return pltpu.CompilerParams(vmem_limit_bytes=limit * MIB)


def difference_kernel(at, sizes, pieces, base, local, *refs):
    held, sems = refs[-2:]
    outs = refs[-2 - len(sizes):-2]
    rows = held.shape[1]
    piece = rows // pieces
    copies = []
    for j in range(pieces):
        for i, ref in enumerate((base, local)):
            part = pl.ds(j * piece, piece)
            copies.append(
                pltpu.make_async_copy(ref.at[pl.ds(at + j * piece, piece), :], held.at[i, part, :], sems.at[i, j])
            )
    for copy in copies:
        copy.start()
    extra = outs[0].shape[0] - sizes[0]
    if extra:
        count = jnp.broadcast_to(refs[0][...].astype(F32), (extra, outs[0].shape[1]))
        outs[0][pl.ds(sizes[0], extra), :] = count.astype(BF16)
    which, put = 0, 0
    for j in range(pieces):
        copies[2 * j].wait()
        copies[2 * j + 1].wait()
        part = pl.ds(j * piece, piece)
        outs[which][pl.ds(put, piece), :] = (held[0, part, :] - held[1, part, :]).astype(BF16)
        put += piece
        if put == sizes[which]:
            which, put = which + 1, 0


def difference(base, local, at, sizes, pieces, steps=()):
    width = base.shape[1]
    rows = sum(sizes)
    shapes = [jax.ShapeDtypeStruct((n, width), BF16) for n in sizes]
    if steps:
        shapes[0] = jax.ShapeDtypeStruct((sizes[0] + 16, width), BF16)
    return pl.pallas_call(
        functools.partial(difference_kernel, at, tuple(sizes), pieces),
        out_shape=tuple(shapes),
        in_specs=[HBM, HBM] + [VMEM] * len(steps),
        out_specs=(VMEM,) * len(sizes),
        scratch_shapes=[pltpu.VMEM((2, rows, width), F32), pltpu.SemaphoreType.DMA((2, pieces))],
        compiler_params=params(52),
        cost_estimate=cost(2 * rows * width, 10 * rows * width),
        name="difference",
    )(base, local, *steps)


def outer_kernel(base, mom, own, got, mine, theirs, *refs):
    new_base, new_mom = refs[-2:]
    mine = mine[...][0:1, :].astype(F32)
    theirs = theirs[...][0:1, :].astype(F32)
    scale = 1.0 / (mine + theirs)
    average = (mine * scale) * own[...].astype(F32) + (theirs * scale) * got[...].astype(F32)
    momentum = 0.9 * mom[...] + average
    new_mom[...] = momentum
    new_base[...] = base[...] - 0.7 * (average + 0.9 * momentum)


def outer(base, mom, own, got, mine, theirs, at, rows, block, state):
    width = own.shape[1]
    big = pl.BlockSpec((pl.Element(block), pl.Element(width)), lambda i: (pl.multiple_of(at + i * block, 16), 0))
    small = pl.BlockSpec((block, width), lambda i: (i, 0))
    counts = mine.shape[0] // 16 - 1
    steps = pl.BlockSpec((16, width), lambda i: (counts, 0))
    shape = jax.ShapeDtypeStruct(base.shape, F32)
    return pl.pallas_call(
        outer_kernel,
        out_shape=(shape, shape),
        grid=(rows // block,),
        in_specs=[big, big, small, small, steps, steps] + [ANY] * len(state),
        out_specs=(big, big),
        input_output_aliases={6 + i: i for i in range(len(state))},
        compiler_params=params(),
        cost_estimate=cost(10 * rows * width, 20 * rows * width),
        name="outer_step",
    )(base, mom, own, got, mine, theirs, *state)


def dot(a, b):
    return jnp.dot(a, b, preferred_element_type=F32)


def column(back, mine, depth):
    f = lax.axis_index("fsdp")
    z, y, c = f // 4, (f // 2) % 2, f % 2
    p = (z + y * (7 - 2 * z) - back * (1 - 2 * c) + 8) % 8
    far = p // 4
    z, y = p + far * (7 - 2 * p), far
    c = c if mine else 1 - c
    return pl.multiple_of(index(z, y, c) * depth, depth)


def partial_kernel(blocks, first, act, sib, *refs):
    refs, (own_out, sib_out) = refs[:-2], refs[-2:]
    weights, state = (refs, None) if first else (refs[:-2], refs[-2:])
    depth = act.shape[1] // 16
    own = None if first else state[0][...]
    theirs = None if first else state[1][...]
    for (back, mine), ref in zip(blocks, weights):
        w = ref[...]
        columns = pl.ds(column(back, mine, depth), depth)
        a, b = dot(act[:, columns], w), dot(sib[:, columns], w)
        own = a if own is None else own + a
        theirs = b if theirs is None else theirs + b
    own_out[...] = own
    sib_out[...] = theirs.astype(sib_out.dtype)


def partial_sums(blocks, act, sib, weights, state, kind=F32):
    tokens = act.shape[0]
    width = weights[0].shape[1]
    out = jax.ShapeDtypeStruct((tokens, width), F32)
    return pl.pallas_call(
        functools.partial(partial_kernel, blocks, not state),
        out_shape=(out, jax.ShapeDtypeStruct((tokens, width), kind)),
        in_specs=[VMEM] * (2 + len(weights) + len(state)),
        out_specs=(VMEM, VMEM),
        compiler_params=params(),
        cost_estimate=cost(0, 0),
        name="partial_keys",
    )(act, sib, *weights, *state)


def close_kernel(at, act, mine, other, own, got, base, mom, diff, sent, steps0, steps1, *refs):
    keys, new_base, new_mom, loaded, stored, done, sems = refs[-7:]
    rows = diff.shape[0]
    part = pl.ds(at, rows)
    loads = [
        pltpu.make_async_copy(ref.at[part, :], loaded.at[i], sems.at[i]) for i, ref in enumerate((base, mom))
    ]
    for copy in loads:
        copy.start()
    depth = mine.shape[0]
    total = own[...] + got[...].astype(F32)
    total += dot(act[:, pl.ds(column(4, True, depth), depth)], mine[...])
    total += dot(act[:, pl.ds(column(4, False, depth), depth)], other[...])
    done[...] = total.astype(BF16)
    stores = [pltpu.make_async_copy(done, keys, sems.at[2])]
    stores[0].start()
    n = steps0.shape[0]
    ours = steps0[pl.ds(n - 16, 16), :][0:1, :].astype(F32)
    theirs = steps1[pl.ds(n - 16, 16), :][0:1, :].astype(F32)
    scale = 1.0 / (ours + theirs)
    average = (ours * scale) * diff[...].astype(F32) + (theirs * scale) * sent[...].astype(F32)
    for copy in loads:
        copy.wait()
    momentum = 0.9 * loaded[1] + average
    stored[1] = momentum
    stored[0] = loaded[0] - 0.7 * (average + 0.9 * momentum)
    for i, ref in enumerate((new_base, new_mom)):
        stores.append(pltpu.make_async_copy(stored.at[i], ref.at[part, :], sems.at[3 + i]))
        stores[-1].start()
    for copy in stores:
        copy.wait()


def close(act, mine, other, own, got, base, mom, diff, sent, steps0, steps1, at, state):
    tokens, width = own.shape
    rows = diff.shape[0]
    shape = jax.ShapeDtypeStruct(base.shape, F32)
    return pl.pallas_call(
        functools.partial(close_kernel, at),
        out_shape=(jax.ShapeDtypeStruct((tokens, width), BF16), shape, shape),
        in_specs=[VMEM] * 5 + [ANY] * 2 + [VMEM] * 4 + [ANY] * 2,
        out_specs=(ANY, ANY, ANY),
        input_output_aliases={11: 1, 12: 2},
        scratch_shapes=[
            pltpu.VMEM((2, rows, width), F32),
            pltpu.VMEM((2, rows, width), F32),
            pltpu.VMEM((tokens, width), BF16),
            pltpu.SemaphoreType.DMA((5,)),
        ],
        compiler_params=params(),
        cost_estimate=cost(0, 0),
        name="close",
    )(act, mine, other, own, got, base, mom, diff, sent, steps0, steps1, *state)


def special(activations, inner_weight, local_params, base_params, momentum, inner_steps):
    shape = base_params.shape
    flat = lambda a: a.reshape(-1, shape[-1])
    base, mom, local = flat(base_params), flat(momentum), flat(local_params)
    w = inner_weight[0]

    rows = base.shape[0]
    n1 = rows * 4 // 16
    n0 = rows - n1
    sib = send_core(activations)
    own0, own1 = difference(base, local, 0, (n0, n1), 4, (inner_steps.reshape(1, 1),))
    got0, got1 = send_x(own0), send_x(own1)
    w = tie(w, own0)[0]
    a1 = cycle(w)
    wsib = send_core(w)
    b1 = cycle(tie(wsib, sib)[0])
    a2 = cycle(a1)
    b2 = cycle(b1)
    state = partial_sums(((0, True), (1, True), (1, False)), activations, sib, (w, a1, b1), ())
    a2, *state = tie(a2, *state)
    a3 = cycle(a2)
    b3 = cycle(b2)
    state = partial_sums(((2, True), (2, False)), activations, sib, (a2, b2), state)
    a3, *state = tie(a3, *state)
    last = cycle(a3)
    own_sum, sib_sum = partial_sums(((3, True), (3, False)), activations, sib, (a3, b3), state, BF16)
    swapped = send_core(sib_sum)
    got0, own_sum = tie(got0, own_sum)
    new = outer(base, mom, own0, got0, own0, got0, 0, n0, n0 // 2, ())
    last, *new = tie(last, *new)
    other = send_core(last)
    keys, *new = close(
        activations, last, other, own_sum, swapped, base, mom, own1, got1, own0, got0, n0, new
    )
    return (keys, new[0].reshape(shape), new[1].reshape(shape))


def solution(mesh):
    fast = mesh.shape["replica"] == 2 and mesh.shape["fsdp"] == 16
    return jax.shard_map(
        special if fast else general,
        mesh=mesh,
        in_specs=(
            P(("replica", "fsdp"), None),
            P("replica", "fsdp", None),
            P("replica", None, None, "fsdp", None),
            P(None, None, "fsdp", None),
            P(None, None, "fsdp", None),
            P("replica"),
        ),
        out_specs=(
            P(("replica", "fsdp"), None),
            P(None, None, "fsdp", None),
            P(None, None, "fsdp", None),
        ),
        check_vma=False,
    )
```

time: 97 us -> 34.7 us (0.36)
  waiting for transfers between devices: 58.7 us -> 7.88 us
  starting transfers between devices: 0.08 us -> 17.7 us
  between operations: 16.3 us -> 1.37 us
  other arithmetic: 11 us -> 0 us
  Pallas kernels: 0 us -> 7.36 us
  blocking collectives: 5.19 us -> 0 us
  matrix products: 4.14 us -> 0 us
  local copies, waits for them, and re-layouts: 1.39 us -> 0.2 us
    psum x1 -> x0, waiting for transfers between devices: 58.1 us -> none  [body(): average = lax.psum(weighted, 'replica') / total]
    ppermute x0 -> x13, starting transfers between devices: none -> 17.7 us  [the longest x7 14 us: cycle(): return lax.ppermute(x, 'fsdp', pairs)]
    ppermute x0 -> x13, waiting for transfers between devices: none -> 7.88 us  [the longest x7 5.89 us: cycle(): return lax.ppermute(x, 'fsdp', pairs)]
    pallas_call x0 -> x6, Pallas kernels: none -> 7.36 us  [the longest x1 2.41 us: difference(): pl.pallas_call(functools.partial(difference_kernel, at, tuple(sizes), pie...]
    sub x1 -> x0, other arithmetic: 6.37 us -> none  [nesterov(): new_base = base_params - 0.7 * (average + 0.9 * new_momentum)]
    unnamed x1 -> x0, blocking collectives: 5.19 us -> none
    dot_general x1 -> x0, matrix products: 4.14 us -> none  [body(): jnp.dot(activations, lax.all_gather(inner_weight[0], 'fsdp', axis=0, tile...]
    mul x1 -> x0, other arithmetic: 4.04 us -> none  [body(): weighted = own * difference.astype(jnp.float32)]
  transfers between devices with their start and end apart: 2 -> 13, of which waited for: 1 -> 7; matrix products, arithmetic and copies ran while one was open for 9% -> 0% of each run, Pallas kernels for 0% -> 17%
where the time goes in v3:
time: 34.7 us; the launch traced here: 34.5 us
  starting transfers between devices  17.7 us (51%)
  waiting for transfers between devices  7.88 us (23%)
  Pallas kernels  7.36 us (21%)
  between operations  1.37 us (4%)
    ppermute x7, starting transfers between devices, cycle(): return lax.ppermute(x, 'fsdp', pairs)  14 us
    ppermute x7, waiting for transfers between devices, cycle(): return lax.ppermute(x, 'fsdp', pairs)  5.89 us
    ppermute x2, starting transfers between devices, send_x(): return lax.ppermute(x, 'replica', [(0, 1), (1, 0)])  2.98 us
    pallas_call x1, Pallas kernels, difference(): pl.pallas_call(functools.partial(difference_kernel, at, tuple(sizes), pie...  2.41 us
    ppermute x2, waiting for transfers between devices, send_x(): return lax.ppermute(x, 'replica', [(0, 1), (1, 0)])  1.98 us
    pallas_call x1, Pallas kernels, outer(): pl.pallas_call(outer_kernel, out_shape=(shape, shape), grid=(rows // bloc...  1.86 us
    pallas_call x1, Pallas kernels, close(): pl.pallas_call(functools.partial(close_kernel, at), out_shape=(jax.ShapeD...  1.65 us
    pallas_call x3, Pallas kernels, partial_sums(): pl.pallas_call(functools.partial(partial_kernel, blocks, not state), out_...  1.43 us
  transfers between devices with their start and end apart: 13, of which 7 were waited for; matrix products, arithmetic and copies ran while one was open for 0% of the time, Pallas kernels for 17%

profile of v3, /device:TPU:0, one launch (start us, length us, event | category | flops | bytes accessed | tf_op | source)
XLA Modules:
  0.0 34.5 jit_solution(9736762900861553112)
XLA Ops:
  0.6 0.5 %collective-permute-start.2 = (bf16[256,4096]{1,0:T(8,128)(2,1)}, bf16[256,4096]{1,0:T(8,128)(2,1)S(1)}, u32[]{:S(2)}, u32[]{:S(2)}) collective-permute-start(bf16[256,4096]{1,0:T(8,128)(2,1)} %act.7), channel_id=1, source_target_pairs={{0,1},{1,0},{2,3},{3,2},{4,5},{5,4},{6,7},{7,6},{8,9},{9,8},{10,11... | collective-permute-start | bytes 6291464 | tf_op jit(solution)/shard_map/ppermute | solution.py:53
  1.8 0.0 copy-start.3
  1.8 0.0 copy-start
  1.8 2.4 %difference.1 = (bf16[784,512]{1,0:T(8,128)(2,1)S(1)}, bf16[256,512]{1,0:T(8,128)(2,1)S(1)}) custom-call(f32[1024,512]{1,0:T(8,128)} %bitcast.8, f32[1024,512]{1,0:T(8,128)} %bitcast.16, s32[1,1]{1,0:T(1,128)} %bitcast.7.refs_0_), custom_call_target="tpu_custom_call" | custom-call | flops 1048576 | bytes 5242880 | tf_op jit(solution)/shard_map/difference/pallas_call | solution.py:107
  4.2 0.0 copy-done.3
  4.3 0.1 collective-permute-start.3
  4.4 3.0 %collective-permute-start = (bf16[256,512]{1,0:T(8,128)(2,1)S(1)}, bf16[256,512]{1,0:T(8,128)(2,1)S(1)}, u32[]{:S(2)}, u32[]{:S(2)}) collective-permute-start(bf16[256,512]{1,0:T(8,128)(2,1)S(1)} %bitcast.14), channel_id=1, source_target_pairs={{0,4},{1,3},{4,8},{5,1},{8,12},{9,5},{12,14},{13,9},{14,10},{15,13... | collective-permute-start | bytes 786440 | tf_op jit(solution)/shard_map/ppermute | solution.py:48
  7.4 1.5 %collective-permute-start.8 = (bf16[784,512]{1,0:T(8,128)(2,1)S(1)}, bf16[784,512]{1,0:T(8,128)(2,1)S(1)}, u32[]{:S(2)}, u32[]{:S(2)}) collective-permute-start(bf16[784,512]{1,0:T(8,128)(2,1)S(1)} %get-tuple-element.29.own.mine.steps0), channel_id=1, source_target_pairs={{0,16},{16,0},{1,17},{17,1},{2,18},{18,2},{3,19},{19,3},{4,20},{20... | collective-permute-start | bytes 2408456 | tf_op jit(solution)/shard_map/ppermute | solution.py:57
  8.9 0.0 collective-permute-done.3
  8.9 0.0 collective-permute-done.2.sib
  8.9 1.6 %collective-permute-start.4 = (bf16[256,512]{1,0:T(8,128)(2,1)S(1)}, bf16[256,512]{1,0:T(8,128)(2,1)S(1)}, u32[]{:S(2)}, u32[]{:S(2)}) collective-permute-start(bf16[256,512]{1,0:T(8,128)(2,1)S(1)} %collective-permute-done.3), channel_id=1, source_target_pairs={{0,4},{1,3},{4,8},{5,1},{8,12},{9,5},{12,14},{13,9},{14,10},{15,13... | collective-permute-start | bytes 786440 | tf_op jit(solution)/shard_map/ppermute | solution.py:48
  10.5 1.2 %collective-permute-done.refs_1_ = bf16[256,512]{1,0:T(8,128)(2,1)S(1)} collective-permute-done((bf16[256,512]{1,0:T(8,128)(2,1)S(1)}, bf16[256,512]{1,0:T(8,128)(2,1)S(1)}, u32[]{:S(2)}, u32[]{:S(2)}) %collective-permute-start) | collective-permute-done | bytes 262176 | tf_op jit(solution)/shard_map/ppermute | solution.py:48
  11.7 2.1 %collective-permute-start.1 = (bf16[256,512]{1,0:T(8,128)(2,1)S(1)}, bf16[256,512]{1,0:T(8,128)(2,1)S(1)}, u32[]{:S(2)}, u32[]{:S(2)}) collective-permute-start(bf16[256,512]{1,0:T(8,128)(2,1)S(1)} %collective-permute-done.refs_1_), channel_id=1, source_target_pairs={{0,4},{1,3},{4,8},{5,1},{8,12},{9,5},{12,14},{13,9},{14,10},{15,13... | collective-permute-start | bytes 786440 | tf_op jit(solution)/shard_map/ppermute | solution.py:48
  13.8 1.5 %collective-permute-done.4.refs_2_ = bf16[256,512]{1,0:T(8,128)(2,1)S(1)} collective-permute-done((bf16[256,512]{1,0:T(8,128)(2,1)S(1)}, bf16[256,512]{1,0:T(8,128)(2,1)S(1)}, u32[]{:S(2)}, u32[]{:S(2)}) %collective-permute-start.4) | collective-permute-done | bytes 262176 | tf_op jit(solution)/shard_map/ppermute | solution.py:48
  15.3 1.6 %collective-permute-start.6 = (bf16[256,512]{1,0:T(8,128)(2,1)S(1)}, bf16[256,512]{1,0:T(8,128)(2,1)S(1)}, u32[]{:S(2)}, u32[]{:S(2)}) collective-permute-start(bf16[256,512]{1,0:T(8,128)(2,1)S(1)} %collective-permute-done.4.refs_2_), channel_id=1, source_target_pairs={{0,4},{1,3},{4,8},{5,1},{8,12},{9,5},{12,14},{13,9},{14,10},{15,13... | collective-permute-start | bytes 786440 | tf_op jit(solution)/shard_map/ppermute | solution.py:48
  16.8 0.0 copy-done
  16.9 0.6 %partial_keys.3 = (f32[256,512]{1,0:T(8,128)S(1)}, f32[256,512]{1,0:T(8,128)S(1)}) custom-call(bf16[256,4096]{1,0:T(8,128)(2,1)S(1)} %copy-done, bf16[256,4096]{1,0:T(8,128)(2,1)S(1)} %collective-permute-done.2.sib, bf16[256,512]{1,0:T(8,128)(2,1)S(1)} %bitcast.15, bf16[256,512]{1,0:T(8,128)(2,1)S(1)} %collective-permute-done.refs_1_, ...), custom_call_target="tpu_custom_call" | custom-call | tf_op jit(solution)/shard_map/partial_keys/pallas_call | solution.py:184
  17.4 0.7 %collective-permute-done.1.refs_0_ = bf16[256,512]{1,0:T(8,128)(2,1)S(1)} collective-permute-done((bf16[256,512]{1,0:T(8,128)(2,1)S(1)}, bf16[256,512]{1,0:T(8,128)(2,1)S(1)}, u32[]{:S(2)}, u32[]{:S(2)}) %collective-permute-start.1) | collective-permute-done | bytes 262176 | tf_op jit(solution)/shard_map/ppermute | solution.py:48
  18.1 2.1 %collective-permute-start.5 = (bf16[256,512]{1,0:T(8,128)(2,1)S(1)}, bf16[256,512]{1,0:T(8,128)(2,1)S(1)}, u32[]{:S(2)}, u32[]{:S(2)}) collective-permute-start(bf16[256,512]{1,0:T(8,128)(2,1)S(1)} %collective-permute-done.1.refs_0_), channel_id=1, source_target_pairs={{0,4},{1,3},{4,8},{5,1},{8,12},{9,5},{12,14},{13,9},{14,10},{15,13... | collective-permute-start | bytes 786440 | tf_op jit(solution)/shard_map/ppermute | solution.py:48
  20.1 1.5 %collective-permute-done.6.refs_1_ = bf16[256,512]{1,0:T(8,128)(2,1)S(1)} collective-permute-done((bf16[256,512]{1,0:T(8,128)(2,1)S(1)}, bf16[256,512]{1,0:T(8,128)(2,1)S(1)}, u32[]{:S(2)}, u32[]{:S(2)}) %collective-permute-start.6) | collective-permute-done | bytes 262176 | tf_op jit(solution)/shard_map/ppermute | solution.py:48
  21.6 1.6 %collective-permute-start.9 = (bf16[256,512]{1,0:T(8,128)(2,1)S(1)}, bf16[256,512]{1,0:T(8,128)(2,1)S(1)}, u32[]{:S(2)}, u32[]{:S(2)}) collective-permute-start(bf16[256,512]{1,0:T(8,128)(2,1)S(1)} %collective-permute-done.6.refs_1_), channel_id=1, source_target_pairs={{0,4},{1,3},{4,8},{5,1},{8,12},{9,5},{12,14},{13,9},{14,10},{15,13... | collective-permute-start | bytes 786440 | tf_op jit(solution)/shard_map/ppermute | solution.py:48
  23.2 0.4 %partial_keys.4 = (f32[256,512]{1,0:T(8,128)S(1)}, f32[256,512]{1,0:T(8,128)S(1)}) custom-call(bf16[256,4096]{1,0:T(8,128)(2,1)S(1)} %copy-done, bf16[256,4096]{1,0:T(8,128)(2,1)S(1)} %collective-permute-done.2.sib, bf16[256,512]{1,0:T(8,128)(2,1)S(1)} %collective-permute-done.1.refs_0_, bf16[256,512]{1,0:T(8,128)(2,1)S(1)} %collective-permute-done.6.refs_1_, ...), custom_call_target="tpu_custom_call" | custom-call | tf_op jit(solution)/shard_map/partial_keys/pallas_call | solution.py:184
  23.7 0.8 %collective-permute-done.5.refs_0_ = bf16[256,512]{1,0:T(8,128)(2,1)S(1)} collective-permute-done((bf16[256,512]{1,0:T(8,128)(2,1)S(1)}, bf16[256,512]{1,0:T(8,128)(2,1)S(1)}, u32[]{:S(2)}, u32[]{:S(2)}) %collective-permute-start.5) | collective-permute-done | bytes 262176 | tf_op jit(solution)/shard_map/ppermute | solution.py:48
  24.5 2.1 %collective-permute-start.7 = (bf16[256,512]{1,0:T(8,128)(2,1)S(1)}, bf16[256,512]{1,0:T(8,128)(2,1)S(1)}, u32[]{:S(2)}, u32[]{:S(2)}) collective-permute-start(bf16[256,512]{1,0:T(8,128)(2,1)S(1)} %collective-permute-done.5.refs_0_), channel_id=1, source_target_pairs={{0,4},{1,3},{4,8},{5,1},{8,12},{9,5},{12,14},{13,9},{14,10},{15,13... | collective-permute-start | bytes 786440 | tf_op jit(solution)/shard_map/ppermute | solution.py:48
  26.5 0.0 copy-start.1
  26.5 0.0 copy-start.2
  26.5 1.5 %collective-permute-start.12 = (bf16[256,512]{1,0:T(8,128)(2,1)S(1)}, bf16[256,512]{1,0:T(8,128)(2,1)S(1)}, u32[]{:S(2)}, u32[]{:S(2)}) collective-permute-start(bf16[256,512]{1,0:T(8,128)(2,1)S(1)} %get-tuple-element.49.diff), channel_id=1, source_target_pairs={{0,16},{16,0},{1,17},{17,1},{2,18},{18,2},{3,19},{19,3},{4,20},{20... | collective-permute-start | bytes 786440 | tf_op jit(solution)/shard_map/ppermute | solution.py:57
  28.0 0.0 collective-permute-done.9.refs_1_
  28.0 0.4 %partial_keys.5 = (f32[256,512]{1,0:T(8,128)S(1)}, bf16[256,512]{1,0:T(8,128)(2,1)S(1)}) custom-call(bf16[256,4096]{1,0:T(8,128)(2,1)S(1)} %copy-done, bf16[256,4096]{1,0:T(8,128)(2,1)S(1)} %collective-permute-done.2.sib, bf16[256,512]{1,0:T(8,128)(2,1)S(1)} %collective-permute-done.5.refs_0_, bf16[256,512]{1,0:T(8,128)(2,1)S(1)} %collective-permute-done.9.refs_1_, ...), custom_call_target="tpu_custom_call" | custom-call | tf_op jit(solution)/shard_map/partial_keys/pallas_call | solution.py:184
  28.5 0.0 collective-permute-done.8.got.theirs.steps1
  28.5 0.1 collective-permute-start.11
  28.5 0.0 copy-done.1
  28.6 0.2 copy-done.2
  28.7 1.9 %outer_step.1 = (f32[1024,512]{1,0:T(8,128)}, f32[1024,512]{1,0:T(8,128)}) custom-call(f32[1024,512]{1,0:T(8,128)S(1)} %bitcast.9, f32[1024,512]{1,0:T(8,128)S(1)} %bitcast.11, bf16[784,512]{1,0:T(8,128)(2,1)S(1)} %get-tuple-element.29.own.mine.steps0, bf16[784,512]{1,0:T(8,128)(2,1)S(1)} %collective-permute-done.8.got.theirs.steps1, ...), custom_call_target="tpu_custom_call" | custom-call | flops 3932160 | bytes 7864320 | tf_op jit(solution)/shard_map/outer_step/pallas_call | solution.py:137
  30.6 0.2 collective-permute-done.7.mine
  30.8 0.1 collective-permute-start.10
  30.9 2.0 %collective-permute-done.12.sent = bf16[256,512]{1,0:T(8,128)(2,1)S(1)} collective-permute-done((bf16[256,512]{1,0:T(8,128)(2,1)S(1)}, bf16[256,512]{1,0:T(8,128)(2,1)S(1)}, u32[]{:S(2)}, u32[]{:S(2)}) %collective-permute-start.12) | collective-permute-done | bytes 262176 | tf_op jit(solution)/shard_map/ppermute | solution.py:57
  32.9 0.0 collective-permute-done.11.got
  32.9 0.0 collective-permute-done.10.other
  32.9 1.6 %close.1 = (bf16[256,512]{1,0:T(8,128)(2,1)}, f32[1024,512]{1,0:T(8,128)}, f32[1024,512]{1,0:T(8,128)}) custom-call(bf16[256,4096]{1,0:T(8,128)(2,1)S(1)} %copy-done, bf16[256,512]{1,0:T(8,128)(2,1)S(1)} %collective-permute-done.7.mine, bf16[256,512]{1,0:T(8,128)(2,1)S(1)} %collective-permute-done.10.other, ...), custom_call_target="tpu_custom_call", output_to_operand_aliasing={{1}: (11, {}), {2}: (12, {})} | custom-call | tf_op jit(solution)/shard_map/close/pallas_call | solution.py:232
Async XLA Ops:
  0.6 8.3 %collective-permute-start.2 = (bf16[256,4096]{1,0:T(8,128)(2,1)}, bf16[256,4096]{1,0:T(8,128)(2,1)S(1)}, u32[]{:S(2)}, u32[]{:S(2)}) collective-permute-start(bf16[256,4096]{1,0:T(8,128)(2,1)} %act.7), channel_id=1, source_target_pairs={{0,1},{1,0},{2,3},{3,2},{4,5},{5,4},{6,7},{7,6},{8,9},{9,8},{10,11... | collective-permute-start | bytes 6291464 | tf_op jit(solution)/shard_map/ppermute | solution.py:53
  1.8 2.4 %copy-start.3 = (bf16[1,256,512]{2,1,0:T(8,128)(2,1)S(1)}, bf16[1,256,512]{2,1,0:T(8,128)(2,1)}, u32[]{:S(2)}) copy-start(bf16[1,256,512]{2,1,0:T(8,128)(2,1)} %param.7) | copy-start | bytes 786436
  1.8 15.0 %copy-start = (bf16[256,4096]{1,0:T(8,128)(2,1)S(1)}, bf16[256,4096]{1,0:T(8,128)(2,1)}, u32[]{:S(2)}) copy-start(bf16[256,4096]{1,0:T(8,128)(2,1)} %act.7) | copy-start | bytes 6291460
  4.3 4.6 %collective-permute-start.3 = (bf16[256,512]{1,0:T(8,128)(2,1)S(1)}, bf16[256,512]{1,0:T(8,128)(2,1)S(1)}, u32[]{:S(2)}, u32[]{:S(2)}) collective-permute-start(bf16[256,512]{1,0:T(8,128)(2,1)S(1)} %bitcast.13), channel_id=1, source_target_pairs={{0,1},{1,0},{2,3},{3,2},{4,5},{5,4},{6,7},{7,6},{8,9},{9,8},{10,11... | collective-permute-start | bytes 786440 | tf_op jit(solution)/shard_map/ppermute | solution.py:53
  4.4 7.3 %collective-permute-start = (bf16[256,512]{1,0:T(8,128)(2,1)S(1)}, bf16[256,512]{1,0:T(8,128)(2,1)S(1)}, u32[]{:S(2)}, u32[]{:S(2)}) collective-permute-start(bf16[256,512]{1,0:T(8,128)(2,1)S(1)} %bitcast.14), channel_id=1, source_target_pairs={{0,4},{1,3},{4,8},{5,1},{8,12},{9,5},{12,14},{13,9},{14,10},{15,13... | collective-permute-start | bytes 786440 | tf_op jit(solution)/shard_map/ppermute | solution.py:48
  7.4 21.1 %collective-permute-start.8 = (bf16[784,512]{1,0:T(8,128)(2,1)S(1)}, bf16[784,512]{1,0:T(8,128)(2,1)S(1)}, u32[]{:S(2)}, u32[]{:S(2)}) collective-permute-start(bf16[784,512]{1,0:T(8,128)(2,1)S(1)} %get-tuple-element.29.own.mine.steps0), channel_id=1, source_target_pairs={{0,16},{16,0},{1,17},{17,1},{2,18},{18,2},{3,19},{19,3},{4,20},{20... | collective-permute-start | bytes 2408456 | tf_op jit(solution)/shard_map/ppermute | solution.py:57
  8.9 6.4 %collective-permute-start.4 = (bf16[256,512]{1,0:T(8,128)(2,1)S(1)}, bf16[256,512]{1,0:T(8,128)(2,1)S(1)}, u32[]{:S(2)}, u32[]{:S(2)}) collective-permute-start(bf16[256,512]{1,0:T(8,128)(2,1)S(1)} %collective-permute-done.3), channel_id=1, source_target_pairs={{0,4},{1,3},{4,8},{5,1},{8,12},{9,5},{12,14},{13,9},{14,10},{15,13... | collective-permute-start | bytes 786440 | tf_op jit(solution)/shard_map/ppermute | solution.py:48
  11.7 6.4 %collective-permute-start.1 = (bf16[256,512]{1,0:T(8,128)(2,1)S(1)}, bf16[256,512]{1,0:T(8,128)(2,1)S(1)}, u32[]{:S(2)}, u32[]{:S(2)}) collective-permute-start(bf16[256,512]{1,0:T(8,128)(2,1)S(1)} %collective-permute-done.refs_1_), channel_id=1, source_target_pairs={{0,4},{1,3},{4,8},{5,1},{8,12},{9,5},{12,14},{13,9},{14,10},{15,13... | collective-permute-start | bytes 786440 | tf_op jit(solution)/shard_map/ppermute | solution.py:48
  15.3 6.4 %collective-permute-start.6 = (bf16[256,512]{1,0:T(8,128)(2,1)S(1)}, bf16[256,512]{1,0:T(8,128)(2,1)S(1)}, u32[]{:S(2)}, u32[]{:S(2)}) collective-permute-start(bf16[256,512]{1,0:T(8,128)(2,1)S(1)} %collective-permute-done.4.refs_2_), channel_id=1, source_target_pairs={{0,4},{1,3},{4,8},{5,1},{8,12},{9,5},{12,14},{13,9},{14,10},{15,13... | collective-permute-start | bytes 786440 | tf_op jit(solution)/shard_map/ppermute | solution.py:48
  18.1 6.4 %collective-permute-start.5 = (bf16[256,512]{1,0:T(8,128)(2,1)S(1)}, bf16[256,512]{1,0:T(8,128)(2,1)S(1)}, u32[]{:S(2)}, u32[]{:S(2)}) collective-permute-start(bf16[256,512]{1,0:T(8,128)(2,1)S(1)} %collective-permute-done.1.refs_0_), channel_id=1, source_target_pairs={{0,4},{1,3},{4,8},{5,1},{8,12},{9,5},{12,14},{13,9},{14,10},{15,13... | collective-permute-start | bytes 786440 | tf_op jit(solution)/shard_map/ppermute | solution.py:48
  21.6 6.4 %collective-permute-start.9 = (bf16[256,512]{1,0:T(8,128)(2,1)S(1)}, bf16[256,512]{1,0:T(8,128)(2,1)S(1)}, u32[]{:S(2)}, u32[]{:S(2)}) collective-permute-start(bf16[256,512]{1,0:T(8,128)(2,1)S(1)} %collective-permute-done.6.refs_1_), channel_id=1, source_target_pairs={{0,4},{1,3},{4,8},{5,1},{8,12},{9,5},{12,14},{13,9},{14,10},{15,13... | collective-permute-start | bytes 786440 | tf_op jit(solution)/shard_map/ppermute | solution.py:48
  24.5 6.4 %collective-permute-start.7 = (bf16[256,512]{1,0:T(8,128)(2,1)S(1)}, bf16[256,512]{1,0:T(8,128)(2,1)S(1)}, u32[]{:S(2)}, u32[]{:S(2)}) collective-permute-start(bf16[256,512]{1,0:T(8,128)(2,1)S(1)} %collective-permute-done.5.refs_0_), channel_id=1, source_target_pairs={{0,4},{1,3},{4,8},{5,1},{8,12},{9,5},{12,14},{13,9},{14,10},{15,13... | collective-permute-start | bytes 786440 | tf_op jit(solution)/shard_map/ppermute | solution.py:48
  26.5 2.0 %copy-start.1 = (f32[2,2,256,512]{3,2,1,0:T(8,128)S(1)}, f32[2,2,256,512]{3,2,1,0:T(8,128)}, u32[]{:S(2)}) copy-start(f32[2,2,256,512]{3,2,1,0:T(8,128)} %param.9) | copy-start | bytes 6291460
  26.5 2.2 %copy-start.2 = (f32[2,2,256,512]{3,2,1,0:T(8,128)S(1)}, f32[2,2,256,512]{3,2,1,0:T(8,128)}, u32[]{:S(2)}) copy-start(f32[2,2,256,512]{3,2,1,0:T(8,128)} %param.10) | copy-start | bytes 6291460
  26.5 6.4 %collective-permute-start.12 = (bf16[256,512]{1,0:T(8,128)(2,1)S(1)}, bf16[256,512]{1,0:T(8,128)(2,1)S(1)}, u32[]{:S(2)}, u32[]{:S(2)}) collective-permute-start(bf16[256,512]{1,0:T(8,128)(2,1)S(1)} %get-tuple-element.49.diff), channel_id=1, source_target_pairs={{0,16},{16,0},{1,17},{17,1},{2,18},{18,2},{3,19},{19,3},{4,20},{20... | collective-permute-start | bytes 786440 | tf_op jit(solution)/shard_map/ppermute | solution.py:57
  28.5 4.4 %collective-permute-start.11 = (bf16[256,512]{1,0:T(8,128)(2,1)S(1)}, bf16[256,512]{1,0:T(8,128)(2,1)S(1)}, u32[]{:S(2)}, u32[]{:S(2)}) collective-permute-start(bf16[256,512]{1,0:T(8,128)(2,1)S(1)} %get-tuple-element.48), channel_id=1, source_target_pairs={{0,1},{1,0},{2,3},{3,2},{4,5},{5,4},{6,7},{7,6},{8,9},{9,8},{10,11... | collective-permute-start | bytes 786440 | tf_op jit(solution)/shard_map/ppermute | solution.py:53
  30.8 2.1 %collective-permute-start.10 = (bf16[256,512]{1,0:T(8,128)(2,1)S(1)}, bf16[256,512]{1,0:T(8,128)(2,1)S(1)}, u32[]{:S(2)}, u32[]{:S(2)}) collective-permute-start(bf16[256,512]{1,0:T(8,128)(2,1)S(1)} %collective-permute-done.7.mine), channel_id=1, source_target_pairs={{0,1},{1,0},{2,3},{3,2},{4,5},{5,4},{6,7},{7,6},{8,9},{9,8},{10,11... | collective-permute-start | bytes 786440 | tf_op jit(solution)/shard_map/ppermute | solution.py:53

commit v4 on v3

--- a/solution.py
+++ b/solution.py
@@ -259,10 +259,9 @@
     sib = send_core(activations)
     own0, own1 = difference(base, local, 0, (n0, n1), 4, (inner_steps.reshape(1, 1),))
     got0, got1 = send_x(own0), send_x(own1)
-    w = tie(w, own0)[0]
     a1 = cycle(w)
     wsib = send_core(w)
-    b1 = cycle(tie(wsib, sib)[0])
+    b1 = cycle(tie(wsib, sib, own0)[0])
     a2 = cycle(a1)
     b2 = cycle(b1)
     state = partial_sums(((0, True), (1, True), (1, False)), activations, sib, (w, a1, b1), ())

time: 34.7 us -> 34.4 us (level)
  starting transfers between devices: 17.7 us -> 15.3 us
  waiting for transfers between devices: 7.88 us -> 10.1 us
    ppermute x7, waiting for transfers between devices: 5.89 us -> 8.46 us  [cycle(): return lax.ppermute(x, 'fsdp', pairs)]
    ppermute x7, starting transfers between devices: 14 us -> 12.5 us  [cycle(): return lax.ppermute(x, 'fsdp', pairs)]
    ppermute x2, starting transfers between devices: 2.98 us -> 2.09 us  [send_x(): return lax.ppermute(x, 'replica', [(0, 1), (1, 0)])]
where the time goes in v4:
time: 34.4 us; the launch traced here: 34.2 us
  starting transfers between devices  15.3 us (44%)
  waiting for transfers between devices  10.1 us (29%)
  Pallas kernels  7.39 us (21%)
  between operations  1.37 us (4%)
    ppermute x7, starting transfers between devices, cycle(): return lax.ppermute(x, 'fsdp', pairs)  12.5 us
    ppermute x7, waiting for transfers between devices, cycle(): return lax.ppermute(x, 'fsdp', pairs)  8.46 us
    pallas_call x1, Pallas kernels, difference(): pl.pallas_call(functools.partial(difference_kernel, at, tuple(sizes), pie...  2.41 us
    ppermute x2, starting transfers between devices, send_x(): return lax.ppermute(x, 'replica', [(0, 1), (1, 0)])  2.09 us
    pallas_call x1, Pallas kernels, outer(): pl.pallas_call(outer_kernel, out_shape=(shape, shape), grid=(rows // bloc...  1.9 us
    pallas_call x1, Pallas kernels, close(): pl.pallas_call(functools.partial(close_kernel, at), out_shape=(jax.ShapeD...  1.64 us
    ppermute x2, waiting for transfers between devices, send_x(): return lax.ppermute(x, 'replica', [(0, 1), (1, 0)])  1.64 us
    pallas_call x3, Pallas kernels, partial_sums(): pl.pallas_call(functools.partial(partial_kernel, blocks, not state), out_...  1.44 us
  transfers between devices with their start and end apart: 13, of which 7 were waited for; matrix products, arithmetic and copies ran while one was open for 0% of the time, Pallas kernels for 17%

profile of v4, /device:TPU:0, one launch (start us, length us, event | category | flops | bytes accessed | tf_op | source)
XLA Modules:
  0.0 34.2 jit_solution(9172076239592264362)
XLA Ops:
  0.6 0.5 %collective-permute-start.2 = (bf16[256,4096]{1,0:T(8,128)(2,1)}, bf16[256,4096]{1,0:T(8,128)(2,1)S(1)}, u32[]{:S(2)}, u32[]{:S(2)}) collective-permute-start(bf16[256,4096]{1,0:T(8,128)(2,1)} %act.7), channel_id=1, source_target_pairs={{0,1},{1,0},{2,3},{3,2},{4,5},{5,4},{6,7},{7,6},{8,9},{9,8},{10,11... | collective-permute-start | bytes 6291464 | tf_op jit(solution)/shard_map/ppermute | solution.py:53
  1.1 0.1 collective-permute-start.3
  1.2 3.0 %collective-permute-start = (bf16[256,512]{1,0:T(8,128)(2,1)}, bf16[256,512]{1,0:T(8,128)(2,1)S(1)}, u32[]{:S(2)}, u32[]{:S(2)}) collective-permute-start(bf16[256,512]{1,0:T(8,128)(2,1)} %bitcast.14), channel_id=1, source_target_pairs={{0,4},{1,3},{4,8},{5,1},{8,12},{9,5},{12,14},{13,9},{14,10},{15,13... | collective-permute-start | bytes 786440 | tf_op jit(solution)/shard_map/ppermute | solution.py:48
  4.9 0.0 copy-start
  4.9 0.0 copy-start.3
  4.9 2.4 %difference.1 = (bf16[784,512]{1,0:T(8,128)(2,1)S(1)}, bf16[256,512]{1,0:T(8,128)(2,1)S(1)}) custom-call(f32[1024,512]{1,0:T(8,128)} %bitcast.8, f32[1024,512]{1,0:T(8,128)} %bitcast.16, s32[1,1]{1,0:T(1,128)} %bitcast.7.refs_0_), custom_call_target="tpu_custom_call" | custom-call | flops 1048576 | bytes 5242880 | tf_op jit(solution)/shard_map/difference/pallas_call | solution.py:107
  7.3 1.6 %collective-permute-start.8 = (bf16[784,512]{1,0:T(8,128)(2,1)S(1)}, bf16[784,512]{1,0:T(8,128)(2,1)S(1)}, u32[]{:S(2)}, u32[]{:S(2)}) collective-permute-start(bf16[784,512]{1,0:T(8,128)(2,1)S(1)} %get-tuple-element.28.own.mine.steps0), channel_id=1, source_target_pairs={{0,16},{16,0},{1,17},{17,1},{2,18},{18,2},{3,19},{19,3},{4,20},{20... | collective-permute-start | bytes 2408456 | tf_op jit(solution)/shard_map/ppermute | solution.py:57
  8.9 0.0 collective-permute-done.3
  8.9 0.0 collective-permute-done.2.sib
  8.9 1.6 %collective-permute-start.4 = (bf16[256,512]{1,0:T(8,128)(2,1)S(1)}, bf16[256,512]{1,0:T(8,128)(2,1)S(1)}, u32[]{:S(2)}, u32[]{:S(2)}) collective-permute-start(bf16[256,512]{1,0:T(8,128)(2,1)S(1)} %collective-permute-done.3), channel_id=1, source_target_pairs={{0,4},{1,3},{4,8},{5,1},{8,12},{9,5},{12,14},{13,9},{14,10},{15,13... | collective-permute-start | bytes 786440 | tf_op jit(solution)/shard_map/ppermute | solution.py:48
  10.5 0.0 collective-permute-done.refs_1_
  10.5 1.6 %collective-permute-start.1 = (bf16[256,512]{1,0:T(8,128)(2,1)S(1)}, bf16[256,512]{1,0:T(8,128)(2,1)S(1)}, u32[]{:S(2)}, u32[]{:S(2)}) collective-permute-start(bf16[256,512]{1,0:T(8,128)(2,1)S(1)} %collective-permute-done.refs_1_), channel_id=1, source_target_pairs={{0,4},{1,3},{4,8},{5,1},{8,12},{9,5},{12,14},{13,9},{14,10},{15,13... | collective-permute-start | bytes 786440 | tf_op jit(solution)/shard_map/ppermute | solution.py:48
  12.0 3.2 %collective-permute-done.4.refs_2_ = bf16[256,512]{1,0:T(8,128)(2,1)S(1)} collective-permute-done((bf16[256,512]{1,0:T(8,128)(2,1)S(1)}, bf16[256,512]{1,0:T(8,128)(2,1)S(1)}, u32[]{:S(2)}, u32[]{:S(2)}) %collective-permute-start.4) | collective-permute-done | bytes 262176 | tf_op jit(solution)/shard_map/ppermute | solution.py:48
  15.3 1.6 %collective-permute-start.6 = (bf16[256,512]{1,0:T(8,128)(2,1)S(1)}, bf16[256,512]{1,0:T(8,128)(2,1)S(1)}, u32[]{:S(2)}, u32[]{:S(2)}) collective-permute-start(bf16[256,512]{1,0:T(8,128)(2,1)S(1)} %collective-permute-done.4.refs_2_), channel_id=1, source_target_pairs={{0,4},{1,3},{4,8},{5,1},{8,12},{9,5},{12,14},{13,9},{14,10},{15,13... | collective-permute-start | bytes 786440 | tf_op jit(solution)/shard_map/ppermute | solution.py:48
  16.8 0.0 copy-done
  16.8 0.0 copy-done.3
  16.8 0.6 %partial_keys.3 = (f32[256,512]{1,0:T(8,128)S(1)}, f32[256,512]{1,0:T(8,128)S(1)}) custom-call(bf16[256,4096]{1,0:T(8,128)(2,1)S(1)} %copy-done, bf16[256,4096]{1,0:T(8,128)(2,1)S(1)} %collective-permute-done.2.sib, bf16[256,512]{1,0:T(8,128)(2,1)S(1)} %bitcast.15, bf16[256,512]{1,0:T(8,128)(2,1)S(1)} %collective-permute-done.refs_1_, ...), custom_call_target="tpu_custom_call" | custom-call | tf_op jit(solution)/shard_map/partial_keys/pallas_call | solution.py:184
  17.4 0.7 %collective-permute-done.1.refs_0_ = bf16[256,512]{1,0:T(8,128)(2,1)S(1)} collective-permute-done((bf16[256,512]{1,0:T(8,128)(2,1)S(1)}, bf16[256,512]{1,0:T(8,128)(2,1)S(1)}, u32[]{:S(2)}, u32[]{:S(2)}) %collective-permute-start.1) | collective-permute-done | bytes 262176 | tf_op jit(solution)/shard_map/ppermute | solution.py:48
  18.1 1.6 %collective-permute-start.5 = (bf16[256,512]{1,0:T(8,128)(2,1)S(1)}, bf16[256,512]{1,0:T(8,128)(2,1)S(1)}, u32[]{:S(2)}, u32[]{:S(2)}) collective-permute-start(bf16[256,512]{1,0:T(8,128)(2,1)S(1)} %collective-permute-done.1.refs_0_), channel_id=1, source_target_pairs={{0,4},{1,3},{4,8},{5,1},{8,12},{9,5},{12,14},{13,9},{14,10},{15,13... | collective-permute-start | bytes 786440 | tf_op jit(solution)/shard_map/ppermute | solution.py:48
  19.6 2.0 %collective-permute-done.6.refs_1_ = bf16[256,512]{1,0:T(8,128)(2,1)S(1)} collective-permute-done((bf16[256,512]{1,0:T(8,128)(2,1)S(1)}, bf16[256,512]{1,0:T(8,128)(2,1)S(1)}, u32[]{:S(2)}, u32[]{:S(2)}) %collective-permute-start.6) | collective-permute-done | bytes 262176 | tf_op jit(solution)/shard_map/ppermute | solution.py:48
  21.6 1.6 %collective-permute-start.9 = (bf16[256,512]{1,0:T(8,128)(2,1)S(1)}, bf16[256,512]{1,0:T(8,128)(2,1)S(1)}, u32[]{:S(2)}, u32[]{:S(2)}) collective-permute-start(bf16[256,512]{1,0:T(8,128)(2,1)S(1)} %collective-permute-done.6.refs_1_), channel_id=1, source_target_pairs={{0,4},{1,3},{4,8},{5,1},{8,12},{9,5},{12,14},{13,9},{14,10},{15,13... | collective-permute-start | bytes 786440 | tf_op jit(solution)/shard_map/ppermute | solution.py:48
  23.2 0.4 %partial_keys.4 = (f32[256,512]{1,0:T(8,128)S(1)}, f32[256,512]{1,0:T(8,128)S(1)}) custom-call(bf16[256,4096]{1,0:T(8,128)(2,1)S(1)} %copy-done, bf16[256,4096]{1,0:T(8,128)(2,1)S(1)} %collective-permute-done.2.sib, bf16[256,512]{1,0:T(8,128)(2,1)S(1)} %collective-permute-done.1.refs_0_, bf16[256,512]{1,0:T(8,128)(2,1)S(1)} %collective-permute-done.6.refs_1_, ...), custom_call_target="tpu_custom_call" | custom-call | tf_op jit(solution)/shard_map/partial_keys/pallas_call | solution.py:184
  23.7 0.8 %collective-permute-done.5.refs_0_ = bf16[256,512]{1,0:T(8,128)(2,1)S(1)} collective-permute-done((bf16[256,512]{1,0:T(8,128)(2,1)S(1)}, bf16[256,512]{1,0:T(8,128)(2,1)S(1)}, u32[]{:S(2)}, u32[]{:S(2)}) %collective-permute-start.5) | collective-permute-done | bytes 262176 | tf_op jit(solution)/shard_map/ppermute | solution.py:48
  24.4 1.6 %collective-permute-start.7 = (bf16[256,512]{1,0:T(8,128)(2,1)S(1)}, bf16[256,512]{1,0:T(8,128)(2,1)S(1)}, u32[]{:S(2)}, u32[]{:S(2)}) collective-permute-start(bf16[256,512]{1,0:T(8,128)(2,1)S(1)} %collective-permute-done.5.refs_0_), channel_id=1, source_target_pairs={{0,4},{1,3},{4,8},{5,1},{8,12},{9,5},{12,14},{13,9},{14,10},{15,13... | collective-permute-start | bytes 786440 | tf_op jit(solution)/shard_map/ppermute | solution.py:48
  26.0 0.0 copy-start.1
  26.0 0.0 copy-start.2
  26.0 0.5 %collective-permute-start.12 = (bf16[256,512]{1,0:T(8,128)(2,1)S(1)}, bf16[256,512]{1,0:T(8,128)(2,1)S(1)}, u32[]{:S(2)}, u32[]{:S(2)}) collective-permute-start(bf16[256,512]{1,0:T(8,128)(2,1)S(1)} %get-tuple-element.47.diff), channel_id=1, source_target_pairs={{0,16},{16,0},{1,17},{17,1},{2,18},{18,2},{3,19},{19,3},{4,20},{20... | collective-permute-start | bytes 786440 | tf_op jit(solution)/shard_map/ppermute | solution.py:57
  26.6 1.4 %collective-permute-done.9.refs_1_ = bf16[256,512]{1,0:T(8,128)(2,1)S(1)} collective-permute-done((bf16[256,512]{1,0:T(8,128)(2,1)S(1)}, bf16[256,512]{1,0:T(8,128)(2,1)S(1)}, u32[]{:S(2)}, u32[]{:S(2)}) %collective-permute-start.9) | collective-permute-done | bytes 262176 | tf_op jit(solution)/shard_map/ppermute | solution.py:48
  28.0 0.4 %partial_keys.5 = (f32[256,512]{1,0:T(8,128)S(1)}, bf16[256,512]{1,0:T(8,128)(2,1)S(1)}) custom-call(bf16[256,4096]{1,0:T(8,128)(2,1)S(1)} %copy-done, bf16[256,4096]{1,0:T(8,128)(2,1)S(1)} %collective-permute-done.2.sib, bf16[256,512]{1,0:T(8,128)(2,1)S(1)} %collective-permute-done.5.refs_0_, bf16[256,512]{1,0:T(8,128)(2,1)S(1)} %collective-permute-done.9.refs_1_, ...), custom_call_target="tpu_custom_call" | custom-call | tf_op jit(solution)/shard_map/partial_keys/pallas_call | solution.py:184
  28.4 0.0 collective-permute-done.8.got.theirs.steps1
  28.5 0.1 collective-permute-start.11
  28.5 0.0 copy-done.1
  28.5 0.0 copy-done.2
  28.6 1.9 %outer_step.1 = (f32[1024,512]{1,0:T(8,128)}, f32[1024,512]{1,0:T(8,128)}) custom-call(f32[1024,512]{1,0:T(8,128)S(1)} %bitcast.9, f32[1024,512]{1,0:T(8,128)S(1)} %bitcast.11, bf16[784,512]{1,0:T(8,128)(2,1)S(1)} %get-tuple-element.28.own.mine.steps0, bf16[784,512]{1,0:T(8,128)(2,1)S(1)} %collective-permute-done.8.got.theirs.steps1, ...), custom_call_target="tpu_custom_call" | custom-call | flops 3932160 | bytes 7864320 | tf_op jit(solution)/shard_map/outer_step/pallas_call | solution.py:137
  30.5 0.4 %collective-permute-done.7.mine = bf16[256,512]{1,0:T(8,128)(2,1)S(1)} collective-permute-done((bf16[256,512]{1,0:T(8,128)(2,1)S(1)}, bf16[256,512]{1,0:T(8,128)(2,1)S(1)}, u32[]{:S(2)}, u32[]{:S(2)}) %collective-permute-start.7) | collective-permute-done | bytes 262176 | tf_op jit(solution)/shard_map/ppermute | solution.py:48
  30.8 0.1 collective-permute-start.10
  30.9 1.6 %collective-permute-done.12.sent = bf16[256,512]{1,0:T(8,128)(2,1)S(1)} collective-permute-done((bf16[256,512]{1,0:T(8,128)(2,1)S(1)}, bf16[256,512]{1,0:T(8,128)(2,1)S(1)}, u32[]{:S(2)}, u32[]{:S(2)}) %collective-permute-start.12) | collective-permute-done | bytes 262176 | tf_op jit(solution)/shard_map/ppermute | solution.py:57
  32.5 0.0 collective-permute-done.11.got
  32.5 0.0 collective-permute-done.10.other
  32.6 1.6 %close.1 = (bf16[256,512]{1,0:T(8,128)(2,1)}, f32[1024,512]{1,0:T(8,128)}, f32[1024,512]{1,0:T(8,128)}) custom-call(bf16[256,4096]{1,0:T(8,128)(2,1)S(1)} %copy-done, bf16[256,512]{1,0:T(8,128)(2,1)S(1)} %collective-permute-done.7.mine, bf16[256,512]{1,0:T(8,128)(2,1)S(1)} %collective-permute-done.10.other, ...), custom_call_target="tpu_custom_call", output_to_operand_aliasing={{1}: (11, {}), {2}: (12, {})} | custom-call | tf_op jit(solution)/shard_map/close/pallas_call | solution.py:232
Async XLA Ops:
  0.6 8.3 %collective-permute-start.2 = (bf16[256,4096]{1,0:T(8,128)(2,1)}, bf16[256,4096]{1,0:T(8,128)(2,1)S(1)}, u32[]{:S(2)}, u32[]{:S(2)}) collective-permute-start(bf16[256,4096]{1,0:T(8,128)(2,1)} %act.7), channel_id=1, source_target_pairs={{0,1},{1,0},{2,3},{3,2},{4,5},{5,4},{6,7},{7,6},{8,9},{9,8},{10,11... | collective-permute-start | bytes 6291464 | tf_op jit(solution)/shard_map/ppermute | solution.py:53
  1.1 7.7 %collective-permute-start.3 = (bf16[256,512]{1,0:T(8,128)(2,1)}, bf16[256,512]{1,0:T(8,128)(2,1)S(1)}, u32[]{:S(2)}, u32[]{:S(2)}) collective-permute-start(bf16[256,512]{1,0:T(8,128)(2,1)} %bitcast.13), channel_id=1, source_target_pairs={{0,1},{1,0},{2,3},{3,2},{4,5},{5,4},{6,7},{7,6},{8,9},{9,8},{10,11... | collective-permute-start | bytes 786440 | tf_op jit(solution)/shard_map/ppermute | solution.py:53
  1.2 9.2 %collective-permute-start = (bf16[256,512]{1,0:T(8,128)(2,1)}, bf16[256,512]{1,0:T(8,128)(2,1)S(1)}, u32[]{:S(2)}, u32[]{:S(2)}) collective-permute-start(bf16[256,512]{1,0:T(8,128)(2,1)} %bitcast.14), channel_id=1, source_target_pairs={{0,4},{1,3},{4,8},{5,1},{8,12},{9,5},{12,14},{13,9},{14,10},{15,13... | collective-permute-start | bytes 786440 | tf_op jit(solution)/shard_map/ppermute | solution.py:48
  4.9 12.0 %copy-start = (bf16[256,4096]{1,0:T(8,128)(2,1)S(1)}, bf16[256,4096]{1,0:T(8,128)(2,1)}, u32[]{:S(2)}) copy-start(bf16[256,4096]{1,0:T(8,128)(2,1)} %act.7) | copy-start | bytes 6291460
  4.9 12.0 %copy-start.3 = (bf16[1,256,512]{2,1,0:T(8,128)(2,1)S(1)}, bf16[1,256,512]{2,1,0:T(8,128)(2,1)}, u32[]{:S(2)}) copy-start(bf16[1,256,512]{2,1,0:T(8,128)(2,1)} %param.7) | copy-start | bytes 786436
  7.3 21.1 %collective-permute-start.8 = (bf16[784,512]{1,0:T(8,128)(2,1)S(1)}, bf16[784,512]{1,0:T(8,128)(2,1)S(1)}, u32[]{:S(2)}, u32[]{:S(2)}) collective-permute-start(bf16[784,512]{1,0:T(8,128)(2,1)S(1)} %get-tuple-element.28.own.mine.steps0), channel_id=1, source_target_pairs={{0,16},{16,0},{1,17},{17,1},{2,18},{18,2},{3,19},{19,3},{4,20},{20... | collective-permute-start | bytes 2408456 | tf_op jit(solution)/shard_map/ppermute | solution.py:57
  8.9 6.4 %collective-permute-start.4 = (bf16[256,512]{1,0:T(8,128)(2,1)S(1)}, bf16[256,512]{1,0:T(8,128)(2,1)S(1)}, u32[]{:S(2)}, u32[]{:S(2)}) collective-permute-start(bf16[256,512]{1,0:T(8,128)(2,1)S(1)} %collective-permute-done.3), channel_id=1, source_target_pairs={{0,4},{1,3},{4,8},{5,1},{8,12},{9,5},{12,14},{13,9},{14,10},{15,13... | collective-permute-start | bytes 786440 | tf_op jit(solution)/shard_map/ppermute | solution.py:48
  10.5 7.6 %collective-permute-start.1 = (bf16[256,512]{1,0:T(8,128)(2,1)S(1)}, bf16[256,512]{1,0:T(8,128)(2,1)S(1)}, u32[]{:S(2)}, u32[]{:S(2)}) collective-permute-start(bf16[256,512]{1,0:T(8,128)(2,1)S(1)} %collective-permute-done.refs_1_), channel_id=1, source_target_pairs={{0,4},{1,3},{4,8},{5,1},{8,12},{9,5},{12,14},{13,9},{14,10},{15,13... | collective-permute-start | bytes 786440 | tf_op jit(solution)/shard_map/ppermute | solution.py:48
  15.3 6.4 %collective-permute-start.6 = (bf16[256,512]{1,0:T(8,128)(2,1)S(1)}, bf16[256,512]{1,0:T(8,128)(2,1)S(1)}, u32[]{:S(2)}, u32[]{:S(2)}) collective-permute-start(bf16[256,512]{1,0:T(8,128)(2,1)S(1)} %collective-permute-done.4.refs_2_), channel_id=1, source_target_pairs={{0,4},{1,3},{4,8},{5,1},{8,12},{9,5},{12,14},{13,9},{14,10},{15,13... | collective-permute-start | bytes 786440 | tf_op jit(solution)/shard_map/ppermute | solution.py:48
  18.1 6.4 %collective-permute-start.5 = (bf16[256,512]{1,0:T(8,128)(2,1)S(1)}, bf16[256,512]{1,0:T(8,128)(2,1)S(1)}, u32[]{:S(2)}, u32[]{:S(2)}) collective-permute-start(bf16[256,512]{1,0:T(8,128)(2,1)S(1)} %collective-permute-done.1.refs_0_), channel_id=1, source_target_pairs={{0,4},{1,3},{4,8},{5,1},{8,12},{9,5},{12,14},{13,9},{14,10},{15,13... | collective-permute-start | bytes 786440 | tf_op jit(solution)/shard_map/ppermute | solution.py:48
  21.6 6.4 %collective-permute-start.9 = (bf16[256,512]{1,0:T(8,128)(2,1)S(1)}, bf16[256,512]{1,0:T(8,128)(2,1)S(1)}, u32[]{:S(2)}, u32[]{:S(2)}) collective-permute-start(bf16[256,512]{1,0:T(8,128)(2,1)S(1)} %collective-permute-done.6.refs_1_), channel_id=1, source_target_pairs={{0,4},{1,3},{4,8},{5,1},{8,12},{9,5},{12,14},{13,9},{14,10},{15,13... | collective-permute-start | bytes 786440 | tf_op jit(solution)/shard_map/ppermute | solution.py:48
  24.4 6.4 %collective-permute-start.7 = (bf16[256,512]{1,0:T(8,128)(2,1)S(1)}, bf16[256,512]{1,0:T(8,128)(2,1)S(1)}, u32[]{:S(2)}, u32[]{:S(2)}) collective-permute-start(bf16[256,512]{1,0:T(8,128)(2,1)S(1)} %collective-permute-done.5.refs_0_), channel_id=1, source_target_pairs={{0,4},{1,3},{4,8},{5,1},{8,12},{9,5},{12,14},{13,9},{14,10},{15,13... | collective-permute-start | bytes 786440 | tf_op jit(solution)/shard_map/ppermute | solution.py:48
  26.0 2.5 %copy-start.1 = (f32[2,2,256,512]{3,2,1,0:T(8,128)S(1)}, f32[2,2,256,512]{3,2,1,0:T(8,128)}, u32[]{:S(2)}) copy-start(f32[2,2,256,512]{3,2,1,0:T(8,128)} %param.9) | copy-start | bytes 6291460
  26.0 2.5 %copy-start.2 = (f32[2,2,256,512]{3,2,1,0:T(8,128)S(1)}, f32[2,2,256,512]{3,2,1,0:T(8,128)}, u32[]{:S(2)}) copy-start(f32[2,2,256,512]{3,2,1,0:T(8,128)} %param.10) | copy-start | bytes 6291460
  26.0 6.5 %collective-permute-start.12 = (bf16[256,512]{1,0:T(8,128)(2,1)S(1)}, bf16[256,512]{1,0:T(8,128)(2,1)S(1)}, u32[]{:S(2)}, u32[]{:S(2)}) collective-permute-start(bf16[256,512]{1,0:T(8,128)(2,1)S(1)} %get-tuple-element.47.diff), channel_id=1, source_target_pairs={{0,16},{16,0},{1,17},{17,1},{2,18},{18,2},{3,19},{19,3},{4,20},{20... | collective-permute-start | bytes 786440 | tf_op jit(solution)/shard_map/ppermute | solution.py:57
  28.5 4.1 %collective-permute-start.11 = (bf16[256,512]{1,0:T(8,128)(2,1)S(1)}, bf16[256,512]{1,0:T(8,128)(2,1)S(1)}, u32[]{:S(2)}, u32[]{:S(2)}) collective-permute-start(bf16[256,512]{1,0:T(8,128)(2,1)S(1)} %get-tuple-element.46), channel_id=1, source_target_pairs={{0,1},{1,0},{2,3},{3,2},{4,5},{5,4},{6,7},{7,6},{8,9},{9,8},{10,11... | collective-permute-start | bytes 786440 | tf_op jit(solution)/shard_map/ppermute | solution.py:53
  30.8 1.7 %collective-permute-start.10 = (bf16[256,512]{1,0:T(8,128)(2,1)S(1)}, bf16[256,512]{1,0:T(8,128)(2,1)S(1)}, u32[]{:S(2)}, u32[]{:S(2)}) collective-permute-start(bf16[256,512]{1,0:T(8,128)(2,1)S(1)} %collective-permute-done.7.mine), channel_id=1, source_target_pairs={{0,1},{1,0},{2,3},{3,2},{4,5},{5,4},{6,7},{7,6},{8,9},{9,8},{10,11... | collective-permute-start | bytes 786440 | tf_op jit(solution)/shard_map/ppermute | solution.py:53

commit v5 on v4

--- a/solution.py
+++ b/solution.py
@@ -110,7 +110,7 @@
         in_specs=[HBM, HBM] + [VMEM] * len(steps),
         out_specs=(VMEM,) * len(sizes),
         scratch_shapes=[pltpu.VMEM((2, rows, width), F32), pltpu.SemaphoreType.DMA((2, pieces))],
-        compiler_params=params(52),
+        compiler_params=params(52 if at == 0 else 16),
         cost_estimate=cost(2 * rows * width, 10 * rows * width),
         name="difference",
     )(base, local, *steps)
@@ -257,12 +257,15 @@
     n1 = rows * 4 // 16
     n0 = rows - n1
     sib = send_core(activations)
-    own0, own1 = difference(base, local, 0, (n0, n1), 4, (inner_steps.reshape(1, 1),))
-    got0, got1 = send_x(own0), send_x(own1)
+    (own0,) = difference(base, local, 0, (n0,), 3, (inner_steps.reshape(1, 1),))
+    (own1,) = difference(tie(base, own0)[0], local, n0, (n1,), 1)
+    got0 = send_x(own0)
     a1 = cycle(w)
     wsib = send_core(w)
     b1 = cycle(tie(wsib, sib, own0)[0])
     a2 = cycle(a1)
+    b1, own1 = tie(b1, own1)
+    got1 = send_x(own1)
     b2 = cycle(b1)
     state = partial_sums(((0, True), (1, True), (1, False)), activations, sib, (w, a1, b1), ())
     a2, *state = tie(a2, *state)

time: 34.4 us -> 34.1 us (level)
    pallas_call x1 -> x2, Pallas kernels: 2.41 us -> 2.22 us  [difference(): pl.pallas_call(functools.partial(difference_kernel, at, tuple(sizes), pie...]
  transfers between devices with their start and end apart: 13 -> 13, of which waited for: 7 -> 7; matrix products, arithmetic and copies ran while one was open for 0% -> 0% of each run, Pallas kernels for 17% -> 16%
where the time goes in v5:
time: 34.1 us; the launch traced here: 33.9 us
  starting transfers between devices  15.3 us (45%)
  waiting for transfers between devices  9.97 us (29%)
  Pallas kernels  7.2 us (21%)
  between operations  1.38 us (4%)
    ppermute x7, starting transfers between devices, cycle(): return lax.ppermute(x, 'fsdp', pairs)  12.5 us
    ppermute x7, waiting for transfers between devices, cycle(): return lax.ppermute(x, 'fsdp', pairs)  8.32 us
    pallas_call x2, Pallas kernels, difference(): pl.pallas_call(functools.partial(difference_kernel, at, tuple(sizes), pie...  2.22 us
    ppermute x2, starting transfers between devices, send_x(): return lax.ppermute(x, 'replica', [(0, 1), (1, 0)])  2.09 us
    pallas_call x1, Pallas kernels, outer(): pl.pallas_call(outer_kernel, out_shape=(shape, shape), grid=(rows // bloc...  1.9 us
    ppermute x2, waiting for transfers between devices, send_x(): return lax.ppermute(x, 'replica', [(0, 1), (1, 0)])  1.65 us
    pallas_call x1, Pallas kernels, close(): pl.pallas_call(functools.partial(close_kernel, at), out_shape=(jax.ShapeD...  1.65 us
    pallas_call x3, Pallas kernels, partial_sums(): pl.pallas_call(functools.partial(partial_kernel, blocks, not state), out_...  1.44 us
  transfers between devices with their start and end apart: 13, of which 7 were waited for; matrix products, arithmetic and copies ran while one was open for 0% of the time, Pallas kernels for 16%

profile of v5, /device:TPU:0, one launch (start us, length us, event | category | flops | bytes accessed | tf_op | source)
XLA Modules:
  0.0 33.9 jit_solution(15338502288758536256)
XLA Ops:
  0.6 0.5 %collective-permute-start.2 = (bf16[256,4096]{1,0:T(8,128)(2,1)}, bf16[256,4096]{1,0:T(8,128)(2,1)S(1)}, u32[]{:S(2)}, u32[]{:S(2)}) collective-permute-start(bf16[256,4096]{1,0:T(8,128)(2,1)} %act.7), channel_id=1, source_target_pairs={{0,1},{1,0},{2,3},{3,2},{4,5},{5,4},{6,7},{7,6},{8,9},{9,8},{10,11... | collective-permute-start | bytes 6291464 | tf_op jit(solution)/shard_map/ppermute | solution.py:53
  1.1 0.1 collective-permute-start.3
  1.2 3.0 %collective-permute-start = (bf16[256,512]{1,0:T(8,128)(2,1)}, bf16[256,512]{1,0:T(8,128)(2,1)S(1)}, u32[]{:S(2)}, u32[]{:S(2)}) collective-permute-start(bf16[256,512]{1,0:T(8,128)(2,1)} %bitcast.17), channel_id=1, source_target_pairs={{0,4},{1,3},{4,8},{5,1},{8,12},{9,5},{12,14},{13,9},{14,10},{15,13... | collective-permute-start | bytes 786440 | tf_op jit(solution)/shard_map/ppermute | solution.py:48
  4.9 0.0 copy-start
  4.9 0.0 copy-start.2
  4.9 2.1 %difference.2.own.mine.steps0 = bf16[784,512]{1,0:T(8,128)(2,1)S(1)} custom-call(f32[1024,512]{1,0:T(8,128)} %bitcast.8, f32[1024,512]{1,0:T(8,128)} %bitcast.12, s32[1,1]{1,0:T(1,128)} %bitcast.7.refs_0_), custom_call_target="tpu_custom_call" | custom-call | flops 786432 | bytes 3932160 | tf_op jit(solution)/shard_map/difference/pallas_call | solution.py:107
  7.0 0.0 copy-start.1
  7.0 0.0 copy-start.4
  7.0 1.6 %collective-permute-start.8 = (bf16[784,512]{1,0:T(8,128)(2,1)S(1)}, bf16[784,512]{1,0:T(8,128)(2,1)S(1)}, u32[]{:S(2)}, u32[]{:S(2)}) collective-permute-start(bf16[784,512]{1,0:T(8,128)(2,1)S(1)} %difference.2.own.mine.steps0), channel_id=1, source_target_pairs={{0,16},{16,0},{1,17},{17,1},{2,18},{18,2},{3,19},{19,3},{4,20},{20... | collective-permute-start | bytes 2408456 | tf_op jit(solution)/shard_map/ppermute | solution.py:57
  8.6 0.0 collective-permute-done.3
  8.6 0.0 collective-permute-done.2.sib
  8.6 1.6 %collective-permute-start.4 = (bf16[256,512]{1,0:T(8,128)(2,1)S(1)}, bf16[256,512]{1,0:T(8,128)(2,1)S(1)}, u32[]{:S(2)}, u32[]{:S(2)}) collective-permute-start(bf16[256,512]{1,0:T(8,128)(2,1)S(1)} %collective-permute-done.3), channel_id=1, source_target_pairs={{0,4},{1,3},{4,8},{5,1},{8,12},{9,5},{12,14},{13,9},{14,10},{15,13... | collective-permute-start | bytes 786440 | tf_op jit(solution)/shard_map/ppermute | solution.py:48
  10.2 0.0 collective-permute-done.refs_1_
  10.2 1.6 %collective-permute-start.1 = (bf16[256,512]{1,0:T(8,128)(2,1)S(1)}, bf16[256,512]{1,0:T(8,128)(2,1)S(1)}, u32[]{:S(2)}, u32[]{:S(2)}) collective-permute-start(bf16[256,512]{1,0:T(8,128)(2,1)S(1)} %collective-permute-done.refs_1_), channel_id=1, source_target_pairs={{0,4},{1,3},{4,8},{5,1},{8,12},{9,5},{12,14},{13,9},{14,10},{15,13... | collective-permute-start | bytes 786440 | tf_op jit(solution)/shard_map/ppermute | solution.py:48
  11.7 0.0 copy-done
  11.7 0.0 copy-done.2
  11.7 0.1 difference.3.diff
  11.9 3.1 %collective-permute-done.4.refs_2_ = bf16[256,512]{1,0:T(8,128)(2,1)S(1)} collective-permute-done((bf16[256,512]{1,0:T(8,128)(2,1)S(1)}, bf16[256,512]{1,0:T(8,128)(2,1)S(1)}, u32[]{:S(2)}, u32[]{:S(2)}) %collective-permute-start.4) | collective-permute-done | bytes 262176 | tf_op jit(solution)/shard_map/ppermute | solution.py:48
  15.0 1.6 %collective-permute-start.6 = (bf16[256,512]{1,0:T(8,128)(2,1)S(1)}, bf16[256,512]{1,0:T(8,128)(2,1)S(1)}, u32[]{:S(2)}, u32[]{:S(2)}) collective-permute-start(bf16[256,512]{1,0:T(8,128)(2,1)S(1)} %collective-permute-done.4.refs_2_), channel_id=1, source_target_pairs={{0,4},{1,3},{4,8},{5,1},{8,12},{9,5},{12,14},{13,9},{14,10},{15,13... | collective-permute-start | bytes 786440 | tf_op jit(solution)/shard_map/ppermute | solution.py:48
  16.5 0.0 copy-done.1
  16.5 0.0 copy-done.4
  16.5 0.6 %partial_keys.3 = (f32[256,512]{1,0:T(8,128)S(1)}, f32[256,512]{1,0:T(8,128)S(1)}) custom-call(bf16[256,4096]{1,0:T(8,128)(2,1)S(1)} %copy-done.1, bf16[256,4096]{1,0:T(8,128)(2,1)S(1)} %collective-permute-done.2.sib, bf16[256,512]{1,0:T(8,128)(2,1)S(1)} %bitcast.18, bf16[256,512]{1,0:T(8,128)(2,1)S(1)} %collective-permute-done.refs_1_, ...), custom_call_target="tpu_custom_call" | custom-call | tf_op jit(solution)/shard_map/partial_keys/pallas_call | solution.py:184
  17.1 0.7 %collective-permute-done.1.refs_0_ = bf16[256,512]{1,0:T(8,128)(2,1)S(1)} collective-permute-done((bf16[256,512]{1,0:T(8,128)(2,1)S(1)}, bf16[256,512]{1,0:T(8,128)(2,1)S(1)}, u32[]{:S(2)}, u32[]{:S(2)}) %collective-permute-start.1) | collective-permute-done | bytes 262176 | tf_op jit(solution)/shard_map/ppermute | solution.py:48
  17.8 1.6 %collective-permute-start.5 = (bf16[256,512]{1,0:T(8,128)(2,1)S(1)}, bf16[256,512]{1,0:T(8,128)(2,1)S(1)}, u32[]{:S(2)}, u32[]{:S(2)}) collective-permute-start(bf16[256,512]{1,0:T(8,128)(2,1)S(1)} %collective-permute-done.1.refs_0_), channel_id=1, source_target_pairs={{0,4},{1,3},{4,8},{5,1},{8,12},{9,5},{12,14},{13,9},{14,10},{15,13... | collective-permute-start | bytes 786440 | tf_op jit(solution)/shard_map/ppermute | solution.py:48
  19.3 2.0 %collective-permute-done.6.refs_1_ = bf16[256,512]{1,0:T(8,128)(2,1)S(1)} collective-permute-done((bf16[256,512]{1,0:T(8,128)(2,1)S(1)}, bf16[256,512]{1,0:T(8,128)(2,1)S(1)}, u32[]{:S(2)}, u32[]{:S(2)}) %collective-permute-start.6) | collective-permute-done | bytes 262176 | tf_op jit(solution)/shard_map/ppermute | solution.py:48
  21.3 1.6 %collective-permute-start.9 = (bf16[256,512]{1,0:T(8,128)(2,1)S(1)}, bf16[256,512]{1,0:T(8,128)(2,1)S(1)}, u32[]{:S(2)}, u32[]{:S(2)}) collective-permute-start(bf16[256,512]{1,0:T(8,128)(2,1)S(1)} %collective-permute-done.6.refs_1_), channel_id=1, source_target_pairs={{0,4},{1,3},{4,8},{5,1},{8,12},{9,5},{12,14},{13,9},{14,10},{15,13... | collective-permute-start | bytes 786440 | tf_op jit(solution)/shard_map/ppermute | solution.py:48
  22.9 0.4 %partial_keys.4 = (f32[256,512]{1,0:T(8,128)S(1)}, f32[256,512]{1,0:T(8,128)S(1)}) custom-call(bf16[256,4096]{1,0:T(8,128)(2,1)S(1)} %copy-done.1, bf16[256,4096]{1,0:T(8,128)(2,1)S(1)} %collective-permute-done.2.sib, bf16[256,512]{1,0:T(8,128)(2,1)S(1)} %collective-permute-done.1.refs_0_, bf16[256,512]{1,0:T(8,128)(2,1)S(1)} %collective-permute-done.6.refs_1_, ...), custom_call_target="tpu_custom_call" | custom-call | tf_op jit(solution)/shard_map/partial_keys/pallas_call | solution.py:184
  23.3 0.8 %collective-permute-done.5.refs_0_ = bf16[256,512]{1,0:T(8,128)(2,1)S(1)} collective-permute-done((bf16[256,512]{1,0:T(8,128)(2,1)S(1)}, bf16[256,512]{1,0:T(8,128)(2,1)S(1)}, u32[]{:S(2)}, u32[]{:S(2)}) %collective-permute-start.5) | collective-permute-done | bytes 262176 | tf_op jit(solution)/shard_map/ppermute | solution.py:48
  24.1 0.0 copy-start.3
  24.1 1.6 %collective-permute-start.7 = (bf16[256,512]{1,0:T(8,128)(2,1)S(1)}, bf16[256,512]{1,0:T(8,128)(2,1)S(1)}, u32[]{:S(2)}, u32[]{:S(2)}) collective-permute-start(bf16[256,512]{1,0:T(8,128)(2,1)S(1)} %collective-permute-done.5.refs_0_), channel_id=1, source_target_pairs={{0,4},{1,3},{4,8},{5,1},{8,12},{9,5},{12,14},{13,9},{14,10},{15,13... | collective-permute-start | bytes 786440 | tf_op jit(solution)/shard_map/ppermute | solution.py:48
  25.7 0.5 %collective-permute-start.12 = (bf16[256,512]{1,0:T(8,128)(2,1)S(1)}, bf16[256,512]{1,0:T(8,128)(2,1)S(1)}, u32[]{:S(2)}, u32[]{:S(2)}) collective-permute-start(bf16[256,512]{1,0:T(8,128)(2,1)S(1)} %difference.3.diff), channel_id=1, source_target_pairs={{0,16},{16,0},{1,17},{17,1},{2,18},{18,2},{3,19},{19,3},{4,20},{20... | collective-permute-start | bytes 786440 | tf_op jit(solution)/shard_map/ppermute | solution.py:57
  26.2 1.4 %collective-permute-done.9.refs_1_ = bf16[256,512]{1,0:T(8,128)(2,1)S(1)} collective-permute-done((bf16[256,512]{1,0:T(8,128)(2,1)S(1)}, bf16[256,512]{1,0:T(8,128)(2,1)S(1)}, u32[]{:S(2)}, u32[]{:S(2)}) %collective-permute-start.9) | collective-permute-done | bytes 262176 | tf_op jit(solution)/shard_map/ppermute | solution.py:48
  27.7 0.4 %partial_keys.5 = (f32[256,512]{1,0:T(8,128)S(1)}, bf16[256,512]{1,0:T(8,128)(2,1)S(1)}) custom-call(bf16[256,4096]{1,0:T(8,128)(2,1)S(1)} %copy-done.1, bf16[256,4096]{1,0:T(8,128)(2,1)S(1)} %collective-permute-done.2.sib, bf16[256,512]{1,0:T(8,128)(2,1)S(1)} %collective-permute-done.5.refs_0_, bf16[256,512]{1,0:T(8,128)(2,1)S(1)} %collective-permute-done.9.refs_1_, ...), custom_call_target="tpu_custom_call" | custom-call | tf_op jit(solution)/shard_map/partial_keys/pallas_call | solution.py:184
  28.1 0.0 collective-permute-done.8.got.theirs.steps1
  28.1 0.1 collective-permute-start.11
  28.2 0.0 copy-done.3
  28.2 1.9 %outer_step.1 = (f32[1024,512]{1,0:T(8,128)}, f32[1024,512]{1,0:T(8,128)}) custom-call(f32[1024,512]{1,0:T(8,128)S(1)} %bitcast.10, f32[1024,512]{1,0:T(8,128)S(1)} %bitcast.14, bf16[784,512]{1,0:T(8,128)(2,1)S(1)} %difference.2.own.mine.steps0, bf16[784,512]{1,0:T(8,128)(2,1)S(1)} %collective-permute-done.8.got.theirs.steps1, ...), custom_call_target="tpu_custom_call" | custom-call | flops 3932160 | bytes 7864320 | tf_op jit(solution)/shard_map/outer_step/pallas_call | solution.py:137
  30.1 0.4 %collective-permute-done.7.mine = bf16[256,512]{1,0:T(8,128)(2,1)S(1)} collective-permute-done((bf16[256,512]{1,0:T(8,128)(2,1)S(1)}, bf16[256,512]{1,0:T(8,128)(2,1)S(1)}, u32[]{:S(2)}, u32[]{:S(2)}) %collective-permute-start.7) | collective-permute-done | bytes 262176 | tf_op jit(solution)/shard_map/ppermute | solution.py:48
  30.5 0.1 collective-permute-start.10
  30.6 1.6 %collective-permute-done.12.sent = bf16[256,512]{1,0:T(8,128)(2,1)S(1)} collective-permute-done((bf16[256,512]{1,0:T(8,128)(2,1)S(1)}, bf16[256,512]{1,0:T(8,128)(2,1)S(1)}, u32[]{:S(2)}, u32[]{:S(2)}) %collective-permute-start.12) | collective-permute-done | bytes 262176 | tf_op jit(solution)/shard_map/ppermute | solution.py:57
  32.2 0.0 collective-permute-done.11.got
  32.2 0.0 collective-permute-done.10.other
  32.2 1.6 %close.1 = (bf16[256,512]{1,0:T(8,128)(2,1)}, f32[1024,512]{1,0:T(8,128)}, f32[1024,512]{1,0:T(8,128)}) custom-call(bf16[256,4096]{1,0:T(8,128)(2,1)S(1)} %copy-done.1, bf16[256,512]{1,0:T(8,128)(2,1)S(1)} %collective-permute-done.7.mine, bf16[256,512]{1,0:T(8,128)(2,1)S(1)} %collective-permute-done.10.other, ...), custom_call_target="tpu_custom_call", output_to_operand_aliasing={{1}: (11, {}), {2}: (12, {})} | custom-call | tf_op jit(solution)/shard_map/close/pallas_call | solution.py:232
Async XLA Ops:
  0.6 7.9 %collective-permute-start.2 = (bf16[256,4096]{1,0:T(8,128)(2,1)}, bf16[256,4096]{1,0:T(8,128)(2,1)S(1)}, u32[]{:S(2)}, u32[]{:S(2)}) collective-permute-start(bf16[256,4096]{1,0:T(8,128)(2,1)} %act.7), channel_id=1, source_target_pairs={{0,1},{1,0},{2,3},{3,2},{4,5},{5,4},{6,7},{7,6},{8,9},{9,8},{10,11... | collective-permute-start | bytes 6291464 | tf_op jit(solution)/shard_map/ppermute | solution.py:53
  1.1 7.4 %collective-permute-start.3 = (bf16[256,512]{1,0:T(8,128)(2,1)}, bf16[256,512]{1,0:T(8,128)(2,1)S(1)}, u32[]{:S(2)}, u32[]{:S(2)}) collective-permute-start(bf16[256,512]{1,0:T(8,128)(2,1)} %bitcast.16), channel_id=1, source_target_pairs={{0,1},{1,0},{2,3},{3,2},{4,5},{5,4},{6,7},{7,6},{8,9},{9,8},{10,11... | collective-permute-start | bytes 786440 | tf_op jit(solution)/shard_map/ppermute | solution.py:53
  1.2 8.9 %collective-permute-start = (bf16[256,512]{1,0:T(8,128)(2,1)}, bf16[256,512]{1,0:T(8,128)(2,1)S(1)}, u32[]{:S(2)}, u32[]{:S(2)}) collective-permute-start(bf16[256,512]{1,0:T(8,128)(2,1)} %bitcast.17), channel_id=1, source_target_pairs={{0,4},{1,3},{4,8},{5,1},{8,12},{9,5},{12,14},{13,9},{14,10},{15,13... | collective-permute-start | bytes 786440 | tf_op jit(solution)/shard_map/ppermute | solution.py:48
  4.9 6.9 %copy-start = (f32[2,2,256,512]{3,2,1,0:T(8,128)S(1)}, f32[2,2,256,512]{3,2,1,0:T(8,128)}, u32[]{:S(2)}) copy-start(f32[2,2,256,512]{3,2,1,0:T(8,128)} %param.9) | copy-start | bytes 6291460
  4.9 6.8 %copy-start.2 = (f32[1,2,2,256,512]{4,3,2,1,0:T(8,128)S(1)}, f32[1,2,2,256,512]{4,3,2,1,0:T(8,128)}, u32[]{:S(2)}) copy-start(f32[1,2,2,256,512]{4,3,2,1,0:T(8,128)} %param.8) | copy-start | bytes 6291460
  7.0 9.5 %copy-start.1 = (bf16[256,4096]{1,0:T(8,128)(2,1)S(1)}, bf16[256,4096]{1,0:T(8,128)(2,1)}, u32[]{:S(2)}) copy-start(bf16[256,4096]{1,0:T(8,128)(2,1)} %act.7) | copy-start | bytes 6291460
  7.0 9.5 %copy-start.4 = (bf16[1,256,512]{2,1,0:T(8,128)(2,1)S(1)}, bf16[1,256,512]{2,1,0:T(8,128)(2,1)}, u32[]{:S(2)}) copy-start(bf16[1,256,512]{2,1,0:T(8,128)(2,1)} %param.7) | copy-start | bytes 786436
  7.0 21.1 %collective-permute-start.8 = (bf16[784,512]{1,0:T(8,128)(2,1)S(1)}, bf16[784,512]{1,0:T(8,128)(2,1)S(1)}, u32[]{:S(2)}, u32[]{:S(2)}) collective-permute-start(bf16[784,512]{1,0:T(8,128)(2,1)S(1)} %difference.2.own.mine.steps0), channel_id=1, source_target_pairs={{0,16},{16,0},{1,17},{17,1},{2,18},{18,2},{3,19},{19,3},{4,20},{20... | collective-permute-start | bytes 2408456 | tf_op jit(solution)/shard_map/ppermute | solution.py:57
  8.6 6.4 %collective-permute-start.4 = (bf16[256,512]{1,0:T(8,128)(2,1)S(1)}, bf16[256,512]{1,0:T(8,128)(2,1)S(1)}, u32[]{:S(2)}, u32[]{:S(2)}) collective-permute-start(bf16[256,512]{1,0:T(8,128)(2,1)S(1)} %collective-permute-done.3), channel_id=1, source_target_pairs={{0,4},{1,3},{4,8},{5,1},{8,12},{9,5},{12,14},{13,9},{14,10},{15,13... | collective-permute-start | bytes 786440 | tf_op jit(solution)/shard_map/ppermute | solution.py:48
  10.2 7.6 %collective-permute-start.1 = (bf16[256,512]{1,0:T(8,128)(2,1)S(1)}, bf16[256,512]{1,0:T(8,128)(2,1)S(1)}, u32[]{:S(2)}, u32[]{:S(2)}) collective-permute-start(bf16[256,512]{1,0:T(8,128)(2,1)S(1)} %collective-permute-done.refs_1_), channel_id=1, source_target_pairs={{0,4},{1,3},{4,8},{5,1},{8,12},{9,5},{12,14},{13,9},{14,10},{15,13... | collective-permute-start | bytes 786440 | tf_op jit(solution)/shard_map/ppermute | solution.py:48
  15.0 6.4 %collective-permute-start.6 = (bf16[256,512]{1,0:T(8,128)(2,1)S(1)}, bf16[256,512]{1,0:T(8,128)(2,1)S(1)}, u32[]{:S(2)}, u32[]{:S(2)}) collective-permute-start(bf16[256,512]{1,0:T(8,128)(2,1)S(1)} %collective-permute-done.4.refs_2_), channel_id=1, source_target_pairs={{0,4},{1,3},{4,8},{5,1},{8,12},{9,5},{12,14},{13,9},{14,10},{15,13... | collective-permute-start | bytes 786440 | tf_op jit(solution)/shard_map/ppermute | solution.py:48
  17.8 6.4 %collective-permute-start.5 = (bf16[256,512]{1,0:T(8,128)(2,1)S(1)}, bf16[256,512]{1,0:T(8,128)(2,1)S(1)}, u32[]{:S(2)}, u32[]{:S(2)}) collective-permute-start(bf16[256,512]{1,0:T(8,128)(2,1)S(1)} %collective-permute-done.1.refs_0_), channel_id=1, source_target_pairs={{0,4},{1,3},{4,8},{5,1},{8,12},{9,5},{12,14},{13,9},{14,10},{15,13... | collective-permute-start | bytes 786440 | tf_op jit(solution)/shard_map/ppermute | solution.py:48
  21.3 6.4 %collective-permute-start.9 = (bf16[256,512]{1,0:T(8,128)(2,1)S(1)}, bf16[256,512]{1,0:T(8,128)(2,1)S(1)}, u32[]{:S(2)}, u32[]{:S(2)}) collective-permute-start(bf16[256,512]{1,0:T(8,128)(2,1)S(1)} %collective-permute-done.6.refs_1_), channel_id=1, source_target_pairs={{0,4},{1,3},{4,8},{5,1},{8,12},{9,5},{12,14},{13,9},{14,10},{15,13... | collective-permute-start | bytes 786440 | tf_op jit(solution)/shard_map/ppermute | solution.py:48
  24.1 4.1 %copy-start.3 = (f32[2,2,256,512]{3,2,1,0:T(8,128)S(1)}, f32[2,2,256,512]{3,2,1,0:T(8,128)}, u32[]{:S(2)}) copy-start(f32[2,2,256,512]{3,2,1,0:T(8,128)} %param.10) | copy-start | bytes 6291460
  24.1 6.4 %collective-permute-start.7 = (bf16[256,512]{1,0:T(8,128)(2,1)S(1)}, bf16[256,512]{1,0:T(8,128)(2,1)S(1)}, u32[]{:S(2)}, u32[]{:S(2)}) collective-permute-start(bf16[256,512]{1,0:T(8,128)(2,1)S(1)} %collective-permute-done.5.refs_0_), channel_id=1, source_target_pairs={{0,4},{1,3},{4,8},{5,1},{8,12},{9,5},{12,14},{13,9},{14,10},{15,13... | collective-permute-start | bytes 786440 | tf_op jit(solution)/shard_map/ppermute | solution.py:48
  25.7 6.5 %collective-permute-start.12 = (bf16[256,512]{1,0:T(8,128)(2,1)S(1)}, bf16[256,512]{1,0:T(8,128)(2,1)S(1)}, u32[]{:S(2)}, u32[]{:S(2)}) collective-permute-start(bf16[256,512]{1,0:T(8,128)(2,1)S(1)} %difference.3.diff), channel_id=1, source_target_pairs={{0,16},{16,0},{1,17},{17,1},{2,18},{18,2},{3,19},{19,3},{4,20},{20... | collective-permute-start | bytes 786440 | tf_op jit(solution)/shard_map/ppermute | solution.py:57
  28.1 4.1 %collective-permute-start.11 = (bf16[256,512]{1,0:T(8,128)(2,1)S(1)}, bf16[256,512]{1,0:T(8,128)(2,1)S(1)}, u32[]{:S(2)}, u32[]{:S(2)}) collective-permute-start(bf16[256,512]{1,0:T(8,128)(2,1)S(1)} %get-tuple-element.48), channel_id=1, source_target_pairs={{0,1},{1,0},{2,3},{3,2},{4,5},{5,4},{6,7},{7,6},{8,9},{9,8},{10,11... | collective-permute-start | bytes 786440 | tf_op jit(solution)/shard_map/ppermute | solution.py:53
  30.5 1.7 %collective-permute-start.10 = (bf16[256,512]{1,0:T(8,128)(2,1)S(1)}, bf16[256,512]{1,0:T(8,128)(2,1)S(1)}, u32[]{:S(2)}, u32[]{:S(2)}) collective-permute-start(bf16[256,512]{1,0:T(8,128)(2,1)S(1)} %collective-permute-done.7.mine), channel_id=1, source_target_pairs={{0,1},{1,0},{2,3},{3,2},{4,5},{5,4},{6,7},{7,6},{8,9},{9,8},{10,11... | collective-permute-start | bytes 786440 | tf_op jit(solution)/shard_map/ppermute | solution.py:53

commit v6 on v5

--- a/solution.py
+++ b/solution.py
@@ -215,12 +215,18 @@
     average = (ours * scale) * diff[...].astype(F32) + (theirs * scale) * sent[...].astype(F32)
     for copy in loads:
         copy.wait()
-    momentum = 0.9 * loaded[1] + average
-    stored[1] = momentum
-    stored[0] = loaded[0] - 0.7 * (average + 0.9 * momentum)
-    for i, ref in enumerate((new_base, new_mom)):
-        stores.append(pltpu.make_async_copy(stored.at[i], ref.at[part, :], sems.at[3 + i]))
-        stores[-1].start()
+    half = rows // 2
+    for j in range(2):
+        cut = slice(j * half, (j + 1) * half)
+        here, there = pl.ds(j * half, half), pl.ds(at + j * half, half)
+        momentum = 0.9 * loaded[1, here, :] + average[cut]
+        stored[1, here, :] = momentum
+        stored[0, here, :] = loaded[0, here, :] - 0.7 * (average[cut] + 0.9 * momentum)
+        for i, ref in enumerate((new_base, new_mom)):
+            stores.append(
+                pltpu.make_async_copy(stored.at[i, here, :], ref.at[there, :], sems.at[3 + 2 * j + i])
+            )
+            stores[-1].start()
     for copy in stores:
         copy.wait()
 
@@ -239,7 +245,7 @@
             pltpu.VMEM((2, rows, width), F32),
             pltpu.VMEM((2, rows, width), F32),
             pltpu.VMEM((tokens, width), BF16),
-            pltpu.SemaphoreType.DMA((5,)),
+            pltpu.SemaphoreType.DMA((7,)),
         ],
         compiler_params=params(),
         cost_estimate=cost(0, 0),
@@ -257,12 +263,12 @@
     n1 = rows * 4 // 16
     n0 = rows - n1
     sib = send_core(activations)
-    (own0,) = difference(base, local, 0, (n0,), 3, (inner_steps.reshape(1, 1),))
+    (own0,) = difference(base, local, 0, (n0,), 6, (inner_steps.reshape(1, 1),))
     (own1,) = difference(tie(base, own0)[0], local, n0, (n1,), 1)
     got0 = send_x(own0)
     a1 = cycle(w)
     wsib = send_core(w)
-    b1 = cycle(tie(wsib, sib, own0)[0])
+    b1 = cycle(tie(wsib, own0)[0])
     a2 = cycle(a1)
     b1, own1 = tie(b1, own1)
     got1 = send_x(own1)

time: 34.1 us -> 34 us (level)
  transfers between devices with their start and end apart: 13 -> 13, of which waited for: 7 -> 7; matrix products, arithmetic and copies ran while one was open for 0% -> 0% of each run, Pallas kernels for 16% -> 17%
where the time goes in v6:
time: 34 us; the launch traced here: 33.8 us
  starting transfers between devices  15.3 us (45%)
  waiting for transfers between devices  9.96 us (29%)
  Pallas kernels  7.16 us (21%)
  between operations  1.39 us (4%)
    ppermute x7, starting transfers between devices, cycle(): return lax.ppermute(x, 'fsdp', pairs)  12.5 us
    ppermute x7, waiting for transfers between devices, cycle(): return lax.ppermute(x, 'fsdp', pairs)  8.3 us
    pallas_call x2, Pallas kernels, difference(): pl.pallas_call(functools.partial(difference_kernel, at, tuple(sizes), pie...  2.24 us
    ppermute x2, starting transfers between devices, send_x(): return lax.ppermute(x, 'replica', [(0, 1), (1, 0)])  2.09 us
    pallas_call x1, Pallas kernels, outer(): pl.pallas_call(outer_kernel, out_shape=(shape, shape), grid=(rows // bloc...  1.9 us
    ppermute x2, waiting for transfers between devices, send_x(): return lax.ppermute(x, 'replica', [(0, 1), (1, 0)])  1.65 us
    pallas_call x1, Pallas kernels, close(): pl.pallas_call(functools.partial(close_kernel, at), out_shape=(jax.ShapeD...  1.58 us
    pallas_call x3, Pallas kernels, partial_sums(): pl.pallas_call(functools.partial(partial_kernel, blocks, not state), out_...  1.44 us
  transfers between devices with their start and end apart: 13, of which 7 were waited for; matrix products, arithmetic and copies ran while one was open for 0% of the time, Pallas kernels for 17%

profile of v6, /device:TPU:0, one launch (start us, length us, event | category | flops | bytes accessed | tf_op | source)
XLA Modules:
  0.0 33.8 jit_solution(11351787467459982609)
XLA Ops:
  0.6 0.5 %collective-permute-start.2 = (bf16[256,4096]{1,0:T(8,128)(2,1)}, bf16[256,4096]{1,0:T(8,128)(2,1)S(1)}, u32[]{:S(2)}, u32[]{:S(2)}) collective-permute-start(bf16[256,4096]{1,0:T(8,128)(2,1)} %act.7), channel_id=1, source_target_pairs={{0,1},{1,0},{2,3},{3,2},{4,5},{5,4},{6,7},{7,6},{8,9},{9,8},{10,11... | collective-permute-start | bytes 6291464 | tf_op jit(solution)/shard_map/ppermute | solution.py:53
  1.1 0.1 collective-permute-start.3
  1.2 3.0 %collective-permute-start = (bf16[256,512]{1,0:T(8,128)(2,1)}, bf16[256,512]{1,0:T(8,128)(2,1)S(1)}, u32[]{:S(2)}, u32[]{:S(2)}) collective-permute-start(bf16[256,512]{1,0:T(8,128)(2,1)} %bitcast.17), channel_id=1, source_target_pairs={{0,4},{1,3},{4,8},{5,1},{8,12},{9,5},{12,14},{13,9},{14,10},{15,13... | collective-permute-start | bytes 786440 | tf_op jit(solution)/shard_map/ppermute | solution.py:48
  4.9 0.0 copy-start
  4.9 0.0 copy-start.2
  4.9 2.1 %difference.2.own.mine.steps0 = bf16[784,512]{1,0:T(8,128)(2,1)S(1)} custom-call(f32[1024,512]{1,0:T(8,128)} %bitcast.8, f32[1024,512]{1,0:T(8,128)} %bitcast.12, s32[1,1]{1,0:T(1,128)} %bitcast.7.refs_0_), custom_call_target="tpu_custom_call" | custom-call | flops 786432 | bytes 3932160 | tf_op jit(solution)/shard_map/difference/pallas_call | solution.py:107
  7.0 0.0 copy-start.1
  7.0 0.0 copy-start.4
  7.0 1.6 %collective-permute-start.8 = (bf16[784,512]{1,0:T(8,128)(2,1)S(1)}, bf16[784,512]{1,0:T(8,128)(2,1)S(1)}, u32[]{:S(2)}, u32[]{:S(2)}) collective-permute-start(bf16[784,512]{1,0:T(8,128)(2,1)S(1)} %difference.2.own.mine.steps0), channel_id=1, source_target_pairs={{0,16},{16,0},{1,17},{17,1},{2,18},{18,2},{3,19},{19,3},{4,20},{20... | collective-permute-start | bytes 2408456 | tf_op jit(solution)/shard_map/ppermute | solution.py:57
  8.6 0.0 collective-permute-done.3
  8.6 1.6 %collective-permute-start.4 = (bf16[256,512]{1,0:T(8,128)(2,1)S(1)}, bf16[256,512]{1,0:T(8,128)(2,1)S(1)}, u32[]{:S(2)}, u32[]{:S(2)}) collective-permute-start(bf16[256,512]{1,0:T(8,128)(2,1)S(1)} %collective-permute-done.3), channel_id=1, source_target_pairs={{0,4},{1,3},{4,8},{5,1},{8,12},{9,5},{12,14},{13,9},{14,10},{15,13... | collective-permute-start | bytes 786440 | tf_op jit(solution)/shard_map/ppermute | solution.py:48
  10.2 0.0 collective-permute-done.refs_1_
  10.2 1.6 %collective-permute-start.1 = (bf16[256,512]{1,0:T(8,128)(2,1)S(1)}, bf16[256,512]{1,0:T(8,128)(2,1)S(1)}, u32[]{:S(2)}, u32[]{:S(2)}) collective-permute-start(bf16[256,512]{1,0:T(8,128)(2,1)S(1)} %collective-permute-done.refs_1_), channel_id=1, source_target_pairs={{0,4},{1,3},{4,8},{5,1},{8,12},{9,5},{12,14},{13,9},{14,10},{15,13... | collective-permute-start | bytes 786440 | tf_op jit(solution)/shard_map/ppermute | solution.py:48
  11.7 0.0 copy-done
  11.8 0.0 copy-done.2
  11.8 0.1 difference.3.diff
  11.9 3.1 %collective-permute-done.4.refs_2_ = bf16[256,512]{1,0:T(8,128)(2,1)S(1)} collective-permute-done((bf16[256,512]{1,0:T(8,128)(2,1)S(1)}, bf16[256,512]{1,0:T(8,128)(2,1)S(1)}, u32[]{:S(2)}, u32[]{:S(2)}) %collective-permute-start.4) | collective-permute-done | bytes 262176 | tf_op jit(solution)/shard_map/ppermute | solution.py:48
  15.0 1.6 %collective-permute-start.6 = (bf16[256,512]{1,0:T(8,128)(2,1)S(1)}, bf16[256,512]{1,0:T(8,128)(2,1)S(1)}, u32[]{:S(2)}, u32[]{:S(2)}) collective-permute-start(bf16[256,512]{1,0:T(8,128)(2,1)S(1)} %collective-permute-done.4.refs_2_), channel_id=1, source_target_pairs={{0,4},{1,3},{4,8},{5,1},{8,12},{9,5},{12,14},{13,9},{14,10},{15,13... | collective-permute-start | bytes 786440 | tf_op jit(solution)/shard_map/ppermute | solution.py:48
  16.5 0.0 collective-permute-done.2.sib
  16.5 0.0 copy-done.1
  16.5 0.0 copy-done.4
  16.6 0.6 %partial_keys.3 = (f32[256,512]{1,0:T(8,128)S(1)}, f32[256,512]{1,0:T(8,128)S(1)}) custom-call(bf16[256,4096]{1,0:T(8,128)(2,1)S(1)} %copy-done.1, bf16[256,4096]{1,0:T(8,128)(2,1)S(1)} %collective-permute-done.2.sib, bf16[256,512]{1,0:T(8,128)(2,1)S(1)} %bitcast.18, bf16[256,512]{1,0:T(8,128)(2,1)S(1)} %collective-permute-done.refs_1_, ...), custom_call_target="tpu_custom_call" | custom-call | tf_op jit(solution)/shard_map/partial_keys/pallas_call | solution.py:184
  17.1 0.6 %collective-permute-done.1.refs_0_ = bf16[256,512]{1,0:T(8,128)(2,1)S(1)} collective-permute-done((bf16[256,512]{1,0:T(8,128)(2,1)S(1)}, bf16[256,512]{1,0:T(8,128)(2,1)S(1)}, u32[]{:S(2)}, u32[]{:S(2)}) %collective-permute-start.1) | collective-permute-done | bytes 262176 | tf_op jit(solution)/shard_map/ppermute | solution.py:48
  17.8 1.6 %collective-permute-start.5 = (bf16[256,512]{1,0:T(8,128)(2,1)S(1)}, bf16[256,512]{1,0:T(8,128)(2,1)S(1)}, u32[]{:S(2)}, u32[]{:S(2)}) collective-permute-start(bf16[256,512]{1,0:T(8,128)(2,1)S(1)} %collective-permute-done.1.refs_0_), channel_id=1, source_target_pairs={{0,4},{1,3},{4,8},{5,1},{8,12},{9,5},{12,14},{13,9},{14,10},{15,13... | collective-permute-start | bytes 786440 | tf_op jit(solution)/shard_map/ppermute | solution.py:48
  19.3 2.0 %collective-permute-done.6.refs_1_ = bf16[256,512]{1,0:T(8,128)(2,1)S(1)} collective-permute-done((bf16[256,512]{1,0:T(8,128)(2,1)S(1)}, bf16[256,512]{1,0:T(8,128)(2,1)S(1)}, u32[]{:S(2)}, u32[]{:S(2)}) %collective-permute-start.6) | collective-permute-done | bytes 262176 | tf_op jit(solution)/shard_map/ppermute | solution.py:48
  21.3 1.6 %collective-permute-start.9 = (bf16[256,512]{1,0:T(8,128)(2,1)S(1)}, bf16[256,512]{1,0:T(8,128)(2,1)S(1)}, u32[]{:S(2)}, u32[]{:S(2)}) collective-permute-start(bf16[256,512]{1,0:T(8,128)(2,1)S(1)} %collective-permute-done.6.refs_1_), channel_id=1, source_target_pairs={{0,4},{1,3},{4,8},{5,1},{8,12},{9,5},{12,14},{13,9},{14,10},{15,13... | collective-permute-start | bytes 786440 | tf_op jit(solution)/shard_map/ppermute | solution.py:48
  22.9 0.4 %partial_keys.4 = (f32[256,512]{1,0:T(8,128)S(1)}, f32[256,512]{1,0:T(8,128)S(1)}) custom-call(bf16[256,4096]{1,0:T(8,128)(2,1)S(1)} %copy-done.1, bf16[256,4096]{1,0:T(8,128)(2,1)S(1)} %collective-permute-done.2.sib, bf16[256,512]{1,0:T(8,128)(2,1)S(1)} %collective-permute-done.1.refs_0_, bf16[256,512]{1,0:T(8,128)(2,1)S(1)} %collective-permute-done.6.refs_1_, ...), custom_call_target="tpu_custom_call" | custom-call | tf_op jit(solution)/shard_map/partial_keys/pallas_call | solution.py:184
  23.4 0.8 %collective-permute-done.5.refs_0_ = bf16[256,512]{1,0:T(8,128)(2,1)S(1)} collective-permute-done((bf16[256,512]{1,0:T(8,128)(2,1)S(1)}, bf16[256,512]{1,0:T(8,128)(2,1)S(1)}, u32[]{:S(2)}, u32[]{:S(2)}) %collective-permute-start.5) | collective-permute-done | bytes 262176 | tf_op jit(solution)/shard_map/ppermute | solution.py:48
  24.1 0.0 copy-start.3
  24.1 1.6 %collective-permute-start.7 = (bf16[256,512]{1,0:T(8,128)(2,1)S(1)}, bf16[256,512]{1,0:T(8,128)(2,1)S(1)}, u32[]{:S(2)}, u32[]{:S(2)}) collective-permute-start(bf16[256,512]{1,0:T(8,128)(2,1)S(1)} %collective-permute-done.5.refs_0_), channel_id=1, source_target_pairs={{0,4},{1,3},{4,8},{5,1},{8,12},{9,5},{12,14},{13,9},{14,10},{15,13... | collective-permute-start | bytes 786440 | tf_op jit(solution)/shard_map/ppermute | solution.py:48
  25.7 0.5 %collective-permute-start.12 = (bf16[256,512]{1,0:T(8,128)(2,1)S(1)}, bf16[256,512]{1,0:T(8,128)(2,1)S(1)}, u32[]{:S(2)}, u32[]{:S(2)}) collective-permute-start(bf16[256,512]{1,0:T(8,128)(2,1)S(1)} %difference.3.diff), channel_id=1, source_target_pairs={{0,16},{16,0},{1,17},{17,1},{2,18},{18,2},{3,19},{19,3},{4,20},{20... | collective-permute-start | bytes 786440 | tf_op jit(solution)/shard_map/ppermute | solution.py:57
  26.3 1.4 %collective-permute-done.9.refs_1_ = bf16[256,512]{1,0:T(8,128)(2,1)S(1)} collective-permute-done((bf16[256,512]{1,0:T(8,128)(2,1)S(1)}, bf16[256,512]{1,0:T(8,128)(2,1)S(1)}, u32[]{:S(2)}, u32[]{:S(2)}) %collective-permute-start.9) | collective-permute-done | bytes 262176 | tf_op jit(solution)/shard_map/ppermute | solution.py:48
  27.7 0.4 %partial_keys.5 = (f32[256,512]{1,0:T(8,128)S(1)}, bf16[256,512]{1,0:T(8,128)(2,1)S(1)}) custom-call(bf16[256,4096]{1,0:T(8,128)(2,1)S(1)} %copy-done.1, bf16[256,4096]{1,0:T(8,128)(2,1)S(1)} %collective-permute-done.2.sib, bf16[256,512]{1,0:T(8,128)(2,1)S(1)} %collective-permute-done.5.refs_0_, bf16[256,512]{1,0:T(8,128)(2,1)S(1)} %collective-permute-done.9.refs_1_, ...), custom_call_target="tpu_custom_call" | custom-call | tf_op jit(solution)/shard_map/partial_keys/pallas_call | solution.py:184
  28.1 0.0 collective-permute-done.8.got.theirs.steps1
  28.2 0.1 collective-permute-start.11
  28.2 0.0 copy-done.3
  28.2 1.9 %outer_step.1 = (f32[1024,512]{1,0:T(8,128)}, f32[1024,512]{1,0:T(8,128)}) custom-call(f32[1024,512]{1,0:T(8,128)S(1)} %bitcast.10, f32[1024,512]{1,0:T(8,128)S(1)} %bitcast.14, bf16[784,512]{1,0:T(8,128)(2,1)S(1)} %difference.2.own.mine.steps0, bf16[784,512]{1,0:T(8,128)(2,1)S(1)} %collective-permute-done.8.got.theirs.steps1, ...), custom_call_target="tpu_custom_call" | custom-call | flops 3932160 | bytes 7864320 | tf_op jit(solution)/shard_map/outer_step/pallas_call | solution.py:137
  30.1 0.4 %collective-permute-done.7.mine = bf16[256,512]{1,0:T(8,128)(2,1)S(1)} collective-permute-done((bf16[256,512]{1,0:T(8,128)(2,1)S(1)}, bf16[256,512]{1,0:T(8,128)(2,1)S(1)}, u32[]{:S(2)}, u32[]{:S(2)}) %collective-permute-start.7) | collective-permute-done | bytes 262176 | tf_op jit(solution)/shard_map/ppermute | solution.py:48
  30.5 0.1 collective-permute-start.10
  30.6 1.6 %collective-permute-done.12.sent = bf16[256,512]{1,0:T(8,128)(2,1)S(1)} collective-permute-done((bf16[256,512]{1,0:T(8,128)(2,1)S(1)}, bf16[256,512]{1,0:T(8,128)(2,1)S(1)}, u32[]{:S(2)}, u32[]{:S(2)}) %collective-permute-start.12) | collective-permute-done | bytes 262176 | tf_op jit(solution)/shard_map/ppermute | solution.py:57
  32.3 0.0 collective-permute-done.11.got
  32.3 0.0 collective-permute-done.10.other
  32.3 1.6 %close.1 = (bf16[256,512]{1,0:T(8,128)(2,1)}, f32[1024,512]{1,0:T(8,128)}, f32[1024,512]{1,0:T(8,128)}) custom-call(bf16[256,4096]{1,0:T(8,128)(2,1)S(1)} %copy-done.1, bf16[256,512]{1,0:T(8,128)(2,1)S(1)} %collective-permute-done.7.mine, bf16[256,512]{1,0:T(8,128)(2,1)S(1)} %collective-permute-done.10.other, ...), custom_call_target="tpu_custom_call", output_to_operand_aliasing={{1}: (11, {}), {2}: (12, {})} | custom-call | tf_op jit(solution)/shard_map/close/pallas_call | solution.py:238
Async XLA Ops:
  0.6 15.9 %collective-permute-start.2 = (bf16[256,4096]{1,0:T(8,128)(2,1)}, bf16[256,4096]{1,0:T(8,128)(2,1)S(1)}, u32[]{:S(2)}, u32[]{:S(2)}) collective-permute-start(bf16[256,4096]{1,0:T(8,128)(2,1)} %act.7), channel_id=1, source_target_pairs={{0,1},{1,0},{2,3},{3,2},{4,5},{5,4},{6,7},{7,6},{8,9},{9,8},{10,11... | collective-permute-start | bytes 6291464 | tf_op jit(solution)/shard_map/ppermute | solution.py:53
  1.1 7.4 %collective-permute-start.3 = (bf16[256,512]{1,0:T(8,128)(2,1)}, bf16[256,512]{1,0:T(8,128)(2,1)S(1)}, u32[]{:S(2)}, u32[]{:S(2)}) collective-permute-start(bf16[256,512]{1,0:T(8,128)(2,1)} %bitcast.16), channel_id=1, source_target_pairs={{0,1},{1,0},{2,3},{3,2},{4,5},{5,4},{6,7},{7,6},{8,9},{9,8},{10,11... | collective-permute-start | bytes 786440 | tf_op jit(solution)/shard_map/ppermute | solution.py:53
  1.2 8.9 %collective-permute-start = (bf16[256,512]{1,0:T(8,128)(2,1)}, bf16[256,512]{1,0:T(8,128)(2,1)S(1)}, u32[]{:S(2)}, u32[]{:S(2)}) collective-permute-start(bf16[256,512]{1,0:T(8,128)(2,1)} %bitcast.17), channel_id=1, source_target_pairs={{0,4},{1,3},{4,8},{5,1},{8,12},{9,5},{12,14},{13,9},{14,10},{15,13... | collective-permute-start | bytes 786440 | tf_op jit(solution)/shard_map/ppermute | solution.py:48
  4.9 6.9 %copy-start = (f32[2,2,256,512]{3,2,1,0:T(8,128)S(1)}, f32[2,2,256,512]{3,2,1,0:T(8,128)}, u32[]{:S(2)}) copy-start(f32[2,2,256,512]{3,2,1,0:T(8,128)} %param.9) | copy-start | bytes 6291460
  4.9 6.9 %copy-start.2 = (f32[1,2,2,256,512]{4,3,2,1,0:T(8,128)S(1)}, f32[1,2,2,256,512]{4,3,2,1,0:T(8,128)}, u32[]{:S(2)}) copy-start(f32[1,2,2,256,512]{4,3,2,1,0:T(8,128)} %param.8) | copy-start | bytes 6291460
  7.0 9.5 %copy-start.1 = (bf16[256,4096]{1,0:T(8,128)(2,1)S(1)}, bf16[256,4096]{1,0:T(8,128)(2,1)}, u32[]{:S(2)}) copy-start(bf16[256,4096]{1,0:T(8,128)(2,1)} %act.7) | copy-start | bytes 6291460
  7.0 9.5 %copy-start.4 = (bf16[1,256,512]{2,1,0:T(8,128)(2,1)S(1)}, bf16[1,256,512]{2,1,0:T(8,128)(2,1)}, u32[]{:S(2)}) copy-start(bf16[1,256,512]{2,1,0:T(8,128)(2,1)} %param.7) | copy-start | bytes 786436
  7.0 21.1 %collective-permute-start.8 = (bf16[784,512]{1,0:T(8,128)(2,1)S(1)}, bf16[784,512]{1,0:T(8,128)(2,1)S(1)}, u32[]{:S(2)}, u32[]{:S(2)}) collective-permute-start(bf16[784,512]{1,0:T(8,128)(2,1)S(1)} %difference.2.own.mine.steps0), channel_id=1, source_target_pairs={{0,16},{16,0},{1,17},{17,1},{2,18},{18,2},{3,19},{19,3},{4,20},{20... | collective-permute-start | bytes 2408456 | tf_op jit(solution)/shard_map/ppermute | solution.py:57
  8.6 6.4 %collective-permute-start.4 = (bf16[256,512]{1,0:T(8,128)(2,1)S(1)}, bf16[256,512]{1,0:T(8,128)(2,1)S(1)}, u32[]{:S(2)}, u32[]{:S(2)}) collective-permute-start(bf16[256,512]{1,0:T(8,128)(2,1)S(1)} %collective-permute-done.3), channel_id=1, source_target_pairs={{0,4},{1,3},{4,8},{5,1},{8,12},{9,5},{12,14},{13,9},{14,10},{15,13... | collective-permute-start | bytes 786440 | tf_op jit(solution)/shard_map/ppermute | solution.py:48
  10.2 7.6 %collective-permute-start.1 = (bf16[256,512]{1,0:T(8,128)(2,1)S(1)}, bf16[256,512]{1,0:T(8,128)(2,1)S(1)}, u32[]{:S(2)}, u32[]{:S(2)}) collective-permute-start(bf16[256,512]{1,0:T(8,128)(2,1)S(1)} %collective-permute-done.refs_1_), channel_id=1, source_target_pairs={{0,4},{1,3},{4,8},{5,1},{8,12},{9,5},{12,14},{13,9},{14,10},{15,13... | collective-permute-start | bytes 786440 | tf_op jit(solution)/shard_map/ppermute | solution.py:48
  15.0 6.4 %collective-permute-start.6 = (bf16[256,512]{1,0:T(8,128)(2,1)S(1)}, bf16[256,512]{1,0:T(8,128)(2,1)S(1)}, u32[]{:S(2)}, u32[]{:S(2)}) collective-permute-start(bf16[256,512]{1,0:T(8,128)(2,1)S(1)} %collective-permute-done.4.refs_2_), channel_id=1, source_target_pairs={{0,4},{1,3},{4,8},{5,1},{8,12},{9,5},{12,14},{13,9},{14,10},{15,13... | collective-permute-start | bytes 786440 | tf_op jit(solution)/shard_map/ppermute | solution.py:48
  17.8 6.4 %collective-permute-start.5 = (bf16[256,512]{1,0:T(8,128)(2,1)S(1)}, bf16[256,512]{1,0:T(8,128)(2,1)S(1)}, u32[]{:S(2)}, u32[]{:S(2)}) collective-permute-start(bf16[256,512]{1,0:T(8,128)(2,1)S(1)} %collective-permute-done.1.refs_0_), channel_id=1, source_target_pairs={{0,4},{1,3},{4,8},{5,1},{8,12},{9,5},{12,14},{13,9},{14,10},{15,13... | collective-permute-start | bytes 786440 | tf_op jit(solution)/shard_map/ppermute | solution.py:48
  21.3 6.4 %collective-permute-start.9 = (bf16[256,512]{1,0:T(8,128)(2,1)S(1)}, bf16[256,512]{1,0:T(8,128)(2,1)S(1)}, u32[]{:S(2)}, u32[]{:S(2)}) collective-permute-start(bf16[256,512]{1,0:T(8,128)(2,1)S(1)} %collective-permute-done.6.refs_1_), channel_id=1, source_target_pairs={{0,4},{1,3},{4,8},{5,1},{8,12},{9,5},{12,14},{13,9},{14,10},{15,13... | collective-permute-start | bytes 786440 | tf_op jit(solution)/shard_map/ppermute | solution.py:48
  24.1 4.1 %copy-start.3 = (f32[2,2,256,512]{3,2,1,0:T(8,128)S(1)}, f32[2,2,256,512]{3,2,1,0:T(8,128)}, u32[]{:S(2)}) copy-start(f32[2,2,256,512]{3,2,1,0:T(8,128)} %param.10) | copy-start | bytes 6291460
  24.1 6.4 %collective-permute-start.7 = (bf16[256,512]{1,0:T(8,128)(2,1)S(1)}, bf16[256,512]{1,0:T(8,128)(2,1)S(1)}, u32[]{:S(2)}, u32[]{:S(2)}) collective-permute-start(bf16[256,512]{1,0:T(8,128)(2,1)S(1)} %collective-permute-done.5.refs_0_), channel_id=1, source_target_pairs={{0,4},{1,3},{4,8},{5,1},{8,12},{9,5},{12,14},{13,9},{14,10},{15,13... | collective-permute-start | bytes 786440 | tf_op jit(solution)/shard_map/ppermute | solution.py:48
  25.7 6.5 %collective-permute-start.12 = (bf16[256,512]{1,0:T(8,128)(2,1)S(1)}, bf16[256,512]{1,0:T(8,128)(2,1)S(1)}, u32[]{:S(2)}, u32[]{:S(2)}) collective-permute-start(bf16[256,512]{1,0:T(8,128)(2,1)S(1)} %difference.3.diff), channel_id=1, source_target_pairs={{0,16},{16,0},{1,17},{17,1},{2,18},{18,2},{3,19},{19,3},{4,20},{20... | collective-permute-start | bytes 786440 | tf_op jit(solution)/shard_map/ppermute | solution.py:57
  28.2 4.1 %collective-permute-start.11 = (bf16[256,512]{1,0:T(8,128)(2,1)S(1)}, bf16[256,512]{1,0:T(8,128)(2,1)S(1)}, u32[]{:S(2)}, u32[]{:S(2)}) collective-permute-start(bf16[256,512]{1,0:T(8,128)(2,1)S(1)} %get-tuple-element.48), channel_id=1, source_target_pairs={{0,1},{1,0},{2,3},{3,2},{4,5},{5,4},{6,7},{7,6},{8,9},{9,8},{10,11... | collective-permute-start | bytes 786440 | tf_op jit(solution)/shard_map/ppermute | solution.py:53
  30.5 1.7 %collective-permute-start.10 = (bf16[256,512]{1,0:T(8,128)(2,1)S(1)}, bf16[256,512]{1,0:T(8,128)(2,1)S(1)}, u32[]{:S(2)}, u32[]{:S(2)}) collective-permute-start(bf16[256,512]{1,0:T(8,128)(2,1)S(1)} %collective-permute-done.7.mine), channel_id=1, source_target_pairs={{0,1},{1,0},{2,3},{3,2},{4,5},{5,4},{6,7},{7,6},{8,9},{9,8},{10,11... | collective-permute-start | bytes 786440 | tf_op jit(solution)/shard_map/ppermute | solution.py:53

commit v7 on v6

--- a/solution.py
+++ b/solution.py
@@ -283,7 +283,7 @@
     own_sum, sib_sum = partial_sums(((3, True), (3, False)), activations, sib, (a3, b3), state, BF16)
     swapped = send_core(sib_sum)
     got0, own_sum = tie(got0, own_sum)
-    new = outer(base, mom, own0, got0, own0, got0, 0, n0, n0 // 2, ())
+    new = outer(base, mom, own0, got0, own0, got0, 0, n0, n0 // 3, ())
     last, *new = tie(last, *new)
     other = send_core(last)
     keys, *new = close(

time: 34 us -> 34 us (level)
  waiting for transfers between devices: 9.96 us -> 9.29 us
  transfers between devices with their start and end apart: 13 -> 13, of which waited for: 7 -> 6; matrix products, arithmetic and copies ran while one was open for 0% -> 0% of each run, Pallas kernels for 17% -> 17%
where the time goes in v7:
time: 34 us; the launch traced here: 33.8 us
  starting transfers between devices  15.6 us (46%)
  waiting for transfers between devices  9.29 us (27%)
  Pallas kernels  7.49 us (22%)
  between operations  1.39 us (4%)
    ppermute x7, starting transfers between devices, cycle(): return lax.ppermute(x, 'fsdp', pairs)  12.5 us
    ppermute x7, waiting for transfers between devices, cycle(): return lax.ppermute(x, 'fsdp', pairs)  7.97 us
    pallas_call x2, Pallas kernels, difference(): pl.pallas_call(functools.partial(difference_kernel, at, tuple(sizes), pie...  2.24 us
    pallas_call x1, Pallas kernels, outer(): pl.pallas_call(outer_kernel, out_shape=(shape, shape), grid=(rows // bloc...  2.23 us
    ppermute x2, starting transfers between devices, send_x(): return lax.ppermute(x, 'replica', [(0, 1), (1, 0)])  2.09 us
    pallas_call x1, Pallas kernels, close(): pl.pallas_call(functools.partial(close_kernel, at), out_shape=(jax.ShapeD...  1.58 us
    pallas_call x3, Pallas kernels, partial_sums(): pl.pallas_call(functools.partial(partial_kernel, blocks, not state), out_...  1.44 us
    ppermute x2, waiting for transfers between devices, send_x(): return lax.ppermute(x, 'replica', [(0, 1), (1, 0)])  1.31 us
  transfers between devices with their start and end apart: 13, of which 6 were waited for; matrix products, arithmetic and copies ran while one was open for 0% of the time, Pallas kernels for 17%

profile of v7, /device:TPU:0, one launch (start us, length us, event | category | flops | bytes accessed | tf_op | source)
XLA Modules:
  0.0 33.8 jit_solution(8223847475756806476)
XLA Ops:
  0.6 0.5 %collective-permute-start.2 = (bf16[256,4096]{1,0:T(8,128)(2,1)}, bf16[256,4096]{1,0:T(8,128)(2,1)S(1)}, u32[]{:S(2)}, u32[]{:S(2)}) collective-permute-start(bf16[256,4096]{1,0:T(8,128)(2,1)} %act.7), channel_id=1, source_target_pairs={{0,1},{1,0},{2,3},{3,2},{4,5},{5,4},{6,7},{7,6},{8,9},{9,8},{10,11... | collective-permute-start | bytes 6291464 | tf_op jit(solution)/shard_map/ppermute | solution.py:53
  1.1 0.1 collective-permute-start.3
  1.2 3.0 %collective-permute-start = (bf16[256,512]{1,0:T(8,128)(2,1)}, bf16[256,512]{1,0:T(8,128)(2,1)S(1)}, u32[]{:S(2)}, u32[]{:S(2)}) collective-permute-start(bf16[256,512]{1,0:T(8,128)(2,1)} %bitcast.17), channel_id=1, source_target_pairs={{0,4},{1,3},{4,8},{5,1},{8,12},{9,5},{12,14},{13,9},{14,10},{15,13... | collective-permute-start | bytes 786440 | tf_op jit(solution)/shard_map/ppermute | solution.py:48
  4.9 0.0 copy-start
  4.9 0.0 copy-start.2
  4.9 2.1 %difference.2.own.mine.steps0 = bf16[784,512]{1,0:T(8,128)(2,1)S(1)} custom-call(f32[1024,512]{1,0:T(8,128)} %bitcast.8, f32[1024,512]{1,0:T(8,128)} %bitcast.12, s32[1,1]{1,0:T(1,128)} %bitcast.7.refs_0_), custom_call_target="tpu_custom_call" | custom-call | flops 786432 | bytes 3932160 | tf_op jit(solution)/shard_map/difference/pallas_call | solution.py:107
  7.0 0.0 copy-start.1
  7.0 0.0 copy-start.4
  7.0 1.6 %collective-permute-start.8 = (bf16[784,512]{1,0:T(8,128)(2,1)S(1)}, bf16[784,512]{1,0:T(8,128)(2,1)S(1)}, u32[]{:S(2)}, u32[]{:S(2)}) collective-permute-start(bf16[784,512]{1,0:T(8,128)(2,1)S(1)} %difference.2.own.mine.steps0), channel_id=1, source_target_pairs={{0,16},{16,0},{1,17},{17,1},{2,18},{18,2},{3,19},{19,3},{4,20},{20... | collective-permute-start | bytes 2408456 | tf_op jit(solution)/shard_map/ppermute | solution.py:57
  8.6 0.0 collective-permute-done.3
  8.6 1.6 %collective-permute-start.4 = (bf16[256,512]{1,0:T(8,128)(2,1)S(1)}, bf16[256,512]{1,0:T(8,128)(2,1)S(1)}, u32[]{:S(2)}, u32[]{:S(2)}) collective-permute-start(bf16[256,512]{1,0:T(8,128)(2,1)S(1)} %collective-permute-done.3), channel_id=1, source_target_pairs={{0,4},{1,3},{4,8},{5,1},{8,12},{9,5},{12,14},{13,9},{14,10},{15,13... | collective-permute-start | bytes 786440 | tf_op jit(solution)/shard_map/ppermute | solution.py:48
  10.2 0.0 collective-permute-done.refs_1_
  10.2 1.6 %collective-permute-start.1 = (bf16[256,512]{1,0:T(8,128)(2,1)S(1)}, bf16[256,512]{1,0:T(8,128)(2,1)S(1)}, u32[]{:S(2)}, u32[]{:S(2)}) collective-permute-start(bf16[256,512]{1,0:T(8,128)(2,1)S(1)} %collective-permute-done.refs_1_), channel_id=1, source_target_pairs={{0,4},{1,3},{4,8},{5,1},{8,12},{9,5},{12,14},{13,9},{14,10},{15,13... | collective-permute-start | bytes 786440 | tf_op jit(solution)/shard_map/ppermute | solution.py:48
  11.7 0.0 copy-done
  11.8 0.0 copy-done.2
  11.8 0.1 difference.3.diff
  11.9 3.1 %collective-permute-done.4.refs_2_ = bf16[256,512]{1,0:T(8,128)(2,1)S(1)} collective-permute-done((bf16[256,512]{1,0:T(8,128)(2,1)S(1)}, bf16[256,512]{1,0:T(8,128)(2,1)S(1)}, u32[]{:S(2)}, u32[]{:S(2)}) %collective-permute-start.4) | collective-permute-done | bytes 262176 | tf_op jit(solution)/shard_map/ppermute | solution.py:48
  15.0 1.6 %collective-permute-start.6 = (bf16[256,512]{1,0:T(8,128)(2,1)S(1)}, bf16[256,512]{1,0:T(8,128)(2,1)S(1)}, u32[]{:S(2)}, u32[]{:S(2)}) collective-permute-start(bf16[256,512]{1,0:T(8,128)(2,1)S(1)} %collective-permute-done.4.refs_2_), channel_id=1, source_target_pairs={{0,4},{1,3},{4,8},{5,1},{8,12},{9,5},{12,14},{13,9},{14,10},{15,13... | collective-permute-start | bytes 786440 | tf_op jit(solution)/shard_map/ppermute | solution.py:48
  16.5 0.0 collective-permute-done.2.sib
  16.5 0.0 copy-done.1
  16.5 0.0 copy-done.4
  16.6 0.6 %partial_keys.3 = (f32[256,512]{1,0:T(8,128)S(1)}, f32[256,512]{1,0:T(8,128)S(1)}) custom-call(bf16[256,4096]{1,0:T(8,128)(2,1)S(1)} %copy-done.1, bf16[256,4096]{1,0:T(8,128)(2,1)S(1)} %collective-permute-done.2.sib, bf16[256,512]{1,0:T(8,128)(2,1)S(1)} %bitcast.18, bf16[256,512]{1,0:T(8,128)(2,1)S(1)} %collective-permute-done.refs_1_, ...), custom_call_target="tpu_custom_call" | custom-call | tf_op jit(solution)/shard_map/partial_keys/pallas_call | solution.py:184
  17.1 0.6 %collective-permute-done.1.refs_0_ = bf16[256,512]{1,0:T(8,128)(2,1)S(1)} collective-permute-done((bf16[256,512]{1,0:T(8,128)(2,1)S(1)}, bf16[256,512]{1,0:T(8,128)(2,1)S(1)}, u32[]{:S(2)}, u32[]{:S(2)}) %collective-permute-start.1) | collective-permute-done | bytes 262176 | tf_op jit(solution)/shard_map/ppermute | solution.py:48
  17.8 1.6 %collective-permute-start.5 = (bf16[256,512]{1,0:T(8,128)(2,1)S(1)}, bf16[256,512]{1,0:T(8,128)(2,1)S(1)}, u32[]{:S(2)}, u32[]{:S(2)}) collective-permute-start(bf16[256,512]{1,0:T(8,128)(2,1)S(1)} %collective-permute-done.1.refs_0_), channel_id=1, source_target_pairs={{0,4},{1,3},{4,8},{5,1},{8,12},{9,5},{12,14},{13,9},{14,10},{15,13... | collective-permute-start | bytes 786440 | tf_op jit(solution)/shard_map/ppermute | solution.py:48
  19.3 2.0 %collective-permute-done.6.refs_1_ = bf16[256,512]{1,0:T(8,128)(2,1)S(1)} collective-permute-done((bf16[256,512]{1,0:T(8,128)(2,1)S(1)}, bf16[256,512]{1,0:T(8,128)(2,1)S(1)}, u32[]{:S(2)}, u32[]{:S(2)}) %collective-permute-start.6) | collective-permute-done | bytes 262176 | tf_op jit(solution)/shard_map/ppermute | solution.py:48
  21.3 1.6 %collective-permute-start.9 = (bf16[256,512]{1,0:T(8,128)(2,1)S(1)}, bf16[256,512]{1,0:T(8,128)(2,1)S(1)}, u32[]{:S(2)}, u32[]{:S(2)}) collective-permute-start(bf16[256,512]{1,0:T(8,128)(2,1)S(1)} %collective-permute-done.6.refs_1_), channel_id=1, source_target_pairs={{0,4},{1,3},{4,8},{5,1},{8,12},{9,5},{12,14},{13,9},{14,10},{15,13... | collective-permute-start | bytes 786440 | tf_op jit(solution)/shard_map/ppermute | solution.py:48
  22.9 0.4 %partial_keys.4 = (f32[256,512]{1,0:T(8,128)S(1)}, f32[256,512]{1,0:T(8,128)S(1)}) custom-call(bf16[256,4096]{1,0:T(8,128)(2,1)S(1)} %copy-done.1, bf16[256,4096]{1,0:T(8,128)(2,1)S(1)} %collective-permute-done.2.sib, bf16[256,512]{1,0:T(8,128)(2,1)S(1)} %collective-permute-done.1.refs_0_, bf16[256,512]{1,0:T(8,128)(2,1)S(1)} %collective-permute-done.6.refs_1_, ...), custom_call_target="tpu_custom_call" | custom-call | tf_op jit(solution)/shard_map/partial_keys/pallas_call | solution.py:184
  23.4 0.8 %collective-permute-done.5.refs_0_ = bf16[256,512]{1,0:T(8,128)(2,1)S(1)} collective-permute-done((bf16[256,512]{1,0:T(8,128)(2,1)S(1)}, bf16[256,512]{1,0:T(8,128)(2,1)S(1)}, u32[]{:S(2)}, u32[]{:S(2)}) %collective-permute-start.5) | collective-permute-done | bytes 262176 | tf_op jit(solution)/shard_map/ppermute | solution.py:48
  24.1 0.0 copy-start.3
  24.1 1.6 %collective-permute-start.7 = (bf16[256,512]{1,0:T(8,128)(2,1)S(1)}, bf16[256,512]{1,0:T(8,128)(2,1)S(1)}, u32[]{:S(2)}, u32[]{:S(2)}) collective-permute-start(bf16[256,512]{1,0:T(8,128)(2,1)S(1)} %collective-permute-done.5.refs_0_), channel_id=1, source_target_pairs={{0,4},{1,3},{4,8},{5,1},{8,12},{9,5},{12,14},{13,9},{14,10},{15,13... | collective-permute-start | bytes 786440 | tf_op jit(solution)/shard_map/ppermute | solution.py:48
  25.7 0.5 %collective-permute-start.12 = (bf16[256,512]{1,0:T(8,128)(2,1)S(1)}, bf16[256,512]{1,0:T(8,128)(2,1)S(1)}, u32[]{:S(2)}, u32[]{:S(2)}) collective-permute-start(bf16[256,512]{1,0:T(8,128)(2,1)S(1)} %difference.3.diff), channel_id=1, source_target_pairs={{0,16},{16,0},{1,17},{17,1},{2,18},{18,2},{3,19},{19,3},{4,20},{20... | collective-permute-start | bytes 786440 | tf_op jit(solution)/shard_map/ppermute | solution.py:57
  26.3 1.4 %collective-permute-done.9.refs_1_ = bf16[256,512]{1,0:T(8,128)(2,1)S(1)} collective-permute-done((bf16[256,512]{1,0:T(8,128)(2,1)S(1)}, bf16[256,512]{1,0:T(8,128)(2,1)S(1)}, u32[]{:S(2)}, u32[]{:S(2)}) %collective-permute-start.9) | collective-permute-done | bytes 262176 | tf_op jit(solution)/shard_map/ppermute | solution.py:48
  27.7 0.4 %partial_keys.5 = (f32[256,512]{1,0:T(8,128)S(1)}, bf16[256,512]{1,0:T(8,128)(2,1)S(1)}) custom-call(bf16[256,4096]{1,0:T(8,128)(2,1)S(1)} %copy-done.1, bf16[256,4096]{1,0:T(8,128)(2,1)S(1)} %collective-permute-done.2.sib, bf16[256,512]{1,0:T(8,128)(2,1)S(1)} %collective-permute-done.5.refs_0_, bf16[256,512]{1,0:T(8,128)(2,1)S(1)} %collective-permute-done.9.refs_1_, ...), custom_call_target="tpu_custom_call" | custom-call | tf_op jit(solution)/shard_map/partial_keys/pallas_call | solution.py:184
  28.1 0.0 collective-permute-done.8.got.theirs.steps1
  28.2 0.1 collective-permute-start.11
  28.2 0.0 copy-done.3
  28.2 2.2 %outer_step.1 = (f32[1024,512]{1,0:T(8,128)}, f32[1024,512]{1,0:T(8,128)}) custom-call(f32[1024,512]{1,0:T(8,128)S(1)} %bitcast.10, f32[1024,512]{1,0:T(8,128)S(1)} %bitcast.14, bf16[784,512]{1,0:T(8,128)(2,1)S(1)} %difference.2.own.mine.steps0, bf16[784,512]{1,0:T(8,128)(2,1)S(1)} %collective-permute-done.8.got.theirs.steps1, ...), custom_call_target="tpu_custom_call" | custom-call | flops 3932160 | bytes 7864320 | tf_op jit(solution)/shard_map/outer_step/pallas_call | solution.py:137
  30.5 0.0 collective-permute-done.7.mine
  30.5 0.4 %collective-permute-start.10 = (bf16[256,512]{1,0:T(8,128)(2,1)S(1)}, bf16[256,512]{1,0:T(8,128)(2,1)S(1)}, u32[]{:S(2)}, u32[]{:S(2)}) collective-permute-start(bf16[256,512]{1,0:T(8,128)(2,1)S(1)} %collective-permute-done.7.mine), channel_id=1, source_target_pairs={{0,1},{1,0},{2,3},{3,2},{4,5},{5,4},{6,7},{7,6},{8,9},{9,8},{10,11... | collective-permute-start | bytes 786440 | tf_op jit(solution)/shard_map/ppermute | solution.py:53
  30.9 1.3 %collective-permute-done.12.sent = bf16[256,512]{1,0:T(8,128)(2,1)S(1)} collective-permute-done((bf16[256,512]{1,0:T(8,128)(2,1)S(1)}, bf16[256,512]{1,0:T(8,128)(2,1)S(1)}, u32[]{:S(2)}, u32[]{:S(2)}) %collective-permute-start.12) | collective-permute-done | bytes 262176 | tf_op jit(solution)/shard_map/ppermute | solution.py:57
  32.3 0.0 collective-permute-done.11.got
  32.3 0.0 collective-permute-done.10.other
  32.3 1.6 %close.1 = (bf16[256,512]{1,0:T(8,128)(2,1)}, f32[1024,512]{1,0:T(8,128)}, f32[1024,512]{1,0:T(8,128)}) custom-call(bf16[256,4096]{1,0:T(8,128)(2,1)S(1)} %copy-done.1, bf16[256,512]{1,0:T(8,128)(2,1)S(1)} %collective-permute-done.7.mine, bf16[256,512]{1,0:T(8,128)(2,1)S(1)} %collective-permute-done.10.other, ...), custom_call_target="tpu_custom_call", output_to_operand_aliasing={{1}: (11, {}), {2}: (12, {})} | custom-call | tf_op jit(solution)/shard_map/close/pallas_call | solution.py:238
Async XLA Ops:
  0.6 15.9 %collective-permute-start.2 = (bf16[256,4096]{1,0:T(8,128)(2,1)}, bf16[256,4096]{1,0:T(8,128)(2,1)S(1)}, u32[]{:S(2)}, u32[]{:S(2)}) collective-permute-start(bf16[256,4096]{1,0:T(8,128)(2,1)} %act.7), channel_id=1, source_target_pairs={{0,1},{1,0},{2,3},{3,2},{4,5},{5,4},{6,7},{7,6},{8,9},{9,8},{10,11... | collective-permute-start | bytes 6291464 | tf_op jit(solution)/shard_map/ppermute | solution.py:53
  1.1 7.4 %collective-permute-start.3 = (bf16[256,512]{1,0:T(8,128)(2,1)}, bf16[256,512]{1,0:T(8,128)(2,1)S(1)}, u32[]{:S(2)}, u32[]{:S(2)}) collective-permute-start(bf16[256,512]{1,0:T(8,128)(2,1)} %bitcast.16), channel_id=1, source_target_pairs={{0,1},{1,0},{2,3},{3,2},{4,5},{5,4},{6,7},{7,6},{8,9},{9,8},{10,11... | collective-permute-start | bytes 786440 | tf_op jit(solution)/shard_map/ppermute | solution.py:53
  1.2 8.9 %collective-permute-start = (bf16[256,512]{1,0:T(8,128)(2,1)}, bf16[256,512]{1,0:T(8,128)(2,1)S(1)}, u32[]{:S(2)}, u32[]{:S(2)}) collective-permute-start(bf16[256,512]{1,0:T(8,128)(2,1)} %bitcast.17), channel_id=1, source_target_pairs={{0,4},{1,3},{4,8},{5,1},{8,12},{9,5},{12,14},{13,9},{14,10},{15,13... | collective-permute-start | bytes 786440 | tf_op jit(solution)/shard_map/ppermute | solution.py:48
  4.9 6.9 %copy-start = (f32[2,2,256,512]{3,2,1,0:T(8,128)S(1)}, f32[2,2,256,512]{3,2,1,0:T(8,128)}, u32[]{:S(2)}) copy-start(f32[2,2,256,512]{3,2,1,0:T(8,128)} %param.9) | copy-start | bytes 6291460
  4.9 6.9 %copy-start.2 = (f32[1,2,2,256,512]{4,3,2,1,0:T(8,128)S(1)}, f32[1,2,2,256,512]{4,3,2,1,0:T(8,128)}, u32[]{:S(2)}) copy-start(f32[1,2,2,256,512]{4,3,2,1,0:T(8,128)} %param.8) | copy-start | bytes 6291460
  7.0 9.5 %copy-start.1 = (bf16[256,4096]{1,0:T(8,128)(2,1)S(1)}, bf16[256,4096]{1,0:T(8,128)(2,1)}, u32[]{:S(2)}) copy-start(bf16[256,4096]{1,0:T(8,128)(2,1)} %act.7) | copy-start | bytes 6291460
  7.0 9.5 %copy-start.4 = (bf16[1,256,512]{2,1,0:T(8,128)(2,1)S(1)}, bf16[1,256,512]{2,1,0:T(8,128)(2,1)}, u32[]{:S(2)}) copy-start(bf16[1,256,512]{2,1,0:T(8,128)(2,1)} %param.7) | copy-start | bytes 786436
  7.0 21.1 %collective-permute-start.8 = (bf16[784,512]{1,0:T(8,128)(2,1)S(1)}, bf16[784,512]{1,0:T(8,128)(2,1)S(1)}, u32[]{:S(2)}, u32[]{:S(2)}) collective-permute-start(bf16[784,512]{1,0:T(8,128)(2,1)S(1)} %difference.2.own.mine.steps0), channel_id=1, source_target_pairs={{0,16},{16,0},{1,17},{17,1},{2,18},{18,2},{3,19},{19,3},{4,20},{20... | collective-permute-start | bytes 2408456 | tf_op jit(solution)/shard_map/ppermute | solution.py:57
  8.6 6.4 %collective-permute-start.4 = (bf16[256,512]{1,0:T(8,128)(2,1)S(1)}, bf16[256,512]{1,0:T(8,128)(2,1)S(1)}, u32[]{:S(2)}, u32[]{:S(2)}) collective-permute-start(bf16[256,512]{1,0:T(8,128)(2,1)S(1)} %collective-permute-done.3), channel_id=1, source_target_pairs={{0,4},{1,3},{4,8},{5,1},{8,12},{9,5},{12,14},{13,9},{14,10},{15,13... | collective-permute-start | bytes 786440 | tf_op jit(solution)/shard_map/ppermute | solution.py:48
  10.2 7.6 %collective-permute-start.1 = (bf16[256,512]{1,0:T(8,128)(2,1)S(1)}, bf16[256,512]{1,0:T(8,128)(2,1)S(1)}, u32[]{:S(2)}, u32[]{:S(2)}) collective-permute-start(bf16[256,512]{1,0:T(8,128)(2,1)S(1)} %collective-permute-done.refs_1_), channel_id=1, source_target_pairs={{0,4},{1,3},{4,8},{5,1},{8,12},{9,5},{12,14},{13,9},{14,10},{15,13... | collective-permute-start | bytes 786440 | tf_op jit(solution)/shard_map/ppermute | solution.py:48
  15.0 6.4 %collective-permute-start.6 = (bf16[256,512]{1,0:T(8,128)(2,1)S(1)}, bf16[256,512]{1,0:T(8,128)(2,1)S(1)}, u32[]{:S(2)}, u32[]{:S(2)}) collective-permute-start(bf16[256,512]{1,0:T(8,128)(2,1)S(1)} %collective-permute-done.4.refs_2_), channel_id=1, source_target_pairs={{0,4},{1,3},{4,8},{5,1},{8,12},{9,5},{12,14},{13,9},{14,10},{15,13... | collective-permute-start | bytes 786440 | tf_op jit(solution)/shard_map/ppermute | solution.py:48
  17.8 6.4 %collective-permute-start.5 = (bf16[256,512]{1,0:T(8,128)(2,1)S(1)}, bf16[256,512]{1,0:T(8,128)(2,1)S(1)}, u32[]{:S(2)}, u32[]{:S(2)}) collective-permute-start(bf16[256,512]{1,0:T(8,128)(2,1)S(1)} %collective-permute-done.1.refs_0_), channel_id=1, source_target_pairs={{0,4},{1,3},{4,8},{5,1},{8,12},{9,5},{12,14},{13,9},{14,10},{15,13... | collective-permute-start | bytes 786440 | tf_op jit(solution)/shard_map/ppermute | solution.py:48
  21.3 6.4 %collective-permute-start.9 = (bf16[256,512]{1,0:T(8,128)(2,1)S(1)}, bf16[256,512]{1,0:T(8,128)(2,1)S(1)}, u32[]{:S(2)}, u32[]{:S(2)}) collective-permute-start(bf16[256,512]{1,0:T(8,128)(2,1)S(1)} %collective-permute-done.6.refs_1_), channel_id=1, source_target_pairs={{0,4},{1,3},{4,8},{5,1},{8,12},{9,5},{12,14},{13,9},{14,10},{15,13... | collective-permute-start | bytes 786440 | tf_op jit(solution)/shard_map/ppermute | solution.py:48
  24.1 4.1 %copy-start.3 = (f32[2,2,256,512]{3,2,1,0:T(8,128)S(1)}, f32[2,2,256,512]{3,2,1,0:T(8,128)}, u32[]{:S(2)}) copy-start(f32[2,2,256,512]{3,2,1,0:T(8,128)} %param.10) | copy-start | bytes 6291460
  24.1 6.4 %collective-permute-start.7 = (bf16[256,512]{1,0:T(8,128)(2,1)S(1)}, bf16[256,512]{1,0:T(8,128)(2,1)S(1)}, u32[]{:S(2)}, u32[]{:S(2)}) collective-permute-start(bf16[256,512]{1,0:T(8,128)(2,1)S(1)} %collective-permute-done.5.refs_0_), channel_id=1, source_target_pairs={{0,4},{1,3},{4,8},{5,1},{8,12},{9,5},{12,14},{13,9},{14,10},{15,13... | collective-permute-start | bytes 786440 | tf_op jit(solution)/shard_map/ppermute | solution.py:48
  25.7 6.5 %collective-permute-start.12 = (bf16[256,512]{1,0:T(8,128)(2,1)S(1)}, bf16[256,512]{1,0:T(8,128)(2,1)S(1)}, u32[]{:S(2)}, u32[]{:S(2)}) collective-permute-start(bf16[256,512]{1,0:T(8,128)(2,1)S(1)} %difference.3.diff), channel_id=1, source_target_pairs={{0,16},{16,0},{1,17},{17,1},{2,18},{18,2},{3,19},{19,3},{4,20},{20... | collective-permute-start | bytes 786440 | tf_op jit(solution)/shard_map/ppermute | solution.py:57
  28.2 4.1 %collective-permute-start.11 = (bf16[256,512]{1,0:T(8,128)(2,1)S(1)}, bf16[256,512]{1,0:T(8,128)(2,1)S(1)}, u32[]{:S(2)}, u32[]{:S(2)}) collective-permute-start(bf16[256,512]{1,0:T(8,128)(2,1)S(1)} %get-tuple-element.48), channel_id=1, source_target_pairs={{0,1},{1,0},{2,3},{3,2},{4,5},{5,4},{6,7},{7,6},{8,9},{9,8},{10,11... | collective-permute-start | bytes 786440 | tf_op jit(solution)/shard_map/ppermute | solution.py:53
  30.5 1.7 %collective-permute-start.10 = (bf16[256,512]{1,0:T(8,128)(2,1)S(1)}, bf16[256,512]{1,0:T(8,128)(2,1)S(1)}, u32[]{:S(2)}, u32[]{:S(2)}) collective-permute-start(bf16[256,512]{1,0:T(8,128)(2,1)S(1)} %collective-permute-done.7.mine), channel_id=1, source_target_pairs={{0,1},{1,0},{2,3},{3,2},{4,5},{5,4},{6,7},{7,6},{8,9},{9,8},{10,11... | collective-permute-start | bytes 786440 | tf_op jit(solution)/shard_map/ppermute | solution.py:53
